TPU v7x, 32 devices: a whole 2x2x4 slice. The times are simulated.
32 devices in a mesh: slab: 16 (over z, y, core), sub: 2 (over x).
Axes of the slice: x: 2, y: 2, z: 4, core: 2. Of those that a mesh axis runs over, the one named last changes fastest.
Arguments:
- positions: float32 [3, 4096], P(None, ('slab', 'sub')), may hold values from 0 to 1
- velocities: float32 [3, 4096], P(None, ('slab', 'sub'))
- species: int32 [4096], P(('slab', 'sub')), may hold values from 0 to 7
- ghost_species: int32 [6144], P(('slab', 'sub')), may hold values from 0 to 7, as said below
- neighbours: int32 [20, 4096], P(None, ('slab', 'sub')), may hold values from 0 to 319, as said below
- slot_mask: int32 [20, 4096], P(None, ('slab', 'sub')), may hold values from 0 to 1, as said below
- edge_vectors: float32 [3, 20, 4096], P(None, None, ('slab', 'sub')), may hold values from -4.8 to 4.8, as said below
- send_slab: int32 [2, 1536], P(None, ('slab', 'sub')), may hold values from 0 to 127, as said below
- send_sub: int32 [2, 1536], P(None, ('slab', 'sub')), may hold values from 0 to 127, as said below
- migrants: int32 [4, 128], P(None, ('slab', 'sub')), may hold values from 0 to 127, as said below
- embedding: float32 [8, 128], replicated, may hold values from -6 to 6
- energy_shift: float32 [8], replicated, may hold values from -4 to 4
- masses: float32 [8], replicated, may hold values from 0.5 to 4
- radial_one_in: float32 [64, 8], replicated, may hold values from -2 to 2
- radial_one_mid: float32 [2, 64, 64], replicated, may hold values from -0.75 to 0.75
- radial_one_out: float32 [256, 64], replicated, may hold values from -0.75 to 0.75
- node_one: float32 [6, 128, 128], replicated, may hold values from -0.5 to 0.5
- radial_two_in: float32 [64, 8], replicated, may hold values from -2 to 2
- radial_two_mid: float32 [2, 64, 64], replicated, may hold values from -0.75 to 0.75
- radial_two_out: float32 [512, 64], replicated, may hold values from -0.75 to 0.75
- node_two: float32 [5, 128, 128], replicated, may hold values from -0.5 to 0.5
- readout_linear: float32 [128], replicated, may hold values from -0.5 to 0.5
- readout_hidden: float32 [16, 128], replicated, may hold values from -0.5 to 0.5
- readout_out: float32 [16], replicated, may hold values from -1.5 to 1.5
- box_matrix: float32 [3, 3], replicated, as said below
- box_velocity: float32 [3, 3], replicated, may hold values from -3 to 3
Outputs:
- atom_energy: float32 [4096], P(('slab', 'sub'))
- forces: float32 [3, 4096], P(None, ('slab', 'sub'))
- new_velocities: float32 [3, 4096], P(None, ('slab', 'sub'))
- new_positions: float32 [3, 4096], P(None, ('slab', 'sub'))
- arrivals: float32 [6, 512], P(None, ('slab', 'sub'))
- new_box: float32 [3, 3], replicated
- new_box_velocity: float32 [3, 3], replicated
Inputs may be any that keep to these rules, and one draw needn't show every extreme that they name: `neighbours`: the 20 entries of an atom are distinct extended rows of its device. `slot_mask`: live slots of an atom come first; every atom has 10 to 20 live slots and the first atom of each device has all 20. `edge_vectors`: every edge vector has a length between 1.8 and 4.8. `send_slab`: each row holds, for each device, 48 distinct own atoms; row 0 goes to slab index - 1, row 1 to slab index + 1. `send_sub`: each row holds, for each device, 48 distinct own atoms; row 0 goes to sub index - 1, row 1 to sub index + 1. `migrants`: for each device the four rows hold 16 distinct own atoms, moving to slab index - 1, slab index + 1, sub index - 1 and sub index + 1. `ghost_species`: each ghost row holds the species of the atom that the send lists deliver to it. `box_matrix`: the diagonal dominates each row, so the determinant is positive.
All inputs are finite; a program needn't handle non-finite values.
Results may differ from a plain program's by a relative error of at most 0.000061.
Values sent between devices are 32-bit elements; how exact they have to be, the bound alone decides.
No kernel may reach another device: no remote copies, remote signals or barrier semaphores. Data moves between devices by JAX's collectives and lax.ppermute only.
A program may use at most 128 MiB of HBM per device.

v0:
```python
import math

import jax
import jax.numpy as jnp
from jax import lax
from jax.experimental import pallas as pl
from jax.experimental.pallas import tpu as pltpu
from jax.sharding import PartitionSpec as P

cutoff = 5.0
neighbor_norm = 0.125
time_step = 0.5
outside_pressure = 0.5
box_mass = 0.125
highest = lax.Precision.HIGHEST
f32 = jnp.float32
bf16 = jnp.bfloat16
GROUP = 4


def shifted(block, axis, distance):
    count = lax.axis_size(axis)
    return lax.ppermute(block, axis, [((i - distance) % count, i) for i in range(count)])


def trade(to_minus, to_plus, to_prev, to_next):
    from_minus, from_plus = shifted(to_plus, "slab", 1), shifted(to_minus, "slab", -1)
    return from_minus, from_plus, shifted(to_next, "sub", 1), shifted(to_prev, "sub", -1)


def parts(x):
    high = x.astype(bf16)
    return high, (x - high.astype(f32)).astype(bf16)


def dot(a, b):
    return jnp.dot(a, b, preferred_element_type=f32)


def dot_nt(a, b):
    return lax.dot_general(a, b, (((1,), (1,)), ((), ())), preferred_element_type=f32)


def exact(a, b, dims=((1,), (0,))):
    return lax.dot_general(a, b, (dims, ((), ())), precision=highest, preferred_element_type=f32)


def product(weight, x):
    high, low = parts(x)
    return dot(weight[0], high) + dot(weight[0], low) + dot(weight[1], high)


def weight_stack(w):
    high = w.astype(bf16).astype(f32)
    return jnp.concatenate([high, high, w - high], axis=1).astype(bf16)


def weight_stack_t(w):
    high = w.astype(bf16).astype(f32)
    return jnp.transpose(jnp.concatenate([high, high, w - high], axis=0)).astype(bf16)


def value_stack(x):
    high, low = parts(x)
    return jnp.concatenate([high, low, high], axis=0)


def value_stack_small(x):
    high = x.astype(bf16).astype(f32)
    return jnp.concatenate([high, x - high, high], axis=0).astype(bf16)


def over_groups(count, step, carry):
    for i in range(count):
        carry = step(i, carry)
    return carry


def span_of(first, count):
    if isinstance(first, int):
        return pl.ds(first, count)
    return pl.ds(pl.multiple_of(first, count), count)


def iota(shape, axis):
    return lax.broadcasted_iota(jnp.int32, shape, axis)


def column(row):
    n = row.shape[1]
    return jnp.sum(jnp.where(iota((n, n), 0) == iota((n, n), 1), row, 0.0), axis=1, keepdims=True)


def sigmoid(x):
    return 0.5 + 0.5 * jnp.tanh(0.5 * x)


def basis(distance, inverse_distance, count, with_slope):
    orders = (iota((count, distance.shape[1]), 0) + 1).astype(f32)
    scaled = distance * (1.0 / cutoff)
    angle = orders * (math.pi * scaled)
    second = scaled * scaled
    fourth = second * second
    fifth = fourth * scaled
    sixth = fourth * second
    scale = math.sqrt(2.0 / cutoff)
    envelope = 1.0 + sixth * (-28.0 + scaled * (48.0 - 21.0 * scaled))
    sine = jnp.sin(angle)
    front = scale * envelope * inverse_distance
    value = sine * front
    if not with_slope:
        return value, None
    slope_envelope = fifth * (-168.0 + scaled * (336.0 - 168.0 * scaled)) * (1.0 / cutoff)
    slope_front = scale * inverse_distance * (slope_envelope - envelope * inverse_distance)
    slope = sine * slope_front + jnp.cos(angle) * (orders * (math.pi / cutoff)) * front
    return value, slope


def basis_group(geo, first, count, with_slope):
    found = [
        basis(geo[4, pl.ds(first + j, 1), :], geo[5, pl.ds(first + j, 1), :], count, with_slope)
        for j in range(GROUP)
    ]
    value = jnp.concatenate([pair[0] for pair in found], axis=1)
    slope = jnp.concatenate([pair[1] for pair in found], axis=1) if with_slope else None
    return value, slope


def hidden_values(value, inner, mid_a, mid_b):
    x = dot(inner, value_stack_small(value))
    h = x * sigmoid(x)
    x = dot(mid_a, value_stack(h))
    h = x * sigmoid(x)
    x = dot(mid_b, value_stack(h))
    return x * sigmoid(x)


def hidden_pairs(value, slope, inner, mid_a, mid_b):
    x, dx = dot(inner, value_stack_small(value)), dot(inner, value_stack_small(slope))
    for mid in (mid_a, mid_b, None):
        gate = sigmoid(x)
        h = x * gate
        dh = (gate + h * (1.0 - gate)) * dx
        if mid is not None:
            x, dx = dot(mid, value_stack(h)), dot(mid, value_stack(dh))
    return h, dh


def species_matrix(first_mixing, embedding):
    lifted = exact(first_mixing, embedding, ((1,), (1,)))
    high = lifted.astype(bf16).astype(f32)
    rest = lifted - high
    mid = rest.astype(bf16).astype(f32)
    return jnp.concatenate([high, mid, rest - mid], axis=1).astype(bf16)


def picked_group(lifted, geo, kinds, first, species_count):
    blocks = []
    for j in range(GROUP):
        kind = kinds[pl.ds(first + j, 1), :]
        weight = geo[3, pl.ds(first + j, 1), :]
        blocks.append(jnp.where(iota((species_count, kind.shape[1]), 0) == kind, weight, 0.0))
    block = jnp.concatenate(blocks, axis=1)
    return dot(lifted, jnp.concatenate([block, block, block], axis=0).astype(bf16))


def send_onehot(facts, first, slab_rows, sub_rows):
    atoms = facts.shape[1]
    lengths = (slab_rows, slab_rows, sub_rows, sub_rows)
    rows = [facts[first + 9 + i : first + 10 + i, :n] for i, n in enumerate(lengths)]
    rows = jnp.concatenate(rows, axis=1)
    return (iota((atoms, rows.shape[1]), 0).astype(f32) == rows).astype(f32)


FIRST_INPUTS = 24
FACTS = 16


def packed_step(slots):
    return -(-slots // 8) * 8


def first_kernel(
    *refs,
):
    count = FIRST_INPUTS
    buffers, ready, gone = refs[-count - 2 : -2], refs[-2], refs[-1]
    copies = [pltpu.make_async_copy(refs[i], buffers[i], ready.at[i]) for i in range(count)]
    for copy in copies:
        copy.start()
    (
        edges, mask, neighbours, species, ghosts, embedding, radial_in, radial_mid, radial_out, node_one,
        send_slab, send_sub, velocities, positions, migrants, masses, shifts,
        hidden_head, linear_head, out_head, next_in, next_mid, next_out, node_two,
    ) = buffers
    kinds, far_sums, far_packed, to_minus, to_plus, to_prev, to_next, geo, packed, sums = refs[count : -count - 2]
    for copy in copies[:2]:
        copy.wait()
    slots, atoms = mask.shape
    width = node_one.shape[1]
    species_count, basis_count = embedding.shape[0], radial_in.shape[0]
    ex, ey, ez = edges[0], edges[1], edges[2]
    square = ex * ex + ey * ey + ez * ez
    distance = jnp.sqrt(square)
    inverse_distance = 1.0 / distance
    for a, e in enumerate((ex, ey, ez)):
        geo[a] = e * inverse_distance
    geo[3] = mask[...].astype(f32) * neighbor_norm
    geo[4] = distance
    geo[5] = inverse_distance
    base = 5 * width
    step = packed_step(slots)
    for a in range(6):
        packed[base + a * step : base + a * step + slots] = geo[a]
    for copy in copies[2:5]:
        copy.wait()
    ghost_row = ghosts[...]
    extra = -ghost_row.shape[1] % atoms
    if extra:
        ghost_row = jnp.concatenate([ghost_row, jnp.zeros((1, extra), jnp.int32)], axis=1)
    tables = [species[...]] + [ghost_row[:, i : i + atoms] for i in range(0, ghost_row.shape[1], atoms)]
    pad = -slots % 8
    rows = neighbours[...]
    if pad:
        rows = jnp.concatenate([rows, jnp.zeros((pad, atoms), jnp.int32)], axis=0)
    inner_index = lax.rem(rows, atoms)
    block_index = lax.div(rows, atoms)
    found = jnp.zeros_like(rows)
    for i, table in enumerate(tables):
        spread = jnp.broadcast_to(table, rows.shape)
        got = jnp.take_along_axis(spread, inner_index, axis=1)
        found = jnp.where(block_index == i, got, found)
    kinds[...] = found[:slots]

    for copy in copies[5:10]:
        copy.wait()
    inner = weight_stack_t(radial_in[...])
    mid_a, mid_b = weight_stack(radial_mid[0]), weight_stack(radial_mid[1])
    outer = weight_stack_t(radial_out[...])
    lifted = species_matrix(node_one[0], embedding[...])
    sums[...] = jnp.zeros_like(sums)

    def group(step, carry):
        first = step * GROUP
        value, _ = basis_group(geo, first, basis_count, False)
        h = hidden_values(value, inner, mid_a, mid_b)
        weights = dot(outer, value_stack(h))
        picked = picked_group(lifted, geo, kinds, first, species_count)
        totals = [0.0] * 4
        for j in range(GROUP):
            at = slice(j * atoms, (j + 1) * atoms)
            p = picked[:, at]
            totals[0] = totals[0] + weights[:width, at] * p
            q = weights[width:, at] * p
            for a in range(3):
                totals[a + 1] = totals[a + 1] + q * geo[a, pl.ds(first + j, 1), :]
        for a in range(4):
            sums[a] += totals[a]
        return carry

    over_groups(slots // GROUP, group, 0)

    early_sums = pltpu.make_async_copy(sums.at[:4], far_sums.at[:4], gone.at[2])
    early_sums.start()
    for copy in copies[10:]:
        copy.wait()
    mass = shift = jnp.zeros((1, atoms), f32)
    for i in range(masses.shape[1]):
        mass = jnp.where(species[...] == i, masses[:, i : i + 1], mass)
        shift = jnp.where(species[...] == i, shifts[:, i : i + 1], shift)
    facts = base + 6 * step
    packed[facts : facts + 1] = iota((1, atoms), 1).astype(f32)
    packed[facts + 1 : facts + 4] = velocities[...]
    packed[facts + 4 : facts + 7] = positions[...]
    packed[facts + 7 : facts + 8] = 1.0 / jnp.sqrt(mass)
    packed[facts + 8 : facts + 9] = mass
    packed[facts + 9 : facts + FACTS] = jnp.zeros((FACTS - 9, atoms), f32)
    for i, (lists, at) in enumerate(((send_slab, 1), (send_slab, 0), (send_sub, 1), (send_sub, 0))):
        packed[facts + 9 + i : facts + 10 + i, : lists.shape[1]] = lists[at : at + 1, :].astype(f32)
    count = migrants.shape[1]
    for i, at in enumerate((1, 0, 3, 2)):
        packed[facts + 13 : facts + 14, i * count : (i + 1) * count] = migrants[at : at + 1, :].astype(f32)
    inner_rows = next_mid.shape[1]
    start = facts + FACTS
    for i in range(3):
        packed[start : start + width] = node_two[i + 2]
        start += width
    for i in range(next_out.shape[1] // atoms):
        packed[start : start + inner_rows] = next_out[:, i * atoms : (i + 1) * atoms]
        start += inner_rows
    for i in range(2):
        packed[start : start + inner_rows, :inner_rows] = next_mid[i]
        start += inner_rows
    packed[start : start + next_in.shape[0], :inner_rows] = next_in[...]
    start += next_in.shape[0]
    packed[start : start + slots] = neighbours[...].astype(f32)
    start += step
    count = hidden_head.shape[0]
    packed[start : start + count] = hidden_head[...]
    packed[start + count : start + count + 1] = linear_head[...]
    packed[start + count + 1 : start + count + 2, : out_head.shape[1]] = out_head[...]
    packed[start + count + 2 : start + count + 3] = shift
    early = pltpu.make_async_copy(packed.at[base:], far_packed.at[base:], gone.at[0])
    early.start()

    own_onehot = (iota((species_count, atoms), 0) == species[...]).astype(f32)
    own = exact(embedding[...], own_onehot, ((0,), (0,)))
    scalar_sum = sums[0]
    vectors = [sums[1], sums[2], sums[3]]
    squares = vectors[0] * vectors[0] + vectors[1] * vectors[1] + vectors[2] * vectors[2]
    scalars = (
        own
        + product(parts(node_one[1]), scalar_sum)
        + product(parts(node_one[2]), scalar_sum * scalar_sum)
        + product(parts(node_one[3]), squares)
    )
    gate = product(parts(node_one[5]), scalar_sum)
    sums[4] = gate
    late_sums = pltpu.make_async_copy(sums.at[4:], far_sums.at[4:], gone.at[3])
    late_sums.start()
    turned = product(parts(node_one[4]), jnp.concatenate(vectors, axis=1))
    moved = turned + jnp.concatenate([gate * v for v in vectors], axis=1)
    packed[:width] = scalars
    x = product(parts(node_two[0]), scalars)
    y = product(parts(node_two[1]), moved)
    table = jnp.concatenate([x] + [y[:, a * atoms : (a + 1) * atoms] for a in range(3)], axis=0)
    packed[width : 5 * width] = table
    late = pltpu.make_async_copy(packed.at[:base], far_packed.at[:base], gone.at[1])
    late.start()
    pick = send_onehot(packed, facts, send_slab.shape[1], send_sub.shape[1]).astype(bf16)
    high, low = parts(table)
    sent = jnp.transpose(dot(high, pick) + dot(low, pick))
    slab_rows = send_slab.shape[1]
    to_plus[...] = sent[:slab_rows]
    to_minus[...] = sent[slab_rows : 2 * slab_rows]
    sub_rows = send_sub.shape[1]
    to_next[...] = sent[2 * slab_rows : 2 * slab_rows + sub_rows]
    to_prev[...] = sent[2 * slab_rows + sub_rows :]
    for copy in (early, late, early_sums, late_sums):
        copy.wait()


def radial_kernel(
    packed,
    weights_all, slopes, onehot, outer, forward_high, forward_low, backward_high, backward_low,
    geo, table, scalars, extras, facts, heads, *, slab_rows, sub_rows, moves, basis_count,
):
    slots, atoms = geo.shape[1:]
    width = scalars.shape[0]
    depth = 4 * width
    inner_rows = slopes.shape[0] // 3
    scalars[...] = packed[:width]
    first_fact = 5 * width + 6 * packed_step(slots)
    start = first_fact + FACTS
    mixings = [packed[start + i * width : start + (i + 1) * width] for i in range(3)]
    start += 3 * width
    pieces = depth // atoms
    radial_out = [packed[start + i * inner_rows : start + (i + 1) * inner_rows] for i in range(pieces)]
    radial_out = jnp.concatenate(radial_out, axis=1)
    start += pieces * inner_rows
    radial_mid = [packed[start + i * inner_rows : start + (i + 1) * inner_rows, :inner_rows] for i in range(2)]
    start += 2 * inner_rows
    radial_in = packed[start : start + basis_count, :inner_rows]
    first_row = start + basis_count
    heads[...] = packed[first_row + packed_step(slots) :]
    table[:, :atoms], table[:, atoms:] = parts(packed[width : 5 * width])
    for a in range(6):
        start = 5 * width + a * packed_step(slots)
        geo[a] = packed[start : start + slots]
    facts[...] = packed[first_fact : first_fact + FACTS]
    listed = exact(facts[:8], send_onehot(facts, 0, slab_rows, sub_rows))
    moving = exact(facts[:8], (iota((atoms, 4 * moves), 0).astype(f32) == facts[13:14, : 4 * moves]).astype(f32))
    start = 0
    extras[...] = jnp.zeros_like(extras)
    for i, length in enumerate((slab_rows, slab_rows, sub_rows, sub_rows)):
        extras[i, :, :length] = listed[:, start : start + length]
        extras[i, :, atoms : atoms + moves] = moving[:, i * moves : (i + 1) * moves]
        start += length
    rows = onehot.shape[0] // 2
    outer[...] = weight_stack_t(radial_out)
    mixing = jnp.concatenate(mixings, axis=1)
    forward_high[...], forward_low[...] = parts(mixing)
    turned = jnp.concatenate([jnp.transpose(m) for m in mixings], axis=0)
    backward_high[...], backward_low[...] = parts(turned)
    inner = weight_stack_t(radial_in)
    mid_a, mid_b = weight_stack(radial_mid[0]), weight_stack(radial_mid[1])

    def group(step, carry):
        first = step * GROUP
        at = span_of(step * GROUP * atoms, GROUP * atoms)
        value, slope = basis_group(geo, first, basis_count, True)
        h, dh = hidden_pairs(value, slope, inner, mid_a, mid_b)
        slopes[:, at] = value_stack(dh)
        blocks = []
        for j in range(GROUP):
            row = packed[first_row + first + j : first_row + first + j + 1]
            weight = geo[3, pl.ds(first + j, 1), :]
            row = row.astype(jnp.int32)
            blocks.append(jnp.where(iota((rows, atoms), 0) == row, weight, 0.0).astype(bf16))
        block = jnp.concatenate(blocks, axis=1)
        own, ghosts = block[:atoms], block[atoms:]
        onehot[:, at] = jnp.concatenate([own, own, ghosts, ghosts], axis=0)
        weights_all[:, at] = dot(outer[...], value_stack(h))
        return carry

    over_groups(slots // GROUP, group, 0)


def second_kernel(
    geo, own_table, from_minus, from_plus, from_prev, from_next, scalars, extras,
    weights_all, onehot, forward_high, forward_low, backward_high, backward_low, heads,
    energy, scalar_pull, picked_all, sums, own_pull, back_minus, back_plus, back_prev, back_next,
    table, pulled,
):
    slots, atoms = geo.shape[1], geo.shape[2]
    width = scalars.shape[0]
    depth = 4 * width
    ghosts = jnp.concatenate([from_minus[...], from_plus[...], from_prev[...], from_next[...]], axis=0)
    high = ghosts.astype(bf16).astype(f32)
    table[:, : 2 * atoms] = own_table[...]
    table[:, 2 * atoms :] = jnp.transpose(jnp.concatenate([high, ghosts - high], axis=0)).astype(bf16)
    ghost_rows = ghosts.shape[0]
    sums[...] = jnp.zeros_like(sums)

    def units(first, j):
        return [geo[a, pl.ds(first + j, 1), :] for a in range(3)]

    def forward(step, carry):
        first = step * GROUP
        at = span_of(step * GROUP * atoms, GROUP * atoms)
        picked = dot(table[...], onehot[:, at])
        picked_all[:, at] = picked
        totals = [0.0] * 4
        for j in range(GROUP):
            span = slice(j * atoms, (j + 1) * atoms)
            here = span_of((step * GROUP + j) * atoms, atoms)
            p = [picked[a * width : (a + 1) * width, span] for a in range(4)]
            r = [weights_all[a * width : (a + 1) * width, here] for a in range(4)]
            u = units(first, j)
            along = p[1] * u[0] + p[2] * u[1] + p[3] * u[2]
            totals[0] = totals[0] + (r[0] * p[0] + r[3] * along)
            q = r[1] * p[0]
            for a in range(3):
                totals[a + 1] = totals[a + 1] + (q * u[a] + r[2] * p[a + 1])
        for a in range(4):
            sums[a] += totals[a]
        return carry

    over_groups(slots // GROUP, forward, 0)

    scalar_sum = sums[0]
    vectors = [sums[1], sums[2], sums[3]]
    squares = vectors[0] * vectors[0] + vectors[1] * vectors[1] + vectors[2] * vectors[2]
    mixed = jnp.concatenate([scalar_sum, scalar_sum * scalar_sum, squares], axis=0)
    second = scalars[...] + product((forward_high[...], forward_low[...]), mixed)
    units_out = heads.shape[0] - 8
    readout_hidden = heads[:units_out]
    readout_linear, readout_out = heads[units_out : units_out + 1], heads[units_out + 1 : units_out + 2, :units_out]
    hidden_in = product(parts(readout_hidden), second)
    hidden_gate = sigmoid(hidden_in)
    hidden = hidden_in * hidden_gate
    shift = heads[units_out + 2 : units_out + 3]
    energy[...] = shift + exact(readout_linear, scalars[...]) + exact(readout_out, hidden)
    hidden_pull = column(readout_out) * (hidden_gate + hidden * (1.0 - hidden_gate))
    second_pull = exact(readout_hidden, hidden_pull, ((0,), (0,)))
    scalar_pull[...] = second_pull
    spread = product((backward_high[...], backward_low[...]), second_pull)
    double = 2.0 * spread[2 * width :]
    sums[0] = spread[:width] + 2.0 * scalar_sum * spread[width : 2 * width]
    for a in range(3):
        sums[a + 1] = vectors[a] * double
    pulled[...] = jnp.zeros_like(pulled)

    def backward(step, carry):
        first = step * GROUP
        at = span_of(step * GROUP * atoms, GROUP * atoms)
        highs, lows = [], []
        for j in range(GROUP):
            here = span_of((step * GROUP + j) * atoms, atoms)
            r = [weights_all[a * width : (a + 1) * width, here] for a in range(4)]
            u = units(first, j)
            ga = [sums[a] for a in range(4)]
            flow = ga[1] * u[0] + ga[2] * u[1] + ga[3] * u[2]
            pull = r[3] * ga[0]
            given = [r[0] * ga[0] + r[1] * flow] + [pull * u[a] + r[2] * ga[a + 1] for a in range(3)]
            high, low = parts(jnp.concatenate(given, axis=0))
            highs.append(high)
            lows.append(low)
        split = jnp.concatenate(highs + lows, axis=1)
        chosen = jnp.concatenate([onehot[:atoms, at], onehot[2 * atoms : 2 * atoms + ghost_rows, at]], axis=0)
        pulled[...] += dot_nt(jnp.concatenate([chosen, chosen], axis=1), split)
        return carry

    over_groups(slots // GROUP, backward, 0)
    own_pull[...] = pulled[:atoms]
    start = atoms
    fill = jnp.zeros((8, depth - extras.shape[2]), f32)
    for out, which in ((back_minus, 1), (back_plus, 0), (back_prev, 3), (back_next, 2)):
        count = out.shape[0] - 8
        out[:count] = pulled[start : start + count]
        out[count:] = jnp.concatenate([extras[which], fill], axis=1)
        start += count


def edge_kernel(geo, slopes, outer, picked_all, weights_all, sums, geo_pull):
    slots, atoms = geo.shape[1], geo.shape[2]
    width = sums.shape[1]

    def group(step, carry):
        first = step * GROUP
        slope = dot(outer[...], slopes[:, span_of(step * GROUP * atoms, GROUP * atoms)])
        for j in range(GROUP):
            span = slice(j * atoms, (j + 1) * atoms)
            here = span_of((step * GROUP + j) * atoms, atoms)
            p = [picked_all[a * width : (a + 1) * width, here] for a in range(4)]
            r = [weights_all[a * width : (a + 1) * width, here] for a in (1, 3)]
            s = [slope[a * width : (a + 1) * width, span] for a in range(4)]
            u = [geo[a, pl.ds(first + j, 1), :] for a in range(3)]
            ga = [sums[a] for a in range(4)]
            along = p[1] * u[0] + p[2] * u[1] + p[3] * u[2]
            flow = ga[1] * u[0] + ga[2] * u[1] + ga[3] * u[2]
            cross = p[1] * ga[1] + p[2] * ga[2] + p[3] * ga[3]
            stretch = p[0] * (s[0] * ga[0] + s[1] * flow) + s[2] * cross + s[3] * (along * ga[0])
            geo_pull[0, pl.ds(first + j, 1), :] = jnp.sum(stretch, axis=0, keepdims=True)
            lean = r[0] * p[0]
            pull = r[1] * ga[0]
            for a in range(3):
                turn = lean * ga[a + 1] + pull * p[a + 1]
                geo_pull[a + 1, pl.ds(first + j, 1), :] = jnp.sum(turn, axis=0, keepdims=True)
        return carry

    over_groups(slots // GROUP, group, 0)


def slope_kernel(
    geo, kinds, after, embedding, radial_in, radial_mid, radial_out, node_one, node_two, readout_linear,
    scalar_slope, vector_slope, vector_value, turned_high, turned_low, linear,
):
    slots, atoms = kinds.shape
    width = node_one.shape[1]
    species_count, basis_count = embedding.shape[0], radial_in.shape[0]
    inner = weight_stack_t(radial_in[...])
    mid_a, mid_b = weight_stack(radial_mid[0]), weight_stack(radial_mid[1])
    outer = weight_stack_t(radial_out[...])
    lifted = species_matrix(node_one[0], embedding[...])
    linear[...] = jnp.broadcast_to(column(readout_linear[...]), linear.shape)
    mixings = [node_one[i] for i in (1, 2, 3, 4, 5)] + [node_two[0], node_two[1]]
    turned = jnp.concatenate([jnp.transpose(m) for m in mixings], axis=0)
    turned_high[...], turned_low[...] = parts(turned)

    def group(step, carry):
        first = step * GROUP
        at = span_of(step * GROUP * atoms, GROUP * atoms)
        value, slope = basis_group(geo, first, basis_count, True)
        h, dh = hidden_pairs(value, slope, inner, mid_a, mid_b)
        picked = picked_group(lifted, geo, kinds, first, species_count)
        weights_slope = dot(outer, value_stack(dh))
        scalar_slope[:, at] = weights_slope[:width] * picked
        vector_slope[:, at] = weights_slope[width:] * picked
        vector_value[:, at] = dot(outer[width:], value_stack(h)) * picked
        return carry

    over_groups(slots // GROUP, group, 0)


def third_kernel(
    facts, geo, sums, geo_pull, scalar_pull, own_pull, ret_minus, ret_plus, ret_prev, ret_next,
    onehot, scalar_slope, vector_slope, vector_value, turned_high, turned_low, linear,
    everyone, came,
    pieces, pulls, flat, *, moves, slab_rows, sub_rows,
):
    slots, atoms = geo.shape[1], geo.shape[2]
    width = scalar_pull.shape[0]
    pick = send_onehot(facts, 0, slab_rows, sub_rows).astype(bf16)
    returned = jnp.concatenate(
        [ret_plus[:slab_rows], ret_minus[:slab_rows], ret_next[:sub_rows], ret_prev[:sub_rows]], axis=0
    )
    high, low = parts(returned)
    total = jnp.transpose(own_pull[...] + dot(pick, high) + dot(pick, low))
    x_pull = total[:width]
    y_pull = jnp.concatenate([total[a * width : (a + 1) * width] for a in (1, 2, 3)], axis=1)

    def turned(i, count=1):
        at = slice(i * width, (i + count) * width)
        return turned_high[at, :], turned_low[at, :]

    scalars = product(turned(5), x_pull) + linear[...] + scalar_pull[...]
    moved = product(turned(6), y_pull)
    gv = [moved[:, a * atoms : (a + 1) * atoms] for a in range(3)]
    scalar_sum, gate = sums[0], sums[4]
    vectors = [sums[1], sums[2], sums[3]]
    spread = product(turned(0, 3), scalars)
    mixed = product(turned(3), moved)
    gated = product(turned(4), gv[0] * vectors[0] + gv[1] * vectors[1] + gv[2] * vectors[2])
    pulls[0] = spread[:width] + 2.0 * scalar_sum * spread[width : 2 * width] + gated
    double = 2.0 * spread[2 * width :]
    for a in range(3):
        pulls[a + 1] = vectors[a] * double + mixed[:, a * atoms : (a + 1) * atoms] + gate * gv[a]

    def contract(step, carry):
        first = step * GROUP
        for j in range(GROUP):
            here = span_of((step * GROUP + j) * atoms, atoms)
            row = pl.ds(first + j, 1)
            ga = [pulls[a] for a in range(4)]
            u = [geo[a, row, :] for a in range(3)]
            flow = ga[1] * u[0] + ga[2] * u[1] + ga[3] * u[2]
            stretch = scalar_slope[:, here] * ga[0] + vector_slope[:, here] * flow
            value = vector_value[:, here]
            flat[0, row, :] = jnp.sum(stretch, axis=0, keepdims=True)
            for a in range(3):
                flat[a + 1, row, :] = jnp.sum(value * ga[a + 1], axis=0, keepdims=True)
        return carry

    over_groups(slots // GROUP, contract, 0)
    stretch = flat[0] + geo_pull[0]
    turn = [flat[a + 1] + geo_pull[a + 1] for a in range(3)]
    u = [geo[a] for a in range(3)]
    inner = turn[0] * u[0] + turn[1] * u[1] + turn[2] * u[2]
    gradient = [stretch * u[a] + (turn[a] - inner * u[a]) * geo[5] for a in range(3)]
    at_row = iota((8, atoms), 0)
    own = jnp.zeros((8, atoms), f32)
    for a in range(3):
        flat[a] = gradient[a]
        own = jnp.where(at_row == a, jnp.sum(gradient[a], axis=0, keepdims=True), own)

    def push(step, carry):
        blocks = []
        for j in range(GROUP):
            row = pl.ds(step * GROUP + j, 1)
            block = jnp.where(at_row == 0, flat[0, row, :], jnp.where(at_row == 1, flat[1, row, :], flat[2, row, :]))
            blocks.append(block)
        block = jnp.concatenate(blocks, axis=1)
        top = block.astype(bf16).astype(f32)
        rest = block - top
        mid = rest.astype(bf16).astype(f32)
        split = jnp.concatenate([top, mid, rest - mid], axis=0).astype(bf16)
        at = span_of(step * GROUP * atoms, GROUP * atoms)
        chosen = jnp.concatenate([onehot[:atoms, at], onehot[2 * atoms : 2 * atoms + ghost_rows, at]], axis=0)
        return carry + dot_nt(chosen, split)

    ghost_rows = onehot.shape[0] // 2 - atoms
    zero = jnp.zeros((onehot.shape[0] // 2, 24), f32)
    pushed = over_groups(slots // GROUP, push, zero)
    pushed = jnp.transpose(pushed)
    pushed = (pushed[:8] + pushed[8:16] + pushed[16:]) * (1.0 / neighbor_norm)
    own = own - pushed[:, :atoms]
    velocities, mass = facts[1:4], facts[8:9]
    pieces[0:3] = (own * facts[7:8])[:3]
    blocks = ((ret_minus, slab_rows), (ret_plus, slab_rows), (ret_prev, sub_rows), (ret_next, sub_rows))
    start = atoms
    ghost_lines = [[0.0] * 3 for _ in range(3)]
    for i, (ref, count) in enumerate(blocks):
        told = ref[count : count + 8, :count]
        force = -pushed[:, start : start + count]
        start += count
        for a in range(3):
            for b in range(3):
                ghost_lines[a][b] = ghost_lines[a][b] + told[a + 1 : a + 2] * force[b : b + 1]
        scaled = force * told[7:8]
        top = scaled.astype(bf16).astype(f32)
        rest = scaled - top
        mid = rest.astype(bf16).astype(f32)
        split = jnp.concatenate([top, mid, rest - mid], axis=0).astype(bf16)
        place = (iota((atoms, count), 0) == told[0:1].astype(jnp.int32)).astype(bf16)
        spread = dot_nt(split, place)
        pieces[3 * i + 3 : 3 * i + 6] = (spread[:8] + spread[8:16] + spread[16:])[:3]
    came[...] = jnp.zeros_like(came)
    for i, (ref, count) in enumerate(blocks):
        came[:, i * moves : (i + 1) * moves] = ref[count : count + 8, atoms : atoms + moves]

    def line(a, b):
        start = velocities[a : a + 1] * velocities[b : b + 1] * mass
        mixed = velocities[a : a + 1] * own[b : b + 1] + velocities[b : b + 1] * own[a : a + 1]
        return start + time_step * mixed - jnp.sum(u[a] * geo[4] * gradient[b], axis=0, keepdims=True)

    lines = jnp.concatenate([line(a, b) for a in range(3) for b in range(3)] + [jnp.zeros((7, atoms), f32)], axis=0)
    ghosts = [time_step * (ghost_lines[a][b] + ghost_lines[b][a]) for a in range(3) for b in range(3)]
    ghosts = jnp.concatenate(ghosts + [jnp.zeros((7, slab_rows), f32)], axis=0)
    summed = jnp.sum(lines, axis=1, keepdims=True) + jnp.sum(ghosts, axis=1, keepdims=True)
    row = jnp.zeros((1, atoms), f32)
    for i in range(9):
        row = jnp.where(iota((1, atoms), 1) == i, summed[i : i + 1], row)
    pieces[15:16] = row
    for i in range(everyone.shape[0]):
        everyone[i] = pieces[...]


def determinant(m):
    return (
        m[0][0] * (m[1][1] * m[2][2] - m[1][2] * m[2][1])
        - m[0][1] * (m[1][0] * m[2][2] - m[1][2] * m[2][0])
        + m[0][2] * (m[1][0] * m[2][1] - m[1][1] * m[2][0])
    )


def inverse(m):
    whole = determinant(m)
    return [
        [
            (
                m[(j + 1) % 3][(i + 1) % 3] * m[(j + 2) % 3][(i + 2) % 3]
                - m[(j + 1) % 3][(i + 2) % 3] * m[(j + 2) % 3][(i + 1) % 3]
            )
            / whole
            for j in range(3)
        ]
        for i in range(3)
    ]


def fifth_kernel(
    pieces, own_facts, came, box, box_speed,
    forces_out, velocities_out, positions_out, arrivals, new_box, new_box_speed,
    whole, *, atoms_all, slab_count, sub_count,
):
    atoms = own_facts.shape[1]
    velocities, positions = own_facts[1:4], own_facts[4:7]
    devices = slab_count * sub_count
    sub = lax.rem(iota((devices, atoms), 0), sub_count)

    def row_of_all(r):
        return pieces[:, r, :]

    def piece(i, a):
        return row_of_all(3 * i + a)

    def moved(x, step):
        return pltpu.roll(x, (-step) % devices, 0)

    for a in range(3):
        total = piece(0, a) + moved(piece(1, a), sub_count) + moved(piece(2, a), -sub_count)
        x = piece(3, a)
        total = total + jnp.where(sub == sub_count - 1, moved(x, 1 - sub_count), moved(x, 1))
        x = piece(4, a)
        whole[a] = total + jnp.where(sub == 0, moved(x, sub_count - 1), moved(x, -1))
    squares = {}
    for a in range(3):
        for b in range(a, 3):
            squares[a, b] = jnp.sum(whole[a] * whole[b], axis=0, keepdims=True)
    order = list(squares)
    squares = jnp.concatenate([squares[k] for k in order] + [jnp.zeros((2, atoms), f32)], axis=0)
    squares = jnp.sum(squares, axis=1, keepdims=True)
    rest = jnp.sum(row_of_all(15), axis=0, keepdims=True)
    stress = [[None] * 3 for _ in range(3)]
    for i in range(3):
        for j in range(3):
            at = order.index((min(i, j), max(i, j)))
            stress[i][j] = rest[:, 3 * i + j : 3 * i + j + 1] + (time_step * time_step) * squares[at : at + 1]
    slab_at, sub_at = lax.axis_index("slab"), lax.axis_index("sub")
    mine = slab_at * sub_count + sub_at
    root, mass = own_facts[7:8], own_facts[8:9]
    for a in range(3):
        force = whole[a, pl.ds(mine, 1), :] * (mass * root)
        forces_out[a : a + 1, :] = force
        velocities_out[a : a + 1, :] = velocities[a : a + 1, :] + time_step * force / mass
    lane, row = iota((8, atoms), 1), iota((8, atoms), 0)
    facts = came[...]
    index = jnp.broadcast_to(facts[0:1].astype(jnp.int32), (8, atoms))
    count = arrivals.shape[1] // 4
    picked = jnp.zeros((8, atoms), f32)
    for i, (slab_step, sub_step) in enumerate(((-1, 0), (1, 0), (0, -1), (0, 1))):
        slab = lax.rem(slab_at + (slab_step + slab_count), slab_count)
        source = slab * sub_count + lax.rem(sub_at + (sub_step + sub_count), sub_count)
        force = [whole[a, pl.ds(source, 1), :] for a in range(3)]
        force = jnp.where(row == 0, force[0], jnp.where(row == 1, force[1], force[2]))
        found = jnp.take_along_axis(force, index, axis=1)
        picked = jnp.where((lane >= i * count) & (lane < (i + 1) * count), found, picked)
    speeds = [facts[1 + a : 2 + a] + time_step * picked[a : a + 1] * facts[7:8] for a in range(3)]

    def spread(value):
        return jnp.full((1, atoms), value, f32)

    old = [[spread(box[i, j]) for j in range(3)] for i in range(3)]
    volume = determinant(old)
    old_inverse = inverse(old)
    for i in range(3):
        stress[i][i] = stress[i][i] - outside_pressure * volume
    fresh = [[None] * 3 for _ in range(3)]
    for i in range(3):
        for j in range(3):
            push = stress[i][0] * old_inverse[j][0] + stress[i][1] * old_inverse[j][1] + stress[i][2] * old_inverse[j][2]
            speed = spread(box_speed[i, j]) + time_step * push / (box_mass * atoms_all)
            fresh[i][j] = old[i][j] + time_step * speed
            new_box_speed[i : i + 1, j : j + 1] = speed[:, :1]
            new_box[i : i + 1, j : j + 1] = fresh[i][j][:, :1]
    new_inverse = inverse(fresh)
    for i in range(3):
        move = sum(new_inverse[i][j] * velocities_out[j : j + 1, :] for j in range(3))
        positions_out[i : i + 1, :] = positions[i : i + 1, :] + time_step * move
    for i in range(3):
        move = sum(new_inverse[i][j] * speeds[j] for j in range(3))
        arrivals[i : i + 1, :] = (facts[4 + i : 5 + i] + time_step * move)[:, : 4 * count]
        arrivals[3 + i : 4 + i, :] = speeds[i][:, : 4 * count]


VM = pl.BlockSpec(memory_space=pltpu.VMEM)
HB = pl.BlockSpec(memory_space=pltpu.HBM)
SM = pl.BlockSpec(memory_space=pltpu.SMEM)


def shape(*dims, dtype=f32):
    return jax.ShapeDtypeStruct(dims, dtype)


def call(kernel, outs, scalar_inputs=(), far_inputs=False, far_outputs=(), scratch=(), flops=0, vmem=16, name=None):
    def run(*args):
        moved = sum(math.prod(x.shape) * x.dtype.itemsize for x in list(args) + list(outs))
        return pl.pallas_call(
            kernel,
            out_shape=tuple(outs),
            in_specs=[HB if far_inputs else SM if i in scalar_inputs else VM for i in range(len(args))],
            out_specs=tuple(HB if i in far_outputs else VM for i in range(len(outs))),
            scratch_shapes=list(scratch),
            compiler_params=pltpu.CompilerParams(vmem_limit_bytes=vmem * 1024 * 1024),
            cost_estimate=pl.CostEstimate(flops=flops, bytes_accessed=moved, transcendentals=0),
            name=name,
        )(*args)

    return run


def body(
    positions, velocities, species, ghost_species, neighbours, slot_mask, edge_vectors, send_slab, send_sub, migrants,
    embedding, energy_shift, masses, radial_one_in, radial_one_mid, radial_one_out, node_one,
    radial_two_in, radial_two_mid, radial_two_out, node_two, readout_linear, readout_hidden, readout_out,
    box_matrix, box_velocity,
):
    slots, atoms = neighbours.shape
    width = node_one.shape[1]
    hidden = radial_one_mid.shape[1]
    depth = 4 * width
    ghost_slab, ghost_sub = send_slab.shape[1], send_sub.shape[1]
    extended = atoms + 2 * ghost_slab + 2 * ghost_sub
    edges = slots * atoms
    devices = lax.axis_size("slab") * lax.axis_size("sub")
    species_row = species.reshape(1, atoms)
    ghost_row = ghost_species.reshape(1, -1)
    linear_row = readout_linear.reshape(1, -1)
    out_row = readout_out.reshape(1, -1)
    radial_one_in, radial_one_out = jnp.transpose(radial_one_in), jnp.transpose(radial_one_out)
    radial_two_in, radial_two_out = jnp.transpose(radial_two_in), jnp.transpose(radial_two_out)

    first_inputs = (
        edge_vectors, slot_mask, neighbours, species_row, ghost_row, embedding,
        radial_one_in, radial_one_mid, radial_one_out, node_one, send_slab, send_sub,
        velocities, positions, migrants, masses.reshape(1, -1), energy_shift.reshape(1, -1),
        readout_hidden, linear_row, out_row, radial_two_in, radial_two_mid, radial_two_out, node_two,
    )
    packed_rows = (
        8 * width + 6 * packed_step(slots) + FACTS + 6 * hidden + radial_two_in.shape[0] + packed_step(slots)
        + readout_hidden.shape[0] + 8
    )
    kinds, sums, packed, to_minus, to_plus, to_prev, to_next = call(
        first_kernel,
        (
            shape(slots, atoms, dtype=jnp.int32),
            shape(5, width, atoms),
            shape(packed_rows, atoms),
            shape(ghost_slab, depth),
            shape(ghost_slab, depth),
            shape(ghost_sub, depth),
            shape(ghost_sub, depth),
        ),
        far_inputs=True,
        far_outputs=(1, 2),
        scratch=(
            pltpu.VMEM((6, slots, atoms), f32),
            pltpu.VMEM((packed_rows, atoms), f32),
            pltpu.VMEM((5, width, atoms), f32),
        )
        + tuple(pltpu.VMEM(x.shape, x.dtype) for x in first_inputs)
        + (pltpu.SemaphoreType.DMA((FIRST_INPUTS,)), pltpu.SemaphoreType.DMA((4,))),
        flops=6 * edges * 26000,
        vmem=56,
        name="layer_one",
    )(
        *first_inputs
    )
    from_minus, from_plus, from_prev, from_next = trade(to_minus, to_plus, to_prev, to_next)

    def radial(*refs):
        radial_kernel(
            *refs,
            slab_rows=ghost_slab,
            sub_rows=ghost_sub,
            moves=migrants.shape[1],
            basis_count=radial_two_in.shape[0],
        )

    (
        weights_all, slopes, onehot, outer, forward_high, forward_low, backward_high, backward_low,
        geo, own_table, scalars, extras, facts, heads,
    ) = call(
        radial,
        (
            shape(depth, edges),
            shape(3 * hidden, edges, dtype=bf16),
            shape(2 * extended, edges, dtype=bf16),
            shape(depth, 3 * hidden, dtype=bf16),
            shape(width, 3 * width, dtype=bf16),
            shape(width, 3 * width, dtype=bf16),
            shape(3 * width, width, dtype=bf16),
            shape(3 * width, width, dtype=bf16),
            shape(6, slots, atoms),
            shape(depth, 2 * atoms, dtype=bf16),
            shape(width, atoms),
            shape(4, 8, 2 * atoms),
            shape(FACTS, atoms),
            shape(readout_hidden.shape[0] + 8, atoms),
        ),
        flops=12 * edges * 10000,
        vmem=12,
        name="radial_two",
    )(
        packed,
    )

    energy, scalar_pull, picked_all, pulls, own_pull, back_minus, back_plus, back_prev, back_next = call(
        second_kernel,
        (
            shape(1, atoms),
            shape(width, atoms),
            shape(depth, edges),
            shape(4, width, atoms),
            shape(atoms, depth),
            shape(ghost_slab + 8, depth),
            shape(ghost_slab + 8, depth),
            shape(ghost_sub + 8, depth),
            shape(ghost_sub + 8, depth),
        ),
        scratch=(pltpu.VMEM((depth, 2 * extended), bf16), pltpu.VMEM((extended, depth), f32)),
        flops=4 * edges * depth * extended * 2,
        vmem=28,
        name="layer_two",
    )(
        geo, own_table, from_minus, from_plus, from_prev, from_next, scalars, extras,
        weights_all, onehot, forward_high, forward_low, backward_high, backward_low, heads,
    )
    ret_minus, ret_plus, ret_prev, ret_next = trade(back_minus, back_plus, back_prev, back_next)
    (geo_pull,) = call(
        edge_kernel,
        (shape(4, slots, atoms),),
        flops=edges * depth * 400,
        vmem=16,
        name="edge_two",
    )(geo, slopes, outer, picked_all, weights_all, pulls)
    scalar_slope, vector_slope, vector_value, turned_high, turned_low, linear = call(
        slope_kernel,
        (
            shape(width, edges),
            shape(width, edges),
            shape(width, edges),
            shape(7 * width, width, dtype=bf16),
            shape(7 * width, width, dtype=bf16),
            shape(width, atoms),
        ),
        flops=12 * edges * 20000,
        vmem=12,
        name="radial_one",
    )(
        geo, kinds, scalar_pull, embedding, radial_one_in, radial_one_mid, radial_one_out, node_one, node_two, linear_row,
    )


    def back(*refs):
        third_kernel(*refs, moves=migrants.shape[1], slab_rows=ghost_slab, sub_rows=ghost_sub)

    everyone, came = call(
        back,
        (shape(devices, 16, atoms), shape(8, atoms)),
        scratch=(
            pltpu.VMEM((16, atoms), f32),
            pltpu.VMEM((4, width, atoms), f32),
            pltpu.VMEM((4, slots, atoms), f32),
        ),
        flops=6 * edges * 1000,
        vmem=12,
        name="layer_one_back",
    )(
        facts, geo, sums, geo_pull, scalar_pull, own_pull, ret_minus, ret_plus, ret_prev, ret_next,
        onehot, scalar_slope, vector_slope, vector_value, turned_high, turned_low, linear,
    )
    everyone = lax.all_to_all(everyone, ("slab", "sub"), 0, 0, tiled=True)

    def last(*refs):
        fifth_kernel(
            *refs, atoms_all=atoms * devices, slab_count=lax.axis_size("slab"), sub_count=lax.axis_size("sub")
        )

    forces, new_velocities, new_positions, arrivals, new_box, new_box_velocity = call(
        last,
        (
            shape(3, atoms), shape(3, atoms), shape(3, atoms), shape(6, 4 * migrants.shape[1]),
            shape(3, 3), shape(3, 3),
        ),
        scalar_inputs=(3, 4),
        scratch=(pltpu.VMEM((3, devices, atoms), f32),),
        flops=1000000,
        vmem=8,
        name="box",
    )(everyone, facts, came, box_matrix, box_velocity)
    return energy.reshape(atoms), forces, new_velocities, new_positions, arrivals, new_box, new_box_velocity


def solution(mesh):
    split = ("slab", "sub")
    one, two, three, copied = P(split), P(None, split), P(None, None, split), P()
    placed = (two, two, one, one, two, two, three, two, two, two) + (copied,) * 16
    return jax.shard_map(
        body,
        mesh=mesh,
        in_specs=placed,
        out_specs=(one, two, two, two, two, copied, copied),
        check_vma=False,
    )
```

profile of v0, /device:TPU:0, one launch (start us, length us, event | category | flops | bytes accessed | tf_op | source)
XLA Modules:
  0.0 56.0 jit_solution(10719188394953625224)
XLA Ops:
  0.6 7.0 %layer_one.1 = (s32[20,128]{1,0:T(8,128)}, f32[5,128,128]{2,1,0:T(8,128)}, f32[1624,128]{1,0:T(8,128)}, f32[48,512]{1,0:T(8,128)}, f32[48,512]{1,0:T(8,128)}, /*index=5*/f32[48,512]{1,0:T(8,128)}, f32[48,512]{1,0:T(8,128)}) custom-call(f32[3,20,128]{2,1,0:T(8,128)} %refs_0_.1, s32[20,128]{1,0:T(8,128)} %refs_1_.1, s32[20,128]{1,0:T(8,128)} %refs_2_.1, ...), custom_call_target="tpu_custom_call" | custom-call | flops 399360000 | bytes 2619072 | tf_op jit(solution)/shard_map/layer_one/pallas_call | solution.py:809
  7.7 0.5 collective-permute-start
  8.2 5.2 %collective-permute-start.1 = (f32[48,512]{1,0:T(8,128)}, f32[48,512]{1,0:T(8,128)S(1)}, u32[]{:S(2)}, u32[]{:S(2)}) collective-permute-start(f32[48,512]{1,0:T(8,128)} %get-tuple-element.55), channel_id=1, source_target_pairs={{2,0},{4,2},{6,4},{8,6},{10,8},{12,10},{14,12},{16,14},{18,16},{20... | collective-permute-start | bytes 294920 | tf_op jit(solution)/shard_map/ppermute | solution.py:23
  13.4 1.7 %collective-permute-start.2 = (f32[48,512]{1,0:T(8,128)}, f32[48,512]{1,0:T(8,128)S(1)}, u32[]{:S(2)}, u32[]{:S(2)}) collective-permute-start(f32[48,512]{1,0:T(8,128)} %get-tuple-element.56), channel_id=1, source_target_pairs={{1,0},{0,1},{3,2},{2,3},{5,4},{4,5},{7,6},{6,7},{9,8},{8,9},{11,10... | collective-permute-start | bytes 294920 | tf_op jit(solution)/shard_map/ppermute | solution.py:23
  15.1 0.3 collective-permute-start.3
  15.4 1.1 %copy-done.10 = f32[1624,128]{1,0:T(8,128)S(1)} copy-done((f32[1624,128]{1,0:T(8,128)S(1)}, f32[1624,128]{1,0:T(8,128)}, u32[]{:S(2)}) %copy-start.10) | copy-done | bytes 831512
  16.6 4.1 %radial_two.1 = (f32[512,2560]{1,0:T(8,128)S(1)}, bf16[192,2560]{1,0:T(8,128)(2,1)S(1)}, bf16[640,2560]{1,0:T(8,128)(2,1)S(1)}, bf16[512,192]{1,0:T(8,128)(2,1)S...) custom-call(f32[1624,128]{1,0:T(8,128)S(1)} %copy-done.10), custom_call_target="tpu_custom_call" | custom-call | flops 307200000 | bytes 11366400 | tf_op jit(solution)/shard_map/radial_two/pallas_call | solution.py:809
  20.7 0.0 collective-permute-done.1.from_plus
  20.7 0.0 collective-permute-done.2.from_prev
  20.7 5.8 %layer_two.1 = (f32[1,128]{1,0:T(1,128)}, f32[128,128]{1,0:T(8,128)S(1)}, f32[512,2560]{1,0:T(8,128)S(1)}, f32[4,128,128]{2,1,0:T(8,128)S(1)}, f32[128,512]{1,0:...) custom-call(f32[6,20,128]{2,1,0:T(8,128)S(1)} %get-tuple-element.52., ...), custom_call_target="tpu_custom_call" | custom-call | flops 3355443200 | bytes 16032256 | tf_op jit(solution)/shard_map/layer_two/pallas_call | solution.py:809
  26.5 0.1 collective-permute-start.4
  26.6 4.4 %collective-permute-start.5 = (f32[56,512]{1,0:T(8,128)S(1)}, f32[56,512]{1,0:T(8,128)S(1)}, u32[]{:S(2)}, u32[]{:S(2)}) collective-permute-start(f32[56,512]{1,0:T(8,128)S(1)} %get-tuple-element.77), channel_id=1, source_target_pairs={{2,0},{4,2},{6,4},{8,6},{10,8},{12,10},{14,12},{16,14},{18,16},{20... | collective-permute-start | bytes 344072 | tf_op jit(solution)/shard_map/ppermute | solution.py:23
  31.0 1.7 %collective-permute-start.6 = (f32[56,512]{1,0:T(8,128)S(1)}, f32[56,512]{1,0:T(8,128)S(1)}, u32[]{:S(2)}, u32[]{:S(2)}) collective-permute-start(f32[56,512]{1,0:T(8,128)S(1)} %get-tuple-element.78), channel_id=1, source_target_pairs={{1,0},{0,1},{3,2},{2,3},{5,4},{4,5},{7,6},{6,7},{9,8},{8,9},{11,10... | collective-permute-start | bytes 344072 | tf_op jit(solution)/shard_map/ppermute | solution.py:23
  32.7 0.3 collective-permute-start.7
  33.1 0.0 copy-start.7
  33.1 0.0 copy-start.8
  33.1 0.0 copy-start.9
  33.1 2.3 %edge_two.1.refs_3_ = f32[4,20,128]{2,1,0:T(8,128)S(1)} custom-call(f32[6,20,128]{2,1,0:T(8,128)S(1)} %get-tuple-element.52.geo.refs_1_, bf16[192,2560]{1,0:T(8,128)(2,1)S(1)} %get-tuple-element.70.slopes, bf16[512,192]{1,0:T(8,128)(2,1)S(1)} %get-tuple-element.71.outer, f32[512,2560]{1,0:T(8,128)S(1)} %get-tuple-element.72.picked_all, ...), custom_call_target="tpu_custom_call" | custom-call | flops 524288000 | bytes 12029952 | tf_op jit(solution)/shard_map/edge_two/pallas_call | solution.py:809
  35.5 3.4 %radial_one.1 = (f32[128,2560]{1,0:T(8,128)S(1)}, f32[128,2560]{1,0:T(8,128)S(1)}, f32[128,2560]{1,0:T(8,128)S(1)}, bf16[896,128]{1,0:T(8,128)(2,1)S(1)}, bf16[8...) custom-call(f32[6,20,128]{2,1,0:T(8,128)S(1)} %get-tuple-element.52.geo.refs_1_, s32[20,128]{1,0:T(8,128)S(1)} %copy-done.11, ...), custom_call_target="tpu_custom_call" | custom-call | flops 614400000 | bytes 5419520 | tf_op jit(solution)/shard_map/radial_one/pallas_call | solution.py:809
  39.0 0.0 copy-start.1
  39.0 0.0 copy-start.2
  39.0 2.8 %layer_one_back.1 = (f32[32,16,128]{2,1,0:T(8,128)S(1)}, f32[8,128]{1,0:T(8,128)S(1)}) custom-call(f32[16,128]{1,0:T(8,128)S(1)} %get-tuple-element.68.refs_0_.refs_1_, f32[6,20,128]{2,1,0:T(8,128)S(1)} %get-tuple-element.52.geo.refs_1_, f32[5,128,128]{2,1,0:T(8,128)S(1)} %copy-done, f32[4,20,128]{2,1,0:T(8,128)S(1)} %edge_two.1.refs_3_, ...), custom_call_target="tpu_custom_call" | custom-call | flops 15360000 | bytes 9224192 | tf_op jit(solution)/shard_map/layer_one_back/pallas_call | solution.py:809
  41.8 12.6 %all_to_all.5.refs_0_ = f32[32,16,128]{2,1,0:T(8,128)S(1)} all-to-all(f32[32,16,128]{2,1,0:T(8,128)S(1)} %get-tuple-element.87), channel_id=1, replica_groups=mesh['slab'=16,'sub'=2] {'slab','sub'}, dimensions={0} | all-to-all | bytes 524288 | tf_op jit(solution)/shard_map/all_to_all | solution.py:984
  54.4 1.6 %box.1 = (f32[3,128]{1,0:T(4,128)}, f32[3,128]{1,0:T(4,128)}, f32[3,128]{1,0:T(4,128)}, f32[6,16]{1,0:T(8,128)}, f32[3,3]{1,0:T(4,128)}, /*index=5*/f32[3,3]{1,0:T(4,128)}) custom-call(f32[32,16,128]{2,1,0:T(8,128)S(1)} %all_to_all.5.refs_0_, f32[16,128]{1,0:T(8,128)S(1)} %get-tuple-element.68.refs_0_.refs_1_, f32[8,128]{1,0:T(8,128)S(1)} %get-tuple-element.88.refs_2_, ...), custom_call_target="tpu_custom_call" | custom-call | flops 1000000 | bytes 279568 | tf_op jit(solution)/shard_map/box/pallas_call | solution.py:809
  (24 shorter events, 0.1 us)
Async XLA Ops:
  7.7 13.0 %collective-permute-start = (f32[48,512]{1,0:T(8,128)}, f32[48,512]{1,0:T(8,128)S(1)}, u32[]{:S(2)}, u32[]{:S(2)}) collective-permute-start(f32[48,512]{1,0:T(8,128)} %get-tuple-element.54), channel_id=1, source_target_pairs={{30,0},{0,2},{2,4},{4,6},{6,8},{8,10},{10,12},{12,14},{14,16},{16,... | collective-permute-start | bytes 294920 | tf_op jit(solution)/shard_map/ppermute | solution.py:23
  8.2 12.5 %collective-permute-start.1 = (f32[48,512]{1,0:T(8,128)}, f32[48,512]{1,0:T(8,128)S(1)}, u32[]{:S(2)}, u32[]{:S(2)}) collective-permute-start(f32[48,512]{1,0:T(8,128)} %get-tuple-element.55), channel_id=1, source_target_pairs={{2,0},{4,2},{6,4},{8,6},{10,8},{12,10},{14,12},{16,14},{18,16},{20... | collective-permute-start | bytes 294920 | tf_op jit(solution)/shard_map/ppermute | solution.py:23
  13.4 7.3 %collective-permute-start.2 = (f32[48,512]{1,0:T(8,128)}, f32[48,512]{1,0:T(8,128)S(1)}, u32[]{:S(2)}, u32[]{:S(2)}) collective-permute-start(f32[48,512]{1,0:T(8,128)} %get-tuple-element.56), channel_id=1, source_target_pairs={{1,0},{0,1},{3,2},{2,3},{5,4},{4,5},{7,6},{6,7},{9,8},{8,9},{11,10... | collective-permute-start | bytes 294920 | tf_op jit(solution)/shard_map/ppermute | solution.py:23
  15.1 5.6 %collective-permute-start.3 = (f32[48,512]{1,0:T(8,128)}, f32[48,512]{1,0:T(8,128)S(1)}, u32[]{:S(2)}, u32[]{:S(2)}) collective-permute-start(f32[48,512]{1,0:T(8,128)} %get-tuple-element.57), channel_id=1, source_target_pairs={{1,0},{0,1},{3,2},{2,3},{5,4},{4,5},{7,6},{6,7},{9,8},{8,9},{11,10... | collective-permute-start | bytes 294920 | tf_op jit(solution)/shard_map/ppermute | solution.py:23
  15.4 1.1 %copy-start.10 = (f32[1624,128]{1,0:T(8,128)S(1)}, f32[1624,128]{1,0:T(8,128)}, u32[]{:S(2)}) copy-start(f32[1624,128]{1,0:T(8,128)} %get-tuple-element.51.refs_0_) | copy-start | bytes 2494468
  26.5 12.4 %collective-permute-start.4 = (f32[56,512]{1,0:T(8,128)S(1)}, f32[56,512]{1,0:T(8,128)S(1)}, u32[]{:S(2)}, u32[]{:S(2)}) collective-permute-start(f32[56,512]{1,0:T(8,128)S(1)} %get-tuple-element.76), channel_id=1, source_target_pairs={{30,0},{0,2},{2,4},{4,6},{6,8},{8,10},{10,12},{12,14},{14,16},{16,... | collective-permute-start | bytes 344072 | tf_op jit(solution)/shard_map/ppermute | solution.py:23
  26.6 12.4 %collective-permute-start.5 = (f32[56,512]{1,0:T(8,128)S(1)}, f32[56,512]{1,0:T(8,128)S(1)}, u32[]{:S(2)}, u32[]{:S(2)}) collective-permute-start(f32[56,512]{1,0:T(8,128)S(1)} %get-tuple-element.77), channel_id=1, source_target_pairs={{2,0},{4,2},{6,4},{8,6},{10,8},{12,10},{14,12},{16,14},{18,16},{20... | collective-permute-start | bytes 344072 | tf_op jit(solution)/shard_map/ppermute | solution.py:23
  31.0 8.0 %collective-permute-start.6 = (f32[56,512]{1,0:T(8,128)S(1)}, f32[56,512]{1,0:T(8,128)S(1)}, u32[]{:S(2)}, u32[]{:S(2)}) collective-permute-start(f32[56,512]{1,0:T(8,128)S(1)} %get-tuple-element.78), channel_id=1, source_target_pairs={{1,0},{0,1},{3,2},{2,3},{5,4},{4,5},{7,6},{6,7},{9,8},{8,9},{11,10... | collective-permute-start | bytes 344072 | tf_op jit(solution)/shard_map/ppermute | solution.py:23
  32.7 6.3 %collective-permute-start.7 = (f32[56,512]{1,0:T(8,128)S(1)}, f32[56,512]{1,0:T(8,128)S(1)}, u32[]{:S(2)}, u32[]{:S(2)}) collective-permute-start(f32[56,512]{1,0:T(8,128)S(1)} %get-tuple-element.79), channel_id=1, source_target_pairs={{1,0},{0,1},{3,2},{2,3},{5,4},{4,5},{7,6},{6,7},{9,8},{8,9},{11,10... | collective-permute-start | bytes 344072 | tf_op jit(solution)/shard_map/ppermute | solution.py:23
  33.1 2.4 %copy-start.3 = (f32[6,128,128]{2,1,0:T(8,128)S(1)}, f32[6,128,128]{2,1,0:T(8,128)}, u32[]{:S(2)}) copy-start(f32[6,128,128]{2,1,0:T(8,128)} %node_one.1) | copy-start | bytes 1179652
  33.1 2.4 %copy-start.4 = (f32[5,128,128]{2,1,0:T(8,128)S(1)}, f32[5,128,128]{2,1,0:T(8,128)}, u32[]{:S(2)}) copy-start(f32[5,128,128]{2,1,0:T(8,128)} %node_two.1) | copy-start | bytes 983044
  33.1 2.4 %copy-start.5 = (f32[2,64,64]{2,1,0:T(8,128)S(1)}, f32[2,64,64]{2,1,0:T(8,128)}, u32[]{:S(2)}) copy-start(f32[2,64,64]{2,1,0:T(8,128)} %radial_mid.1) | copy-start | bytes 98308
  33.1 2.4 %copy-start.6 = (f32[256,64]{0,1:T(8,128)S(1)}, f32[256,64]{0,1:T(8,128)}, u32[]{:S(2)}) copy-start(f32[256,64]{0,1:T(8,128)} %param.41) | copy-start | bytes 196612
  33.1 2.4 %copy-start.7 = (f32[8,128]{1,0:T(8,128)S(1)}, f32[8,128]{1,0:T(8,128)}, u32[]{:S(2)}) copy-start(f32[8,128]{1,0:T(8,128)} %embedding.1) | copy-start | bytes 12292
  33.1 2.4 %copy-start.8 = (f32[64,8]{0,1:T(8,128)S(1)}, f32[64,8]{0,1:T(8,128)}, u32[]{:S(2)}) copy-start(f32[64,8]{0,1:T(8,128)} %param.39) | copy-start | bytes 6148
  33.1 2.4 %copy-start.9 = (f32[128]{0:T(128)S(1)}, f32[128]{0:T(128)}, u32[]{:S(2)}) copy-start(f32[128]{0:T(128)} %param.47) | copy-start | bytes 1540
  33.1 2.4 %copy-start.11 = (s32[20,128]{1,0:T(8,128)S(1)}, s32[20,128]{1,0:T(8,128)}, u32[]{:S(2)}) copy-start(s32[20,128]{1,0:T(8,128)} %get-tuple-element.80.kinds) | copy-start | bytes 30724
  33.1 5.9 %copy-start = (f32[5,128,128]{2,1,0:T(8,128)S(1)}, f32[5,128,128]{2,1,0:T(8,128)}, u32[]{:S(2)}) copy-start(f32[5,128,128]{2,1,0:T(8,128)} %get-tuple-element.69.refs_2_) | copy-start | bytes 983044
  39.0 15.4 %copy-start.1 = (f32[3,3]{1,0:T(4,128)S(1)}, f32[3,3]{1,0:T(4,128)}, u32[]{:S(2)}) copy-start(f32[3,3]{1,0:T(4,128)} %refs_3_.1) | copy-start | bytes 112
  39.0 15.4 %copy-start.2 = (f32[3,3]{1,0:T(4,128)S(1)}, f32[3,3]{1,0:T(4,128)}, u32[]{:S(2)}) copy-start(f32[3,3]{1,0:T(4,128)} %refs_4_.1) | copy-start | bytes 112
where the time goes:
time: 56.2 us; the launch traced here: 56 us
  Pallas kernels  27 us (48%)
  starting transfers between devices  14.3 us (25%)
  blocking collectives  12.6 us (22%)
  local copies, waits for them, and re-layouts  1.2 us (2%)
  between operations  0.89 us (2%)
    pallas_call x7, Pallas kernels, run(): pl.pallas_call(kernel, out_shape=tuple(outs), in_specs=[HB if far_inputs...  27 us
    ppermute x8, starting transfers between devices, shifted(): lax.ppermute(block, axis, [((i - distance) % count, i) for i in range(cou...  14.3 us
    all_to_all x1, blocking collectives, body(): everyone = lax.all_to_all(everyone, ('slab', 'sub'), 0, 0, tiled=True)  12.6 us
    unnamed x24, local copies, waits for them, and re-layouts  1.2 us
  transfers between devices with their start and end apart: 8, of which 0 were waited for; matrix products, arithmetic and copies ran while one was open for 0% of the time, Pallas kernels for 18%

commit v1 on v0

--- a/solution.py
+++ b/solution.py
@@ -95,35 +95,34 @@
     return 0.5 + 0.5 * jnp.tanh(0.5 * x)
 
 
-def basis(distance, inverse_distance, count, with_slope):
-    orders = (iota((count, distance.shape[1]), 0) + 1).astype(f32)
+def basis(distance, inverse_distance, count):
     scaled = distance * (1.0 / cutoff)
-    angle = orders * (math.pi * scaled)
     second = scaled * scaled
     fourth = second * second
     fifth = fourth * scaled
     sixth = fourth * second
     scale = math.sqrt(2.0 / cutoff)
     envelope = 1.0 + sixth * (-28.0 + scaled * (48.0 - 21.0 * scaled))
-    sine = jnp.sin(angle)
     front = scale * envelope * inverse_distance
-    value = sine * front
-    if not with_slope:
-        return value, None
     slope_envelope = fifth * (-168.0 + scaled * (336.0 - 168.0 * scaled)) * (1.0 / cutoff)
     slope_front = scale * inverse_distance * (slope_envelope - envelope * inverse_distance)
-    slope = sine * slope_front + jnp.cos(angle) * (orders * (math.pi / cutoff)) * front
-    return value, slope
-
-
-def basis_group(geo, first, count, with_slope):
-    found = [
-        basis(geo[4, pl.ds(first + j, 1), :], geo[5, pl.ds(first + j, 1), :], count, with_slope)
-        for j in range(GROUP)
-    ]
-    value = jnp.concatenate([pair[0] for pair in found], axis=1)
-    slope = jnp.concatenate([pair[1] for pair in found], axis=1) if with_slope else None
-    return value, slope
+    angle = math.pi * scaled
+    first_sine, first_cosine = jnp.sin(angle), jnp.cos(angle)
+    sine, cosine = first_sine, first_cosine
+    values, slopes = [], []
+    for order in range(1, count + 1):
+        if order > 1:
+            sine, cosine = (
+                sine * first_cosine + cosine * first_sine,
+                cosine * first_cosine - sine * first_sine,
+            )
+        values.append(sine * front)
+        slopes.append(sine * slope_front + cosine * (front * (order * math.pi / cutoff)))
+    return values, slopes
+
+
+def basis_group(waves, first, start, count):
+    return jnp.concatenate([waves[start : start + count, first + j, :] for j in range(GROUP)], axis=1)
 
 
 def hidden_values(value, inner, mid_a, mid_b):
@@ -193,7 +192,7 @@
         send_slab, send_sub, velocities, positions, migrants, masses, shifts,
         hidden_head, linear_head, out_head, next_in, next_mid, next_out, node_two,
     ) = buffers
-    kinds, far_sums, far_packed, to_minus, to_plus, to_prev, to_next, geo, packed, sums = refs[count : -count - 2]
+    kinds, far_sums, far_packed, to_minus, to_plus, to_prev, to_next, geo, waves, packed, sums = refs[count : -count - 2]
     for copy in copies[:2]:
         copy.wait()
     slots, atoms = mask.shape
@@ -210,6 +209,9 @@
     geo[5] = inverse_distance
     base = 5 * width
     step = packed_step(slots)
+    values, slopes = basis(distance, inverse_distance, radial_in.shape[0])
+    for i, wave in enumerate(values + slopes):
+        waves[i] = wave
     for a in range(6):
         packed[base + a * step : base + a * step + slots] = geo[a]
     for copy in copies[2:5]:
@@ -242,7 +244,7 @@
 
     def group(step, carry):
         first = step * GROUP
-        value, _ = basis_group(geo, first, basis_count, False)
+        value = basis_group(waves, first, 0, basis_count)
         h = hidden_values(value, inner, mid_a, mid_b)
         weights = dot(outer, value_stack(h))
         picked = picked_group(lifted, geo, kinds, first, species_count)
@@ -300,6 +302,9 @@
     packed[start + count : start + count + 1] = linear_head[...]
     packed[start + count + 1 : start + count + 2, : out_head.shape[1]] = out_head[...]
     packed[start + count + 2 : start + count + 3] = shift
+    start += count + 8
+    for i in range(waves.shape[0]):
+        packed[start + i * step : start + i * step + slots] = waves[i]
     early = pltpu.make_async_copy(packed.at[base:], far_packed.at[base:], gone.at[0])
     early.start()
 
@@ -343,7 +348,7 @@
 def radial_kernel(
     packed,
     weights_all, slopes, onehot, outer, forward_high, forward_low, backward_high, backward_low,
-    geo, table, scalars, extras, facts, heads, *, slab_rows, sub_rows, moves, basis_count,
+    geo, table, scalars, extras, facts, heads, waves, *, slab_rows, sub_rows, moves, basis_count,
 ):
     slots, atoms = geo.shape[1:]
     width = scalars.shape[0]
@@ -362,7 +367,11 @@
     start += 2 * inner_rows
     radial_in = packed[start : start + basis_count, :inner_rows]
     first_row = start + basis_count
-    heads[...] = packed[first_row + packed_step(slots) :]
+    start = first_row + packed_step(slots)
+    heads[...] = packed[start : start + heads.shape[0]]
+    start += heads.shape[0]
+    for i in range(2 * basis_count):
+        waves[i] = packed[start + i * packed_step(slots) : start + i * packed_step(slots) + slots]
     table[:, :atoms], table[:, atoms:] = parts(packed[width : 5 * width])
     for a in range(6):
         start = 5 * width + a * packed_step(slots)
@@ -388,7 +397,7 @@
     def group(step, carry):
         first = step * GROUP
         at = span_of(step * GROUP * atoms, GROUP * atoms)
-        value, slope = basis_group(geo, first, basis_count, True)
+        value, slope = (basis_group(waves, first, i * basis_count, basis_count) for i in range(2))
         h, dh = hidden_pairs(value, slope, inner, mid_a, mid_b)
         slopes[:, at] = value_stack(dh)
         blocks = []
@@ -533,7 +542,7 @@
 
 
 def slope_kernel(
-    geo, kinds, after, embedding, radial_in, radial_mid, radial_out, node_one, node_two, readout_linear,
+    geo, waves, kinds, after, embedding, radial_in, radial_mid, radial_out, node_one, node_two, readout_linear,
     scalar_slope, vector_slope, vector_value, turned_high, turned_low, linear,
 ):
     slots, atoms = kinds.shape
@@ -551,7 +560,7 @@
     def group(step, carry):
         first = step * GROUP
         at = span_of(step * GROUP * atoms, GROUP * atoms)
-        value, slope = basis_group(geo, first, basis_count, True)
+        value, slope = (basis_group(waves, first, i * basis_count, basis_count) for i in range(2))
         h, dh = hidden_pairs(value, slope, inner, mid_a, mid_b)
         picked = picked_group(lifted, geo, kinds, first, species_count)
         weights_slope = dot(outer, value_stack(dh))
@@ -849,7 +858,7 @@
     )
     packed_rows = (
         8 * width + 6 * packed_step(slots) + FACTS + 6 * hidden + radial_two_in.shape[0] + packed_step(slots)
-        + readout_hidden.shape[0] + 8
+        + readout_hidden.shape[0] + 8 + 2 * radial_one_in.shape[0] * packed_step(slots)
     )
     kinds, sums, packed, to_minus, to_plus, to_prev, to_next = call(
         first_kernel,
@@ -866,6 +875,7 @@
         far_outputs=(1, 2),
         scratch=(
             pltpu.VMEM((6, slots, atoms), f32),
+            pltpu.VMEM((2 * radial_one_in.shape[0], slots, atoms), f32),
             pltpu.VMEM((packed_rows, atoms), f32),
             pltpu.VMEM((5, width, atoms), f32),
         )
@@ -890,7 +900,7 @@
 
     (
         weights_all, slopes, onehot, outer, forward_high, forward_low, backward_high, backward_low,
-        geo, own_table, scalars, extras, facts, heads,
+        geo, own_table, scalars, extras, facts, heads, waves,
     ) = call(
         radial,
         (
@@ -908,6 +918,7 @@
             shape(4, 8, 2 * atoms),
             shape(FACTS, atoms),
             shape(readout_hidden.shape[0] + 8, atoms),
+            shape(2 * radial_two_in.shape[0], slots, atoms),
         ),
         flops=12 * edges * 10000,
         vmem=12,
@@ -959,7 +970,7 @@
         vmem=12,
         name="radial_one",
     )(
-        geo, kinds, scalar_pull, embedding, radial_one_in, radial_one_mid, radial_one_out, node_one, node_two, linear_row,
+        geo, waves, kinds, scalar_pull, embedding, radial_one_in, radial_one_mid, radial_one_out, node_one, node_two, linear_row,
     )
 
 

time: 56.2 us -> 56.3 us (level)
  transfers between devices with their start and end apart: 8 -> 8, of which waited for: 0 -> 0; matrix products, arithmetic and copies ran while one was open for 0% -> 0% of each run, Pallas kernels for 18% -> 17%
where the time goes in v1:
time: 56.3 us; the launch traced here: 56.1 us
  Pallas kernels  26.9 us (48%)
  starting transfers between devices  14.3 us (25%)
  blocking collectives  12.7 us (23%)
  local copies, waits for them, and re-layouts  1.27 us (2%)
  between operations  0.89 us (2%)
    pallas_call x7, Pallas kernels, run(): pl.pallas_call(kernel, out_shape=tuple(outs), in_specs=[HB if far_inputs...  26.9 us
    ppermute x8, starting transfers between devices, shifted(): lax.ppermute(block, axis, [((i - distance) % count, i) for i in range(cou...  14.3 us
    all_to_all x1, blocking collectives, body(): everyone = lax.all_to_all(everyone, ('slab', 'sub'), 0, 0, tiled=True)  12.7 us
    unnamed x24, local copies, waits for them, and re-layouts  1.27 us
  transfers between devices with their start and end apart: 8, of which 0 were waited for; matrix products, arithmetic and copies ran while one was open for 0% of the time, Pallas kernels for 17%

profile of v1, /device:TPU:0, one launch (start us, length us, event | category | flops | bytes accessed | tf_op | source)
XLA Modules:
  0.0 56.1 jit_solution(6523600969896687493)
XLA Ops:
  0.6 7.0 %layer_one.1 = (s32[20,128]{1,0:T(8,128)}, f32[5,128,128]{2,1,0:T(8,128)}, f32[2008,128]{1,0:T(8,128)}, f32[48,512]{1,0:T(8,128)}, f32[48,512]{1,0:T(8,128)}, /*index=5*/f32[48,512]{1,0:T(8,128)}, f32[48,512]{1,0:T(8,128)}) custom-call(f32[3,20,128]{2,1,0:T(8,128)} %refs_0_.1, s32[20,128]{1,0:T(8,128)} %refs_1_.1, s32[20,128]{1,0:T(8,128)} %refs_2_.1, ...), custom_call_target="tpu_custom_call" | custom-call | flops 399360000 | bytes 2815680 | tf_op jit(solution)/shard_map/layer_one/pallas_call | solution.py:818
  7.6 0.5 collective-permute-start
  8.1 5.1 %collective-permute-start.1 = (f32[48,512]{1,0:T(8,128)}, f32[48,512]{1,0:T(8,128)S(1)}, u32[]{:S(2)}, u32[]{:S(2)}) collective-permute-start(f32[48,512]{1,0:T(8,128)} %get-tuple-element.56), channel_id=1, source_target_pairs={{2,0},{4,2},{6,4},{8,6},{10,8},{12,10},{14,12},{16,14},{18,16},{20... | collective-permute-start | bytes 294920 | tf_op jit(solution)/shard_map/ppermute | solution.py:23
  13.2 1.9 %collective-permute-start.2 = (f32[48,512]{1,0:T(8,128)}, f32[48,512]{1,0:T(8,128)S(1)}, u32[]{:S(2)}, u32[]{:S(2)}) collective-permute-start(f32[48,512]{1,0:T(8,128)} %get-tuple-element.57), channel_id=1, source_target_pairs={{1,0},{0,1},{3,2},{2,3},{5,4},{4,5},{7,6},{6,7},{9,8},{8,9},{11,10... | collective-permute-start | bytes 294920 | tf_op jit(solution)/shard_map/ppermute | solution.py:23
  15.1 0.2 collective-permute-start.3
  15.2 1.2 %copy-done.10 = f32[2008,128]{1,0:T(8,128)S(1)} copy-done((f32[2008,128]{1,0:T(8,128)S(1)}, f32[2008,128]{1,0:T(8,128)}, u32[]{:S(2)}) %copy-start.10) | copy-done | bytes 1028120
  16.4 4.0 %radial_two.1 = (f32[512,2560]{1,0:T(8,128)S(1)}, bf16[192,2560]{1,0:T(8,128)(2,1)S(1)}, bf16[640,2560]{1,0:T(8,128)(2,1)S(1)}, bf16[512,192]{1,0:T(8,128)(2,1)S...) custom-call(f32[2008,128]{1,0:T(8,128)S(1)} %copy-done.10), custom_call_target="tpu_custom_call" | custom-call | flops 307200000 | bytes 11726848 | tf_op jit(solution)/shard_map/radial_two/pallas_call | solution.py:818
  20.5 0.0 collective-permute-done.1.from_plus
  20.5 5.8 %layer_two.1 = (f32[1,128]{1,0:T(1,128)}, f32[128,128]{1,0:T(8,128)S(1)}, f32[512,2560]{1,0:T(8,128)S(1)}, f32[4,128,128]{2,1,0:T(8,128)S(1)}, f32[128,512]{1,0:...) custom-call(f32[6,20,128]{2,1,0:T(8,128)S(1)} %get-tuple-element.53., ...), custom_call_target="tpu_custom_call" | custom-call | flops 3355443200 | bytes 16032256 | tf_op jit(solution)/shard_map/layer_two/pallas_call | solution.py:818
  26.3 0.2 collective-permute-start.4
  26.6 4.4 %collective-permute-start.5 = (f32[56,512]{1,0:T(8,128)S(1)}, f32[56,512]{1,0:T(8,128)S(1)}, u32[]{:S(2)}, u32[]{:S(2)}) collective-permute-start(f32[56,512]{1,0:T(8,128)S(1)} %get-tuple-element.78), channel_id=1, source_target_pairs={{2,0},{4,2},{6,4},{8,6},{10,8},{12,10},{14,12},{16,14},{18,16},{20... | collective-permute-start | bytes 344072 | tf_op jit(solution)/shard_map/ppermute | solution.py:23
  31.0 1.9 %collective-permute-start.6 = (f32[56,512]{1,0:T(8,128)S(1)}, f32[56,512]{1,0:T(8,128)S(1)}, u32[]{:S(2)}, u32[]{:S(2)}) collective-permute-start(f32[56,512]{1,0:T(8,128)S(1)} %get-tuple-element.79), channel_id=1, source_target_pairs={{1,0},{0,1},{3,2},{2,3},{5,4},{4,5},{7,6},{6,7},{9,8},{8,9},{11,10... | collective-permute-start | bytes 344072 | tf_op jit(solution)/shard_map/ppermute | solution.py:23
  32.9 0.2 collective-permute-start.7
  33.1 0.0 copy-start.7
  33.1 0.0 copy-start.8
  33.1 0.0 copy-start.9
  33.1 2.3 %edge_two.1.refs_3_ = f32[4,20,128]{2,1,0:T(8,128)S(1)} custom-call(f32[6,20,128]{2,1,0:T(8,128)S(1)} %get-tuple-element.53.geo.refs_1_, bf16[192,2560]{1,0:T(8,128)(2,1)S(1)} %get-tuple-element.71.slopes, bf16[512,192]{1,0:T(8,128)(2,1)S(1)} %get-tuple-element.72.outer, f32[512,2560]{1,0:T(8,128)S(1)} %get-tuple-element.73.picked_all, ...), custom_call_target="tpu_custom_call" | custom-call | flops 524288000 | bytes 12029952 | tf_op jit(solution)/shard_map/edge_two/pallas_call | solution.py:818
  35.5 3.4 %radial_one.1 = (f32[128,2560]{1,0:T(8,128)S(1)}, f32[128,2560]{1,0:T(8,128)S(1)}, f32[128,2560]{1,0:T(8,128)S(1)}, bf16[896,128]{1,0:T(8,128)(2,1)S(1)}, bf16[8...) custom-call(f32[6,20,128]{2,1,0:T(8,128)S(1)} %get-tuple-element.53.geo.refs_1_, ...), custom_call_target="tpu_custom_call" | custom-call | flops 614400000 | bytes 5583360 | tf_op jit(solution)/shard_map/radial_one/pallas_call | solution.py:818
  39.0 0.0 collective-permute-done.6.refs_8_
  39.0 0.0 copy-start.1
  39.0 0.0 copy-start.2
  39.0 2.8 %layer_one_back.1 = (f32[32,16,128]{2,1,0:T(8,128)S(1)}, f32[8,128]{1,0:T(8,128)S(1)}) custom-call(f32[16,128]{1,0:T(8,128)S(1)} %get-tuple-element.69.refs_0_.refs_1_, f32[6,20,128]{2,1,0:T(8,128)S(1)} %get-tuple-element.53.geo.refs_1_, f32[5,128,128]{2,1,0:T(8,128)S(1)} %copy-done, f32[4,20,128]{2,1,0:T(8,128)S(1)} %edge_two.1.refs_3_, ...), custom_call_target="tpu_custom_call" | custom-call | flops 15360000 | bytes 9224192 | tf_op jit(solution)/shard_map/layer_one_back/pallas_call | solution.py:818
  41.8 12.7 %all_to_all.5.refs_0_ = f32[32,16,128]{2,1,0:T(8,128)S(1)} all-to-all(f32[32,16,128]{2,1,0:T(8,128)S(1)} %get-tuple-element.89), channel_id=1, replica_groups=mesh['slab'=16,'sub'=2] {'slab','sub'}, dimensions={0} | all-to-all | bytes 524288 | tf_op jit(solution)/shard_map/all_to_all | solution.py:995
  54.5 1.6 %box.1 = (f32[3,128]{1,0:T(4,128)}, f32[3,128]{1,0:T(4,128)}, f32[3,128]{1,0:T(4,128)}, f32[6,16]{1,0:T(8,128)}, f32[3,3]{1,0:T(4,128)}, /*index=5*/f32[3,3]{1,0:T(4,128)}) custom-call(f32[32,16,128]{2,1,0:T(8,128)S(1)} %all_to_all.5.refs_0_, f32[16,128]{1,0:T(8,128)S(1)} %get-tuple-element.69.refs_0_.refs_1_, f32[8,128]{1,0:T(8,128)S(1)} %get-tuple-element.90.refs_2_, ...), custom_call_target="tpu_custom_call" | custom-call | flops 1000000 | bytes 279568 | tf_op jit(solution)/shard_map/box/pallas_call | solution.py:818
  (24 shorter events, 0.1 us)
Async XLA Ops:
  7.6 12.8 %collective-permute-start = (f32[48,512]{1,0:T(8,128)}, f32[48,512]{1,0:T(8,128)S(1)}, u32[]{:S(2)}, u32[]{:S(2)}) collective-permute-start(f32[48,512]{1,0:T(8,128)} %get-tuple-element.55), channel_id=1, source_target_pairs={{30,0},{0,2},{2,4},{4,6},{6,8},{8,10},{10,12},{12,14},{14,16},{16,... | collective-permute-start | bytes 294920 | tf_op jit(solution)/shard_map/ppermute | solution.py:23
  8.1 12.3 %collective-permute-start.1 = (f32[48,512]{1,0:T(8,128)}, f32[48,512]{1,0:T(8,128)S(1)}, u32[]{:S(2)}, u32[]{:S(2)}) collective-permute-start(f32[48,512]{1,0:T(8,128)} %get-tuple-element.56), channel_id=1, source_target_pairs={{2,0},{4,2},{6,4},{8,6},{10,8},{12,10},{14,12},{16,14},{18,16},{20... | collective-permute-start | bytes 294920 | tf_op jit(solution)/shard_map/ppermute | solution.py:23
  13.2 7.3 %collective-permute-start.2 = (f32[48,512]{1,0:T(8,128)}, f32[48,512]{1,0:T(8,128)S(1)}, u32[]{:S(2)}, u32[]{:S(2)}) collective-permute-start(f32[48,512]{1,0:T(8,128)} %get-tuple-element.57), channel_id=1, source_target_pairs={{1,0},{0,1},{3,2},{2,3},{5,4},{4,5},{7,6},{6,7},{9,8},{8,9},{11,10... | collective-permute-start | bytes 294920 | tf_op jit(solution)/shard_map/ppermute | solution.py:23
  15.1 5.4 %collective-permute-start.3 = (f32[48,512]{1,0:T(8,128)}, f32[48,512]{1,0:T(8,128)S(1)}, u32[]{:S(2)}, u32[]{:S(2)}) collective-permute-start(f32[48,512]{1,0:T(8,128)} %get-tuple-element.58), channel_id=1, source_target_pairs={{1,0},{0,1},{3,2},{2,3},{5,4},{4,5},{7,6},{6,7},{9,8},{8,9},{11,10... | collective-permute-start | bytes 294920 | tf_op jit(solution)/shard_map/ppermute | solution.py:23
  15.2 1.2 %copy-start.10 = (f32[2008,128]{1,0:T(8,128)S(1)}, f32[2008,128]{1,0:T(8,128)}, u32[]{:S(2)}) copy-start(f32[2008,128]{1,0:T(8,128)} %get-tuple-element.52.refs_0_) | copy-start | bytes 3084292
  26.3 12.6 %collective-permute-start.4 = (f32[56,512]{1,0:T(8,128)S(1)}, f32[56,512]{1,0:T(8,128)S(1)}, u32[]{:S(2)}, u32[]{:S(2)}) collective-permute-start(f32[56,512]{1,0:T(8,128)S(1)} %get-tuple-element.77), channel_id=1, source_target_pairs={{30,0},{0,2},{2,4},{4,6},{6,8},{8,10},{10,12},{12,14},{14,16},{16,... | collective-permute-start | bytes 344072 | tf_op jit(solution)/shard_map/ppermute | solution.py:23
  26.6 12.4 %collective-permute-start.5 = (f32[56,512]{1,0:T(8,128)S(1)}, f32[56,512]{1,0:T(8,128)S(1)}, u32[]{:S(2)}, u32[]{:S(2)}) collective-permute-start(f32[56,512]{1,0:T(8,128)S(1)} %get-tuple-element.78), channel_id=1, source_target_pairs={{2,0},{4,2},{6,4},{8,6},{10,8},{12,10},{14,12},{16,14},{18,16},{20... | collective-permute-start | bytes 344072 | tf_op jit(solution)/shard_map/ppermute | solution.py:23
  31.0 7.9 %collective-permute-start.6 = (f32[56,512]{1,0:T(8,128)S(1)}, f32[56,512]{1,0:T(8,128)S(1)}, u32[]{:S(2)}, u32[]{:S(2)}) collective-permute-start(f32[56,512]{1,0:T(8,128)S(1)} %get-tuple-element.79), channel_id=1, source_target_pairs={{1,0},{0,1},{3,2},{2,3},{5,4},{4,5},{7,6},{6,7},{9,8},{8,9},{11,10... | collective-permute-start | bytes 344072 | tf_op jit(solution)/shard_map/ppermute | solution.py:23
  32.9 6.1 %collective-permute-start.7 = (f32[56,512]{1,0:T(8,128)S(1)}, f32[56,512]{1,0:T(8,128)S(1)}, u32[]{:S(2)}, u32[]{:S(2)}) collective-permute-start(f32[56,512]{1,0:T(8,128)S(1)} %get-tuple-element.80), channel_id=1, source_target_pairs={{1,0},{0,1},{3,2},{2,3},{5,4},{4,5},{7,6},{6,7},{9,8},{8,9},{11,10... | collective-permute-start | bytes 344072 | tf_op jit(solution)/shard_map/ppermute | solution.py:23
  33.0 2.4 %copy-start.3 = (f32[6,128,128]{2,1,0:T(8,128)S(1)}, f32[6,128,128]{2,1,0:T(8,128)}, u32[]{:S(2)}) copy-start(f32[6,128,128]{2,1,0:T(8,128)} %node_one.1) | copy-start | bytes 1179652
  33.0 2.4 %copy-start.4 = (f32[5,128,128]{2,1,0:T(8,128)S(1)}, f32[5,128,128]{2,1,0:T(8,128)}, u32[]{:S(2)}) copy-start(f32[5,128,128]{2,1,0:T(8,128)} %node_two.1) | copy-start | bytes 983044
  33.1 2.4 %copy-start.5 = (f32[2,64,64]{2,1,0:T(8,128)S(1)}, f32[2,64,64]{2,1,0:T(8,128)}, u32[]{:S(2)}) copy-start(f32[2,64,64]{2,1,0:T(8,128)} %radial_mid.1) | copy-start | bytes 98308
  33.1 2.4 %copy-start.6 = (f32[256,64]{0,1:T(8,128)S(1)}, f32[256,64]{0,1:T(8,128)}, u32[]{:S(2)}) copy-start(f32[256,64]{0,1:T(8,128)} %param.41) | copy-start | bytes 196612
  33.1 2.4 %copy-start.7 = (f32[8,128]{1,0:T(8,128)S(1)}, f32[8,128]{1,0:T(8,128)}, u32[]{:S(2)}) copy-start(f32[8,128]{1,0:T(8,128)} %embedding.1) | copy-start | bytes 12292
  33.1 2.4 %copy-start.8 = (f32[64,8]{0,1:T(8,128)S(1)}, f32[64,8]{0,1:T(8,128)}, u32[]{:S(2)}) copy-start(f32[64,8]{0,1:T(8,128)} %param.39) | copy-start | bytes 6148
  33.1 2.4 %copy-start.9 = (f32[128]{0:T(128)S(1)}, f32[128]{0:T(128)}, u32[]{:S(2)}) copy-start(f32[128]{0:T(128)} %param.47) | copy-start | bytes 1540
  33.1 2.4 %copy-start.11 = (s32[20,128]{1,0:T(8,128)S(1)}, s32[20,128]{1,0:T(8,128)}, u32[]{:S(2)}) copy-start(s32[20,128]{1,0:T(8,128)} %get-tuple-element.82.kinds) | copy-start | bytes 30724
  33.1 5.9 %copy-start = (f32[5,128,128]{2,1,0:T(8,128)S(1)}, f32[5,128,128]{2,1,0:T(8,128)}, u32[]{:S(2)}) copy-start(f32[5,128,128]{2,1,0:T(8,128)} %get-tuple-element.70.refs_2_) | copy-start | bytes 983044
  39.0 15.5 %copy-start.1 = (f32[3,3]{1,0:T(4,128)S(1)}, f32[3,3]{1,0:T(4,128)}, u32[]{:S(2)}) copy-start(f32[3,3]{1,0:T(4,128)} %refs_3_.1) | copy-start | bytes 112
  39.0 15.5 %copy-start.2 = (f32[3,3]{1,0:T(4,128)S(1)}, f32[3,3]{1,0:T(4,128)}, u32[]{:S(2)}) copy-start(f32[3,3]{1,0:T(4,128)} %refs_4_.1) | copy-start | bytes 112

commit v2 on v1

--- a/solution.py
+++ b/solution.py
@@ -127,11 +127,11 @@
 
 def hidden_values(value, inner, mid_a, mid_b):
     x = dot(inner, value_stack_small(value))
-    h = x * sigmoid(x)
-    x = dot(mid_a, value_stack(h))
-    h = x * sigmoid(x)
-    x = dot(mid_b, value_stack(h))
-    return x * sigmoid(x)
+    for mid in (mid_a, mid_b, None):
+        h = x * sigmoid(x)
+        if mid is not None:
+            x = dot(mid, value_stack(h))
+    return h
 
 
 def hidden_pairs(value, slope, inner, mid_a, mid_b):
@@ -192,7 +192,10 @@
         send_slab, send_sub, velocities, positions, migrants, masses, shifts,
         hidden_head, linear_head, out_head, next_in, next_mid, next_out, node_two,
     ) = buffers
-    kinds, far_sums, far_packed, to_minus, to_plus, to_prev, to_next, geo, waves, packed, sums = refs[count : -count - 2]
+    (
+        kinds, far_sums, far_packed, to_minus, to_plus, to_prev, to_next,
+        geo, waves, packed, sums,
+    ) = refs[count : -count - 2]
     for copy in copies[:2]:
         copy.wait()
     slots, atoms = mask.shape
@@ -240,30 +243,6 @@
     mid_a, mid_b = weight_stack(radial_mid[0]), weight_stack(radial_mid[1])
     outer = weight_stack_t(radial_out[...])
     lifted = species_matrix(node_one[0], embedding[...])
-    sums[...] = jnp.zeros_like(sums)
-
-    def group(step, carry):
-        first = step * GROUP
-        value = basis_group(waves, first, 0, basis_count)
-        h = hidden_values(value, inner, mid_a, mid_b)
-        weights = dot(outer, value_stack(h))
-        picked = picked_group(lifted, geo, kinds, first, species_count)
-        totals = [0.0] * 4
-        for j in range(GROUP):
-            at = slice(j * atoms, (j + 1) * atoms)
-            p = picked[:, at]
-            totals[0] = totals[0] + weights[:width, at] * p
-            q = weights[width:, at] * p
-            for a in range(3):
-                totals[a + 1] = totals[a + 1] + q * geo[a, pl.ds(first + j, 1), :]
-        for a in range(4):
-            sums[a] += totals[a]
-        return carry
-
-    over_groups(slots // GROUP, group, 0)
-
-    early_sums = pltpu.make_async_copy(sums.at[:4], far_sums.at[:4], gone.at[2])
-    early_sums.start()
     for copy in copies[10:]:
         copy.wait()
     mass = shift = jnp.zeros((1, atoms), f32)
@@ -305,9 +284,32 @@
     start += count + 8
     for i in range(waves.shape[0]):
         packed[start + i * step : start + i * step + slots] = waves[i]
+    sums[...] = jnp.zeros_like(sums)
+
+    def group(step, carry):
+        first = step * GROUP
+        value = basis_group(waves, first, 0, basis_count)
+        h = hidden_values(value, inner, mid_a, mid_b)
+        weights = dot(outer, value_stack(h))
+        picked = picked_group(lifted, geo, kinds, first, species_count)
+        totals = [0.0] * 4
+        for j in range(GROUP):
+            at = slice(j * atoms, (j + 1) * atoms)
+            p = picked[:, at]
+            totals[0] = totals[0] + weights[:width, at] * p
+            q = weights[width:, at] * p
+            for a in range(3):
+                totals[a + 1] = totals[a + 1] + q * geo[a, pl.ds(first + j, 1), :]
+        for a in range(4):
+            sums[a] += totals[a]
+        return carry
+
+    over_groups(slots // GROUP, group, 0)
+
+    early_sums = pltpu.make_async_copy(sums.at[:4], far_sums.at[:4], gone.at[2])
+    early_sums.start()
     early = pltpu.make_async_copy(packed.at[base:], far_packed.at[base:], gone.at[0])
     early.start()
-
     own_onehot = (iota((species_count, atoms), 0) == species[...]).astype(f32)
     own = exact(embedding[...], own_onehot, ((0,), (0,)))
     scalar_sum = sums[0]
@@ -347,7 +349,7 @@
 
 def radial_kernel(
     packed,
-    weights_all, slopes, onehot, outer, forward_high, forward_low, backward_high, backward_low,
+    weights_all, slopes, onehot, outer, fold_high, fold_low, back_high, back_low,
     geo, table, scalars, extras, facts, heads, waves, *, slab_rows, sub_rows, moves, basis_count,
 ):
     slots, atoms = geo.shape[1:]
@@ -387,10 +389,9 @@
         start += length
     rows = onehot.shape[0] // 2
     outer[...] = weight_stack_t(radial_out)
-    mixing = jnp.concatenate(mixings, axis=1)
-    forward_high[...], forward_low[...] = parts(mixing)
-    turned = jnp.concatenate([jnp.transpose(m) for m in mixings], axis=0)
-    backward_high[...], backward_low[...] = parts(turned)
+    folded = product(parts(heads[: heads.shape[0] - 8]), jnp.concatenate(mixings, axis=1))
+    fold_high[...], fold_low[...] = parts(folded)
+    back_high[...], back_low[...] = parts(jnp.transpose(folded))
     inner = weight_stack_t(radial_in)
     mid_a, mid_b = weight_stack(radial_mid[0]), weight_stack(radial_mid[1])
 
@@ -417,7 +418,7 @@
 
 def second_kernel(
     geo, own_table, from_minus, from_plus, from_prev, from_next, scalars, extras,
-    weights_all, onehot, forward_high, forward_low, backward_high, backward_low, heads,
+    weights_all, onehot, fold_high, fold_low, back_high, back_low, heads,
     energy, scalar_pull, picked_all, sums, own_pull, back_minus, back_plus, back_prev, back_next,
     table, pulled,
 ):
@@ -461,19 +462,17 @@
     vectors = [sums[1], sums[2], sums[3]]
     squares = vectors[0] * vectors[0] + vectors[1] * vectors[1] + vectors[2] * vectors[2]
     mixed = jnp.concatenate([scalar_sum, scalar_sum * scalar_sum, squares], axis=0)
-    second = scalars[...] + product((forward_high[...], forward_low[...]), mixed)
     units_out = heads.shape[0] - 8
     readout_hidden = heads[:units_out]
     readout_linear, readout_out = heads[units_out : units_out + 1], heads[units_out + 1 : units_out + 2, :units_out]
-    hidden_in = product(parts(readout_hidden), second)
+    hidden_in = product(parts(readout_hidden), scalars[...]) + product((fold_high[...], fold_low[...]), mixed)
     hidden_gate = sigmoid(hidden_in)
     hidden = hidden_in * hidden_gate
     shift = heads[units_out + 2 : units_out + 3]
     energy[...] = shift + exact(readout_linear, scalars[...]) + exact(readout_out, hidden)
     hidden_pull = column(readout_out) * (hidden_gate + hidden * (1.0 - hidden_gate))
-    second_pull = exact(readout_hidden, hidden_pull, ((0,), (0,)))
-    scalar_pull[...] = second_pull
-    spread = product((backward_high[...], backward_low[...]), second_pull)
+    scalar_pull[...] = exact(readout_hidden, hidden_pull, ((0,), (0,)))
+    spread = product((back_high[...], back_low[...]), hidden_pull)
     double = 2.0 * spread[2 * width :]
     sums[0] = spread[:width] + 2.0 * scalar_sum * spread[width : 2 * width]
     for a in range(3):
@@ -511,13 +510,38 @@
         start += count
 
 
-def edge_kernel(geo, slopes, outer, picked_all, weights_all, sums, geo_pull):
-    slots, atoms = geo.shape[1], geo.shape[2]
-    width = sums.shape[1]
+def window_kernel(
+    slopes, outer_two, picked_all, weights_all, sums,
+    geo, waves, kinds, scalar_pull, embedding, radial_in, radial_mid, radial_out, node_one, node_two, readout_linear,
+    geo_pull, scalar_slope, vector_slope, vector_value, turned_high, turned_low, base,
+):
+    slots, atoms = kinds.shape
+    width = node_one.shape[1]
+    species_count, basis_count = embedding.shape[0], radial_in.shape[0]
+    inner = weight_stack_t(radial_in[...])
+    mid_a, mid_b = weight_stack(radial_mid[0]), weight_stack(radial_mid[1])
+    outer = weight_stack_t(radial_out[...])
+    lifted = species_matrix(node_one[0], embedding[...])
+    scalar_mixing = jnp.concatenate([jnp.transpose(node_one[i]) for i in (1, 2, 3)], axis=0)
+    base[...] = column(readout_linear[...]) + scalar_pull[...]
+    turned = [scalar_mixing] + [jnp.transpose(m) for m in (node_two[1], node_one[4], node_one[5], node_two[0])]
+    turned_high[...], turned_low[...] = parts(jnp.concatenate(turned, axis=0))
 
     def group(step, carry):
         first = step * GROUP
-        slope = dot(outer[...], slopes[:, span_of(step * GROUP * atoms, GROUP * atoms)])
+        at = span_of(step * GROUP * atoms, GROUP * atoms)
+        value, slope = (basis_group(waves, first, i * basis_count, basis_count) for i in range(2))
+        h, dh = hidden_pairs(value, slope, inner, mid_a, mid_b)
+        picked = picked_group(lifted, geo, kinds, first, species_count)
+        weights_slope = dot(outer, value_stack(dh))
+        scalar_slope[:, at] = weights_slope[:width] * picked
+        vector_slope[:, at] = weights_slope[width:] * picked
+        vector_value[:, at] = dot(outer[width:], value_stack(h)) * picked
+        return carry
+
+    def edge_group(step, carry):
+        first = step * GROUP
+        slope = dot(outer_two[...], slopes[:, span_of(step * GROUP * atoms, GROUP * atoms)])
         for j in range(GROUP):
             span = slice(j * atoms, (j + 1) * atoms)
             here = span_of((step * GROUP + j) * atoms, atoms)
@@ -538,48 +562,19 @@
                 geo_pull[a + 1, pl.ds(first + j, 1), :] = jnp.sum(turn, axis=0, keepdims=True)
         return carry
 
-    over_groups(slots // GROUP, group, 0)
-
-
-def slope_kernel(
-    geo, waves, kinds, after, embedding, radial_in, radial_mid, radial_out, node_one, node_two, readout_linear,
-    scalar_slope, vector_slope, vector_value, turned_high, turned_low, linear,
-):
-    slots, atoms = kinds.shape
-    width = node_one.shape[1]
-    species_count, basis_count = embedding.shape[0], radial_in.shape[0]
-    inner = weight_stack_t(radial_in[...])
-    mid_a, mid_b = weight_stack(radial_mid[0]), weight_stack(radial_mid[1])
-    outer = weight_stack_t(radial_out[...])
-    lifted = species_matrix(node_one[0], embedding[...])
-    linear[...] = jnp.broadcast_to(column(readout_linear[...]), linear.shape)
-    mixings = [node_one[i] for i in (1, 2, 3, 4, 5)] + [node_two[0], node_two[1]]
-    turned = jnp.concatenate([jnp.transpose(m) for m in mixings], axis=0)
-    turned_high[...], turned_low[...] = parts(turned)
-
-    def group(step, carry):
-        first = step * GROUP
-        at = span_of(step * GROUP * atoms, GROUP * atoms)
-        value, slope = (basis_group(waves, first, i * basis_count, basis_count) for i in range(2))
-        h, dh = hidden_pairs(value, slope, inner, mid_a, mid_b)
-        picked = picked_group(lifted, geo, kinds, first, species_count)
-        weights_slope = dot(outer, value_stack(dh))
-        scalar_slope[:, at] = weights_slope[:width] * picked
-        vector_slope[:, at] = weights_slope[width:] * picked
-        vector_value[:, at] = dot(outer[width:], value_stack(h)) * picked
-        return carry
-
-    over_groups(slots // GROUP, group, 0)
+    for step in range(slots // GROUP):
+        group(step, 0)
+        edge_group(step, 0)
 
 
 def third_kernel(
-    facts, geo, sums, geo_pull, scalar_pull, own_pull, ret_minus, ret_plus, ret_prev, ret_next,
-    onehot, scalar_slope, vector_slope, vector_value, turned_high, turned_low, linear,
+    facts, geo, sums, geo_pull, own_pull, ret_minus, ret_plus, ret_prev, ret_next,
+    onehot, scalar_slope, vector_slope, vector_value, turned_high, turned_low, base,
     everyone, came,
     pieces, pulls, flat, *, moves, slab_rows, sub_rows,
 ):
     slots, atoms = geo.shape[1], geo.shape[2]
-    width = scalar_pull.shape[0]
+    width = sums.shape[1]
     pick = send_onehot(facts, 0, slab_rows, sub_rows).astype(bf16)
     returned = jnp.concatenate(
         [ret_plus[:slab_rows], ret_minus[:slab_rows], ret_next[:sub_rows], ret_prev[:sub_rows]], axis=0
@@ -593,14 +588,14 @@
         at = slice(i * width, (i + count) * width)
         return turned_high[at, :], turned_low[at, :]
 
-    scalars = product(turned(5), x_pull) + linear[...] + scalar_pull[...]
-    moved = product(turned(6), y_pull)
+    moved = product(turned(3), y_pull)
     gv = [moved[:, a * atoms : (a + 1) * atoms] for a in range(3)]
     scalar_sum, gate = sums[0], sums[4]
     vectors = [sums[1], sums[2], sums[3]]
+    scalars = product(turned(6), x_pull) + base[...]
     spread = product(turned(0, 3), scalars)
-    mixed = product(turned(3), moved)
-    gated = product(turned(4), gv[0] * vectors[0] + gv[1] * vectors[1] + gv[2] * vectors[2])
+    mixed = product(turned(4), moved)
+    gated = product(turned(5), gv[0] * vectors[0] + gv[1] * vectors[1] + gv[2] * vectors[2])
     pulls[0] = spread[:width] + 2.0 * scalar_sum * spread[width : 2 * width] + gated
     double = 2.0 * spread[2 * width :]
     for a in range(3):
@@ -899,7 +894,7 @@
         )
 
     (
-        weights_all, slopes, onehot, outer, forward_high, forward_low, backward_high, backward_low,
+        weights_all, slopes, onehot, outer, fold_high, fold_low, back_high, back_low,
         geo, own_table, scalars, extras, facts, heads, waves,
     ) = call(
         radial,
@@ -908,10 +903,10 @@
             shape(3 * hidden, edges, dtype=bf16),
             shape(2 * extended, edges, dtype=bf16),
             shape(depth, 3 * hidden, dtype=bf16),
-            shape(width, 3 * width, dtype=bf16),
-            shape(width, 3 * width, dtype=bf16),
-            shape(3 * width, width, dtype=bf16),
-            shape(3 * width, width, dtype=bf16),
+            shape(readout_hidden.shape[0], 3 * width, dtype=bf16),
+            shape(readout_hidden.shape[0], 3 * width, dtype=bf16),
+            shape(3 * width, readout_hidden.shape[0], dtype=bf16),
+            shape(3 * width, readout_hidden.shape[0], dtype=bf16),
             shape(6, slots, atoms),
             shape(depth, 2 * atoms, dtype=bf16),
             shape(width, atoms),
@@ -946,19 +941,13 @@
         name="layer_two",
     )(
         geo, own_table, from_minus, from_plus, from_prev, from_next, scalars, extras,
-        weights_all, onehot, forward_high, forward_low, backward_high, backward_low, heads,
+        weights_all, onehot, fold_high, fold_low, back_high, back_low, heads,
     )
     ret_minus, ret_plus, ret_prev, ret_next = trade(back_minus, back_plus, back_prev, back_next)
-    (geo_pull,) = call(
-        edge_kernel,
-        (shape(4, slots, atoms),),
-        flops=edges * depth * 400,
-        vmem=16,
-        name="edge_two",
-    )(geo, slopes, outer, picked_all, weights_all, pulls)
-    scalar_slope, vector_slope, vector_value, turned_high, turned_low, linear = call(
-        slope_kernel,
+    geo_pull, scalar_slope, vector_slope, vector_value, turned_high, turned_low, base = call(
+        window_kernel,
         (
+            shape(4, slots, atoms),
             shape(width, edges),
             shape(width, edges),
             shape(width, edges),
@@ -966,13 +955,14 @@
             shape(7 * width, width, dtype=bf16),
             shape(width, atoms),
         ),
-        flops=12 * edges * 20000,
-        vmem=12,
+        flops=12 * edges * 12000,
+        vmem=20,
         name="radial_one",
     )(
-        geo, waves, kinds, scalar_pull, embedding, radial_one_in, radial_one_mid, radial_one_out, node_one, node_two, linear_row,
+        slopes, outer, picked_all, weights_all, pulls,
+        geo, waves, kinds, scalar_pull, embedding,
+        radial_one_in, radial_one_mid, radial_one_out, node_one, node_two, linear_row,
     )
-
 
     def back(*refs):
         third_kernel(*refs, moves=migrants.shape[1], slab_rows=ghost_slab, sub_rows=ghost_sub)
@@ -989,8 +979,8 @@
         vmem=12,
         name="layer_one_back",
     )(
-        facts, geo, sums, geo_pull, scalar_pull, own_pull, ret_minus, ret_plus, ret_prev, ret_next,
-        onehot, scalar_slope, vector_slope, vector_value, turned_high, turned_low, linear,
+        facts, geo, sums, geo_pull, own_pull, ret_minus, ret_plus, ret_prev, ret_next,
+        onehot, scalar_slope, vector_slope, vector_value, turned_high, turned_low, base,
     )
     everyone = lax.all_to_all(everyone, ("slab", "sub"), 0, 0, tiled=True)
 

time: 56.3 us -> 56.1 us (level)
    pallas_call x7 -> x6, Pallas kernels: 26.9 us -> 26.9 us  [run(): pl.pallas_call(kernel, out_shape=tuple(outs), in_specs=[HB if far_inputs...]
where the time goes in v2:
time: 56.1 us; the launch traced here: 55.9 us
  Pallas kernels  26.9 us (48%)
  starting transfers between devices  14.1 us (25%)
  blocking collectives  12.7 us (23%)
  local copies, waits for them, and re-layouts  1.28 us (2%)
  between operations  0.87 us (2%)
    pallas_call x6, Pallas kernels, run(): pl.pallas_call(kernel, out_shape=tuple(outs), in_specs=[HB if far_inputs...  26.9 us
    ppermute x8, starting transfers between devices, shifted(): lax.ppermute(block, axis, [((i - distance) % count, i) for i in range(cou...  14.1 us
    all_to_all x1, blocking collectives, body(): everyone = lax.all_to_all(everyone, ('slab', 'sub'), 0, 0, tiled=True)  12.7 us
    unnamed x24, local copies, waits for them, and re-layouts  1.28 us
  transfers between devices with their start and end apart: 8, of which 0 were waited for; matrix products, arithmetic and copies ran while one was open for 0% of the time, Pallas kernels for 17%

profile of v2, /device:TPU:0, one launch (start us, length us, event | category | flops | bytes accessed | tf_op | source)
XLA Modules:
  0.0 55.9 jit_solution(1497624635945793591)
XLA Ops:
  0.6 7.3 %layer_one.1 = (s32[20,128]{1,0:T(8,128)}, f32[5,128,128]{2,1,0:T(8,128)}, f32[2008,128]{1,0:T(8,128)}, f32[48,512]{1,0:T(8,128)}, f32[48,512]{1,0:T(8,128)}, /*index=5*/f32[48,512]{1,0:T(8,128)}, f32[48,512]{1,0:T(8,128)}) custom-call(f32[3,20,128]{2,1,0:T(8,128)} %refs_0_.1, s32[20,128]{1,0:T(8,128)} %refs_1_.1, s32[20,128]{1,0:T(8,128)} %refs_2_.1, ...), custom_call_target="tpu_custom_call" | custom-call | flops 399360000 | bytes 2815680 | tf_op jit(solution)/shard_map/layer_one/pallas_call | solution.py:813
  7.9 0.5 collective-permute-start
  8.4 5.1 %collective-permute-start.1 = (f32[48,512]{1,0:T(8,128)}, f32[48,512]{1,0:T(8,128)S(1)}, u32[]{:S(2)}, u32[]{:S(2)}) collective-permute-start(f32[48,512]{1,0:T(8,128)} %get-tuple-element.57), channel_id=1, source_target_pairs={{2,0},{4,2},{6,4},{8,6},{10,8},{12,10},{14,12},{16,14},{18,16},{20... | collective-permute-start | bytes 294920 | tf_op jit(solution)/shard_map/ppermute | solution.py:23
  13.5 1.9 %collective-permute-start.2 = (f32[48,512]{1,0:T(8,128)}, f32[48,512]{1,0:T(8,128)S(1)}, u32[]{:S(2)}, u32[]{:S(2)}) collective-permute-start(f32[48,512]{1,0:T(8,128)} %get-tuple-element.58), channel_id=1, source_target_pairs={{1,0},{0,1},{3,2},{2,3},{5,4},{4,5},{7,6},{6,7},{9,8},{8,9},{11,10... | collective-permute-start | bytes 294920 | tf_op jit(solution)/shard_map/ppermute | solution.py:23
  15.3 0.2 collective-permute-start.3
  15.5 1.2 %copy-done.11 = f32[2008,128]{1,0:T(8,128)S(1)} copy-done((f32[2008,128]{1,0:T(8,128)S(1)}, f32[2008,128]{1,0:T(8,128)}, u32[]{:S(2)}) %copy-start.11) | copy-done | bytes 1028120
  16.7 4.1 %radial_two.1 = (f32[512,2560]{1,0:T(8,128)S(1)}, bf16[192,2560]{1,0:T(8,128)(2,1)S(1)}, bf16[640,2560]{1,0:T(8,128)(2,1)S(1)}, bf16[512,192]{1,0:T(8,128)(2,1)S...) custom-call(f32[2008,128]{1,0:T(8,128)S(1)} %copy-done.11), custom_call_target="tpu_custom_call" | custom-call | flops 307200000 | bytes 11382784 | tf_op jit(solution)/shard_map/radial_two/pallas_call | solution.py:813
  20.8 0.0 copy-start
  20.8 0.0 copy-start.1
  20.8 0.0 copy-start.3
  20.9 0.0 copy-start.4
  20.9 0.0 copy-start.6
  20.9 0.0 copy-start.7
  20.9 0.0 copy-start.10
  20.9 5.7 %layer_two.1 = (f32[1,128]{1,0:T(1,128)}, f32[128,128]{1,0:T(8,128)S(1)}, f32[512,2560]{1,0:T(8,128)S(1)}, f32[4,128,128]{2,1,0:T(8,128)S(1)}, f32[128,512]{1,0:...) custom-call(f32[6,20,128]{2,1,0:T(8,128)S(1)} %get-tuple-element.54., ...), custom_call_target="tpu_custom_call" | custom-call | flops 3355443200 | bytes 15688192 | tf_op jit(solution)/shard_map/layer_two/pallas_call | solution.py:813
  26.6 0.1 collective-permute-start.4
  26.7 4.4 %collective-permute-start.5 = (f32[56,512]{1,0:T(8,128)S(1)}, f32[56,512]{1,0:T(8,128)S(1)}, u32[]{:S(2)}, u32[]{:S(2)}) collective-permute-start(f32[56,512]{1,0:T(8,128)S(1)} %get-tuple-element.82), channel_id=1, source_target_pairs={{2,0},{4,2},{6,4},{8,6},{10,8},{12,10},{14,12},{16,14},{18,16},{20... | collective-permute-start | bytes 344072 | tf_op jit(solution)/shard_map/ppermute | solution.py:23
  31.1 1.9 %collective-permute-start.6 = (f32[56,512]{1,0:T(8,128)S(1)}, f32[56,512]{1,0:T(8,128)S(1)}, u32[]{:S(2)}, u32[]{:S(2)}) collective-permute-start(f32[56,512]{1,0:T(8,128)S(1)} %get-tuple-element.83), channel_id=1, source_target_pairs={{1,0},{0,1},{3,2},{2,3},{5,4},{4,5},{7,6},{6,7},{9,8},{8,9},{11,10... | collective-permute-start | bytes 344072 | tf_op jit(solution)/shard_map/ppermute | solution.py:23
  33.0 0.2 collective-permute-start.7
  33.2 5.5 %radial_one.1 = (f32[4,20,128]{2,1,0:T(8,128)S(1)}, f32[128,2560]{1,0:T(8,128)S(1)}, f32[128,2560]{1,0:T(8,128)S(1)}, f32[128,2560]{1,0:T(8,128)S(1)}, bf16[896,...) custom-call(bf16[192,2560]{1,0:T(8,128)(2,1)S(1)} %get-tuple-element.72.slopes, ...), custom_call_target="tpu_custom_call" | custom-call | flops 368640000 | bytes 17551872 | tf_op jit(solution)/shard_map/radial_one/pallas_call | solution.py:813
  38.8 0.0 copy-start.8
  38.8 2.8 %layer_one_back.1 = (f32[32,16,128]{2,1,0:T(8,128)S(1)}, f32[8,128]{1,0:T(8,128)S(1)}) custom-call(f32[16,128]{1,0:T(8,128)S(1)} %get-tuple-element.70.refs_0_.refs_1_, f32[6,20,128]{2,1,0:T(8,128)S(1)} %get-tuple-element.54.geo.refs_1_, f32[5,128,128]{2,1,0:T(8,128)S(1)} %copy-done.2, f32[4,20,128]{2,1,0:T(8,128)S(1)} %get-tuple-element.79.refs_3_, ...), custom_call_target="tpu_custom_call" | custom-call | flops 15360000 | bytes 9158656 | tf_op jit(solution)/shard_map/layer_one_back/pallas_call | solution.py:813
  41.5 12.7 %all_to_all.5.refs_0_ = f32[32,16,128]{2,1,0:T(8,128)S(1)} all-to-all(f32[32,16,128]{2,1,0:T(8,128)S(1)} %get-tuple-element.91), channel_id=1, replica_groups=mesh['slab'=16,'sub'=2] {'slab','sub'}, dimensions={0} | all-to-all | bytes 524288 | tf_op jit(solution)/shard_map/all_to_all | solution.py:985
  54.3 1.6 %box.1 = (f32[3,128]{1,0:T(4,128)}, f32[3,128]{1,0:T(4,128)}, f32[3,128]{1,0:T(4,128)}, f32[6,16]{1,0:T(8,128)}, f32[3,3]{1,0:T(4,128)}, /*index=5*/f32[3,3]{1,0:T(4,128)}) custom-call(f32[32,16,128]{2,1,0:T(8,128)S(1)} %all_to_all.5.refs_0_, f32[16,128]{1,0:T(8,128)S(1)} %get-tuple-element.70.refs_0_.refs_1_, f32[8,128]{1,0:T(8,128)S(1)} %get-tuple-element.92.refs_2_, ...), custom_call_target="tpu_custom_call" | custom-call | flops 1000000 | bytes 279568 | tf_op jit(solution)/shard_map/box/pallas_call | solution.py:813
  (23 shorter events, 0.1 us)
Async XLA Ops:
  7.9 12.9 %collective-permute-start = (f32[48,512]{1,0:T(8,128)}, f32[48,512]{1,0:T(8,128)S(1)}, u32[]{:S(2)}, u32[]{:S(2)}) collective-permute-start(f32[48,512]{1,0:T(8,128)} %get-tuple-element.56), channel_id=1, source_target_pairs={{30,0},{0,2},{2,4},{4,6},{6,8},{8,10},{10,12},{12,14},{14,16},{16,... | collective-permute-start | bytes 294920 | tf_op jit(solution)/shard_map/ppermute | solution.py:23
  8.4 12.4 %collective-permute-start.1 = (f32[48,512]{1,0:T(8,128)}, f32[48,512]{1,0:T(8,128)S(1)}, u32[]{:S(2)}, u32[]{:S(2)}) collective-permute-start(f32[48,512]{1,0:T(8,128)} %get-tuple-element.57), channel_id=1, source_target_pairs={{2,0},{4,2},{6,4},{8,6},{10,8},{12,10},{14,12},{16,14},{18,16},{20... | collective-permute-start | bytes 294920 | tf_op jit(solution)/shard_map/ppermute | solution.py:23
  13.5 7.3 %collective-permute-start.2 = (f32[48,512]{1,0:T(8,128)}, f32[48,512]{1,0:T(8,128)S(1)}, u32[]{:S(2)}, u32[]{:S(2)}) collective-permute-start(f32[48,512]{1,0:T(8,128)} %get-tuple-element.58), channel_id=1, source_target_pairs={{1,0},{0,1},{3,2},{2,3},{5,4},{4,5},{7,6},{6,7},{9,8},{8,9},{11,10... | collective-permute-start | bytes 294920 | tf_op jit(solution)/shard_map/ppermute | solution.py:23
  15.3 5.5 %collective-permute-start.3 = (f32[48,512]{1,0:T(8,128)}, f32[48,512]{1,0:T(8,128)S(1)}, u32[]{:S(2)}, u32[]{:S(2)}) collective-permute-start(f32[48,512]{1,0:T(8,128)} %get-tuple-element.59), channel_id=1, source_target_pairs={{1,0},{0,1},{3,2},{2,3},{5,4},{4,5},{7,6},{6,7},{9,8},{8,9},{11,10... | collective-permute-start | bytes 294920 | tf_op jit(solution)/shard_map/ppermute | solution.py:23
  15.5 1.2 %copy-start.11 = (f32[2008,128]{1,0:T(8,128)S(1)}, f32[2008,128]{1,0:T(8,128)}, u32[]{:S(2)}) copy-start(f32[2008,128]{1,0:T(8,128)} %get-tuple-element.53.refs_0_) | copy-start | bytes 3084292
  20.8 12.3 %copy-start = (f32[6,128,128]{2,1,0:T(8,128)S(1)}, f32[6,128,128]{2,1,0:T(8,128)}, u32[]{:S(2)}) copy-start(f32[6,128,128]{2,1,0:T(8,128)} %node_one.1) | copy-start | bytes 1179652
  20.8 12.3 %copy-start.1 = (f32[5,128,128]{2,1,0:T(8,128)S(1)}, f32[5,128,128]{2,1,0:T(8,128)}, u32[]{:S(2)}) copy-start(f32[5,128,128]{2,1,0:T(8,128)} %node_two.1) | copy-start | bytes 983044
  20.8 12.3 %copy-start.3 = (f32[2,64,64]{2,1,0:T(8,128)S(1)}, f32[2,64,64]{2,1,0:T(8,128)}, u32[]{:S(2)}) copy-start(f32[2,64,64]{2,1,0:T(8,128)} %radial_mid.1) | copy-start | bytes 98308
  20.9 12.3 %copy-start.4 = (f32[256,64]{0,1:T(8,128)S(1)}, f32[256,64]{0,1:T(8,128)}, u32[]{:S(2)}) copy-start(f32[256,64]{0,1:T(8,128)} %param.41) | copy-start | bytes 196612
  20.9 12.3 %copy-start.5 = (s32[20,128]{1,0:T(8,128)S(1)}, s32[20,128]{1,0:T(8,128)}, u32[]{:S(2)}) copy-start(s32[20,128]{1,0:T(8,128)} %get-tuple-element.77.kinds) | copy-start | bytes 30724
  20.9 12.3 %copy-start.6 = (f32[8,128]{1,0:T(8,128)S(1)}, f32[8,128]{1,0:T(8,128)}, u32[]{:S(2)}) copy-start(f32[8,128]{1,0:T(8,128)} %embedding.1) | copy-start | bytes 12292
  20.9 12.3 %copy-start.7 = (f32[64,8]{0,1:T(8,128)S(1)}, f32[64,8]{0,1:T(8,128)}, u32[]{:S(2)}) copy-start(f32[64,8]{0,1:T(8,128)} %param.39) | copy-start | bytes 6148
  20.9 12.3 %copy-start.10 = (f32[128]{0:T(128)S(1)}, f32[128]{0:T(128)}, u32[]{:S(2)}) copy-start(f32[128]{0:T(128)} %param.47) | copy-start | bytes 1540
  26.6 12.1 %collective-permute-start.4 = (f32[56,512]{1,0:T(8,128)S(1)}, f32[56,512]{1,0:T(8,128)S(1)}, u32[]{:S(2)}, u32[]{:S(2)}) collective-permute-start(f32[56,512]{1,0:T(8,128)S(1)} %get-tuple-element.81), channel_id=1, source_target_pairs={{30,0},{0,2},{2,4},{4,6},{6,8},{8,10},{10,12},{12,14},{14,16},{16,... | collective-permute-start | bytes 344072 | tf_op jit(solution)/shard_map/ppermute | solution.py:23
  26.7 12.0 %collective-permute-start.5 = (f32[56,512]{1,0:T(8,128)S(1)}, f32[56,512]{1,0:T(8,128)S(1)}, u32[]{:S(2)}, u32[]{:S(2)}) collective-permute-start(f32[56,512]{1,0:T(8,128)S(1)} %get-tuple-element.82), channel_id=1, source_target_pairs={{2,0},{4,2},{6,4},{8,6},{10,8},{12,10},{14,12},{16,14},{18,16},{20... | collective-permute-start | bytes 344072 | tf_op jit(solution)/shard_map/ppermute | solution.py:23
  31.1 7.6 %collective-permute-start.6 = (f32[56,512]{1,0:T(8,128)S(1)}, f32[56,512]{1,0:T(8,128)S(1)}, u32[]{:S(2)}, u32[]{:S(2)}) collective-permute-start(f32[56,512]{1,0:T(8,128)S(1)} %get-tuple-element.83), channel_id=1, source_target_pairs={{1,0},{0,1},{3,2},{2,3},{5,4},{4,5},{7,6},{6,7},{9,8},{8,9},{11,10... | collective-permute-start | bytes 344072 | tf_op jit(solution)/shard_map/ppermute | solution.py:23
  33.0 5.8 %collective-permute-start.7 = (f32[56,512]{1,0:T(8,128)S(1)}, f32[56,512]{1,0:T(8,128)S(1)}, u32[]{:S(2)}, u32[]{:S(2)}) collective-permute-start(f32[56,512]{1,0:T(8,128)S(1)} %get-tuple-element.84), channel_id=1, source_target_pairs={{1,0},{0,1},{3,2},{2,3},{5,4},{4,5},{7,6},{6,7},{9,8},{8,9},{11,10... | collective-permute-start | bytes 344072 | tf_op jit(solution)/shard_map/ppermute | solution.py:23
  33.2 5.6 %copy-start.2 = (f32[5,128,128]{2,1,0:T(8,128)S(1)}, f32[5,128,128]{2,1,0:T(8,128)}, u32[]{:S(2)}) copy-start(f32[5,128,128]{2,1,0:T(8,128)} %get-tuple-element.71.refs_2_) | copy-start | bytes 983044
  38.8 15.5 %copy-start.8 = (f32[3,3]{1,0:T(4,128)S(1)}, f32[3,3]{1,0:T(4,128)}, u32[]{:S(2)}) copy-start(f32[3,3]{1,0:T(4,128)} %refs_3_.1) | copy-start | bytes 112
  38.8 15.5 %copy-start.9 = (f32[3,3]{1,0:T(4,128)S(1)}, f32[3,3]{1,0:T(4,128)}, u32[]{:S(2)}) copy-start(f32[3,3]{1,0:T(4,128)} %refs_4_.1) | copy-start | bytes 112

commit v3 on v2

--- a/solution.py
+++ b/solution.py
@@ -23,9 +23,13 @@
     return lax.ppermute(block, axis, [((i - distance) % count, i) for i in range(count)])
 
 
-def trade(to_minus, to_plus, to_prev, to_next):
+def trade(to_minus, to_plus, to_sub, first):
     from_minus, from_plus = shifted(to_plus, "slab", 1), shifted(to_minus, "slab", -1)
-    return from_minus, from_plus, shifted(to_next, "sub", 1), shifted(to_prev, "sub", -1)
+    if lax.axis_size("sub") == 2:
+        return from_minus, from_plus, shifted(to_sub, "sub", 1)
+    one, two = jnp.split(to_sub, 2, axis=0)
+    from_sub = jnp.concatenate([shifted(one, "sub", first), shifted(two, "sub", -first)], axis=0)
+    return from_minus, from_plus, from_sub
 
 
 def parts(x):
@@ -193,7 +197,7 @@
         hidden_head, linear_head, out_head, next_in, next_mid, next_out, node_two,
     ) = buffers
     (
-        kinds, far_sums, far_packed, to_minus, to_plus, to_prev, to_next,
+        kinds, far_sums, far_packed, to_minus, to_plus, to_sub,
         geo, waves, packed, sums,
     ) = refs[count : -count - 2]
     for copy in copies[:2]:
@@ -243,6 +247,30 @@
     mid_a, mid_b = weight_stack(radial_mid[0]), weight_stack(radial_mid[1])
     outer = weight_stack_t(radial_out[...])
     lifted = species_matrix(node_one[0], embedding[...])
+    sums[...] = jnp.zeros_like(sums)
+
+    def group(step, carry):
+        first = step * GROUP
+        value = basis_group(waves, first, 0, basis_count)
+        h = hidden_values(value, inner, mid_a, mid_b)
+        weights = dot(outer, value_stack(h))
+        picked = picked_group(lifted, geo, kinds, first, species_count)
+        totals = [0.0] * 4
+        for j in range(GROUP):
+            at = slice(j * atoms, (j + 1) * atoms)
+            p = picked[:, at]
+            totals[0] = totals[0] + weights[:width, at] * p
+            q = weights[width:, at] * p
+            for a in range(3):
+                totals[a + 1] = totals[a + 1] + q * geo[a, pl.ds(first + j, 1), :]
+        for a in range(4):
+            sums[a] += totals[a]
+        return carry
+
+    over_groups(slots // GROUP, group, 0)
+
+    early_sums = pltpu.make_async_copy(sums.at[:4], far_sums.at[:4], gone.at[2])
+    early_sums.start()
     for copy in copies[10:]:
         copy.wait()
     mass = shift = jnp.zeros((1, atoms), f32)
@@ -284,30 +312,6 @@
     start += count + 8
     for i in range(waves.shape[0]):
         packed[start + i * step : start + i * step + slots] = waves[i]
-    sums[...] = jnp.zeros_like(sums)
-
-    def group(step, carry):
-        first = step * GROUP
-        value = basis_group(waves, first, 0, basis_count)
-        h = hidden_values(value, inner, mid_a, mid_b)
-        weights = dot(outer, value_stack(h))
-        picked = picked_group(lifted, geo, kinds, first, species_count)
-        totals = [0.0] * 4
-        for j in range(GROUP):
-            at = slice(j * atoms, (j + 1) * atoms)
-            p = picked[:, at]
-            totals[0] = totals[0] + weights[:width, at] * p
-            q = weights[width:, at] * p
-            for a in range(3):
-                totals[a + 1] = totals[a + 1] + q * geo[a, pl.ds(first + j, 1), :]
-        for a in range(4):
-            sums[a] += totals[a]
-        return carry
-
-    over_groups(slots // GROUP, group, 0)
-
-    early_sums = pltpu.make_async_copy(sums.at[:4], far_sums.at[:4], gone.at[2])
-    early_sums.start()
     early = pltpu.make_async_copy(packed.at[base:], far_packed.at[base:], gone.at[0])
     early.start()
     own_onehot = (iota((species_count, atoms), 0) == species[...]).astype(f32)
@@ -340,9 +344,7 @@
     slab_rows = send_slab.shape[1]
     to_plus[...] = sent[:slab_rows]
     to_minus[...] = sent[slab_rows : 2 * slab_rows]
-    sub_rows = send_sub.shape[1]
-    to_next[...] = sent[2 * slab_rows : 2 * slab_rows + sub_rows]
-    to_prev[...] = sent[2 * slab_rows + sub_rows :]
+    to_sub[...] = sent[2 * slab_rows :]
     for copy in (early, late, early_sums, late_sums):
         copy.wait()
 
@@ -417,15 +419,15 @@
 
 
 def second_kernel(
-    geo, own_table, from_minus, from_plus, from_prev, from_next, scalars, extras,
+    geo, own_table, from_minus, from_plus, from_sub, scalars, extras,
     weights_all, onehot, fold_high, fold_low, back_high, back_low, heads,
-    energy, scalar_pull, picked_all, sums, own_pull, back_minus, back_plus, back_prev, back_next,
+    energy, scalar_pull, picked_all, sums, own_pull, back_minus, back_plus, back_sub,
     table, pulled,
 ):
     slots, atoms = geo.shape[1], geo.shape[2]
     width = scalars.shape[0]
     depth = 4 * width
-    ghosts = jnp.concatenate([from_minus[...], from_plus[...], from_prev[...], from_next[...]], axis=0)
+    ghosts = jnp.concatenate([from_minus[...], from_plus[...], from_sub[...]], axis=0)
     high = ghosts.astype(bf16).astype(f32)
     table[:, : 2 * atoms] = own_table[...]
     table[:, 2 * atoms :] = jnp.transpose(jnp.concatenate([high, ghosts - high], axis=0)).astype(bf16)
@@ -503,10 +505,16 @@
     own_pull[...] = pulled[:atoms]
     start = atoms
     fill = jnp.zeros((8, depth - extras.shape[2]), f32)
-    for out, which in ((back_minus, 1), (back_plus, 0), (back_prev, 3), (back_next, 2)):
-        count = out.shape[0] - 8
-        out[:count] = pulled[start : start + count]
-        out[count:] = jnp.concatenate([extras[which], fill], axis=1)
+    half = back_sub.shape[0] // 2
+    for out, offset, size, which in (
+        (back_minus, 0, back_minus.shape[0], 1),
+        (back_plus, 0, back_plus.shape[0], 0),
+        (back_sub, 0, half, 3),
+        (back_sub, half, half, 2),
+    ):
+        count = size - 8
+        out[offset : offset + count] = pulled[start : start + count]
+        out[offset + count : offset + size] = jnp.concatenate([extras[which], fill], axis=1)
         start += count
 
 
@@ -568,13 +576,15 @@
 
 
 def third_kernel(
-    facts, geo, sums, geo_pull, own_pull, ret_minus, ret_plus, ret_prev, ret_next,
+    facts, geo, sums, geo_pull, own_pull, ret_minus, ret_plus, ret_sub,
     onehot, scalar_slope, vector_slope, vector_value, turned_high, turned_low, base,
     everyone, came,
     pieces, pulls, flat, *, moves, slab_rows, sub_rows,
 ):
     slots, atoms = geo.shape[1], geo.shape[2]
     width = sums.shape[1]
+    half = sub_rows + 8
+    ret_next, ret_prev = ret_sub.at[:half], ret_sub.at[half:]
     pick = send_onehot(facts, 0, slab_rows, sub_rows).astype(bf16)
     returned = jnp.concatenate(
         [ret_plus[:slab_rows], ret_minus[:slab_rows], ret_next[:sub_rows], ret_prev[:sub_rows]], axis=0
@@ -855,7 +865,7 @@
         8 * width + 6 * packed_step(slots) + FACTS + 6 * hidden + radial_two_in.shape[0] + packed_step(slots)
         + readout_hidden.shape[0] + 8 + 2 * radial_one_in.shape[0] * packed_step(slots)
     )
-    kinds, sums, packed, to_minus, to_plus, to_prev, to_next = call(
+    kinds, sums, packed, to_minus, to_plus, to_sub = call(
         first_kernel,
         (
             shape(slots, atoms, dtype=jnp.int32),
@@ -863,8 +873,7 @@
             shape(packed_rows, atoms),
             shape(ghost_slab, depth),
             shape(ghost_slab, depth),
-            shape(ghost_sub, depth),
-            shape(ghost_sub, depth),
+            shape(2 * ghost_sub, depth),
         ),
         far_inputs=True,
         far_outputs=(1, 2),
@@ -882,7 +891,7 @@
     )(
         *first_inputs
     )
-    from_minus, from_plus, from_prev, from_next = trade(to_minus, to_plus, to_prev, to_next)
+    from_minus, from_plus, from_sub = trade(to_minus, to_plus, to_sub, 1)
 
     def radial(*refs):
         radial_kernel(
@@ -922,7 +931,7 @@
         packed,
     )
 
-    energy, scalar_pull, picked_all, pulls, own_pull, back_minus, back_plus, back_prev, back_next = call(
+    energy, scalar_pull, picked_all, pulls, own_pull, back_minus, back_plus, back_sub = call(
         second_kernel,
         (
             shape(1, atoms),
@@ -932,18 +941,17 @@
             shape(atoms, depth),
             shape(ghost_slab + 8, depth),
             shape(ghost_slab + 8, depth),
-            shape(ghost_sub + 8, depth),
-            shape(ghost_sub + 8, depth),
+            shape(2 * (ghost_sub + 8), depth),
         ),
         scratch=(pltpu.VMEM((depth, 2 * extended), bf16), pltpu.VMEM((extended, depth), f32)),
         flops=4 * edges * depth * extended * 2,
         vmem=28,
         name="layer_two",
     )(
-        geo, own_table, from_minus, from_plus, from_prev, from_next, scalars, extras,
+        geo, own_table, from_minus, from_plus, from_sub, scalars, extras,
         weights_all, onehot, fold_high, fold_low, back_high, back_low, heads,
     )
-    ret_minus, ret_plus, ret_prev, ret_next = trade(back_minus, back_plus, back_prev, back_next)
+    ret_minus, ret_plus, ret_sub = trade(back_minus, back_plus, back_sub, -1)
     geo_pull, scalar_slope, vector_slope, vector_value, turned_high, turned_low, base = call(
         window_kernel,
         (
@@ -979,7 +987,7 @@
         vmem=12,
         name="layer_one_back",
     )(
-        facts, geo, sums, geo_pull, own_pull, ret_minus, ret_plus, ret_prev, ret_next,
+        facts, geo, sums, geo_pull, own_pull, ret_minus, ret_plus, ret_sub,
         onehot, scalar_slope, vector_slope, vector_value, turned_high, turned_low, base,
     )
     everyone = lax.all_to_all(everyone, ("slab", "sub"), 0, 0, tiled=True)

time: 56.1 us -> 54.5 us (0.971)
  starting transfers between devices: 14.1 us -> 12 us
  blocking collectives: 12.7 us -> 13.6 us
    ppermute x8 -> x6, starting transfers between devices: 14.1 us -> 12 us  [shifted(): lax.ppermute(block, axis, [((i - distance) % count, i) for i in range(cou...]
    all_to_all x1, blocking collectives: 12.7 us -> 13.6 us  [body(): everyone = lax.all_to_all(everyone, ('slab', 'sub'), 0, 0, tiled=True)]
  transfers between devices with their start and end apart: 8 -> 6, of which waited for: 0 -> 0; matrix products, arithmetic and copies ran while one was open for 0% -> 0% of each run, Pallas kernels for 17% -> 18%
where the time goes in v3:
time: 54.5 us; the launch traced here: 54.3 us
  Pallas kernels  26.6 us (49%)
  blocking collectives  13.6 us (25%)
  starting transfers between devices  12 us (22%)
  local copies, waits for them, and re-layouts  1.28 us (2%)
  between operations  0.86 us (2%)
    pallas_call x6, Pallas kernels, run(): pl.pallas_call(kernel, out_shape=tuple(outs), in_specs=[HB if far_inputs...  26.6 us
    all_to_all x1, blocking collectives, body(): everyone = lax.all_to_all(everyone, ('slab', 'sub'), 0, 0, tiled=True)  13.6 us
    ppermute x6, starting transfers between devices, shifted(): lax.ppermute(block, axis, [((i - distance) % count, i) for i in range(cou...  12 us
    unnamed x24, local copies, waits for them, and re-layouts  1.28 us
  transfers between devices with their start and end apart: 6, of which 0 were waited for; matrix products, arithmetic and copies ran while one was open for 0% of the time, Pallas kernels for 18%

profile of v3, /device:TPU:0, one launch (start us, length us, event | category | flops | bytes accessed | tf_op | source)
XLA Modules:
  0.0 54.3 jit_solution(10016448812511293327)
XLA Ops:
  0.6 7.0 %layer_one.1 = (s32[20,128]{1,0:T(8,128)}, f32[5,128,128]{2,1,0:T(8,128)}, f32[2008,128]{1,0:T(8,128)}, f32[48,512]{1,0:T(8,128)}, f32[48,512]{1,0:T(8,128)}, /*index=5*/f32[96,512]{1,0:T(8,128)}) custom-call(f32[3,20,128]{2,1,0:T(8,128)} %refs_0_.1, s32[20,128]{1,0:T(8,128)} %refs_1_.1, s32[20,128]{1,0:T(8,128)} %refs_2_.1, s32[1,128]{1,0:T(1,128)} %bitcast.20, ...), custom_call_target="tpu_custom_call" | custom-call | flops 399360000 | bytes 2815680 | tf_op jit(solution)/shard_map/layer_one/pallas_call | solution.py:823
  7.6 3.0 %collective-permute-start.2 = (f32[96,512]{1,0:T(8,128)}, f32[96,512]{1,0:T(8,128)S(1)}, u32[]{:S(2)}, u32[]{:S(2)}) collective-permute-start(f32[96,512]{1,0:T(8,128)} %get-tuple-element.56), channel_id=1, source_target_pairs={{1,0},{0,1},{3,2},{2,3},{5,4},{4,5},{7,6},{6,7},{9,8},{8,9},{11,10... | collective-permute-start | bytes 589832 | tf_op jit(solution)/shard_map/ppermute | solution.py:23
  10.6 0.0 collective-permute-start
  10.6 4.4 %collective-permute-start.1 = (f32[48,512]{1,0:T(8,128)}, f32[48,512]{1,0:T(8,128)S(1)}, u32[]{:S(2)}, u32[]{:S(2)}) collective-permute-start(f32[48,512]{1,0:T(8,128)} %get-tuple-element.55), channel_id=1, source_target_pairs={{2,0},{4,2},{6,4},{8,6},{10,8},{12,10},{14,12},{16,14},{18,16},{20... | collective-permute-start | bytes 294920 | tf_op jit(solution)/shard_map/ppermute | solution.py:23
  15.1 1.2 %copy-done.11 = f32[2008,128]{1,0:T(8,128)S(1)} copy-done((f32[2008,128]{1,0:T(8,128)S(1)}, f32[2008,128]{1,0:T(8,128)}, u32[]{:S(2)}) %copy-start.11) | copy-done | bytes 1028120
  16.3 4.0 %radial_two.1 = (f32[512,2560]{1,0:T(8,128)S(1)}, bf16[192,2560]{1,0:T(8,128)(2,1)S(1)}, bf16[640,2560]{1,0:T(8,128)(2,1)S(1)}, bf16[512,192]{1,0:T(8,128)(2,1)S...) custom-call(f32[2008,128]{1,0:T(8,128)S(1)} %copy-done.11), custom_call_target="tpu_custom_call" | custom-call | flops 307200000 | bytes 11382784 | tf_op jit(solution)/shard_map/radial_two/pallas_call | solution.py:823
  20.3 0.0 collective-permute-done.from_minus
  20.4 0.0 copy-start
  20.4 0.0 copy-start.1
  20.4 0.0 copy-start.3
  20.4 0.0 copy-start.4
  20.4 0.0 copy-start.6
  20.4 0.0 copy-start.7
  20.4 0.0 copy-start.10
  20.4 5.7 %layer_two.1 = (f32[1,128]{1,0:T(1,128)}, f32[128,128]{1,0:T(8,128)S(1)}, f32[512,2560]{1,0:T(8,128)S(1)}, f32[4,128,128]{2,1,0:T(8,128)S(1)}, f32[128,512]{1,0:...) custom-call(f32[6,20,128]{2,1,0:T(8,128)S(1)} %get-tuple-element.52.geo.refs_1_, ...), custom_call_target="tpu_custom_call" | custom-call | flops 3355443200 | bytes 15688192 | tf_op jit(solution)/shard_map/layer_two/pallas_call | solution.py:823
  26.1 0.1 collective-permute-start.5
  26.3 0.0 collective-permute-start.3
  26.3 4.4 %collective-permute-start.4 = (f32[56,512]{1,0:T(8,128)S(1)}, f32[56,512]{1,0:T(8,128)S(1)}, u32[]{:S(2)}, u32[]{:S(2)}) collective-permute-start(f32[56,512]{1,0:T(8,128)S(1)} %get-tuple-element.79), channel_id=1, source_target_pairs={{2,0},{4,2},{6,4},{8,6},{10,8},{12,10},{14,12},{16,14},{18,16},{20... | collective-permute-start | bytes 344072 | tf_op jit(solution)/shard_map/ppermute | solution.py:23
  30.8 5.5 %radial_one.1 = (f32[4,20,128]{2,1,0:T(8,128)S(1)}, f32[128,2560]{1,0:T(8,128)S(1)}, f32[128,2560]{1,0:T(8,128)S(1)}, f32[128,2560]{1,0:T(8,128)S(1)}, bf16[896,...) custom-call(bf16[192,2560]{1,0:T(8,128)(2,1)S(1)} %get-tuple-element.69.slopes, ...), custom_call_target="tpu_custom_call" | custom-call | flops 368640000 | bytes 17551872 | tf_op jit(solution)/shard_map/radial_one/pallas_call | solution.py:823
  36.3 0.0 copy-start.8
  36.3 0.0 copy-start.9
  36.4 2.8 %layer_one_back.1 = (f32[32,16,128]{2,1,0:T(8,128)S(1)}, f32[8,128]{1,0:T(8,128)S(1)}) custom-call(f32[16,128]{1,0:T(8,128)S(1)} %get-tuple-element.67.refs_0_.refs_1_, f32[6,20,128]{2,1,0:T(8,128)S(1)} %get-tuple-element.52.geo.refs_1_, f32[5,128,128]{2,1,0:T(8,128)S(1)} %copy-done.2, f32[4,20,128]{2,1,0:T(8,128)S(1)} %get-tuple-element.76.refs_3_, ...), custom_call_target="tpu_custom_call" | custom-call | flops 15360000 | bytes 9158656 | tf_op jit(solution)/shard_map/layer_one_back/pallas_call | solution.py:823
  39.1 13.6 %all_to_all.5.refs_0_ = f32[32,16,128]{2,1,0:T(8,128)S(1)} all-to-all(f32[32,16,128]{2,1,0:T(8,128)S(1)} %get-tuple-element.87), channel_id=1, replica_groups=mesh['slab'=16,'sub'=2] {'slab','sub'}, dimensions={0} | all-to-all | bytes 524288 | tf_op jit(solution)/shard_map/all_to_all | solution.py:993
  52.7 1.6 %box.1 = (f32[3,128]{1,0:T(4,128)}, f32[3,128]{1,0:T(4,128)}, f32[3,128]{1,0:T(4,128)}, f32[6,16]{1,0:T(8,128)}, f32[3,3]{1,0:T(4,128)}, /*index=5*/f32[3,3]{1,0:T(4,128)}) custom-call(f32[32,16,128]{2,1,0:T(8,128)S(1)} %all_to_all.5.refs_0_, f32[16,128]{1,0:T(8,128)S(1)} %get-tuple-element.67.refs_0_.refs_1_, f32[8,128]{1,0:T(8,128)S(1)} %get-tuple-element.88.refs_2_, ...), custom_call_target="tpu_custom_call" | custom-call | flops 1000000 | bytes 279568 | tf_op jit(solution)/shard_map/box/pallas_call | solution.py:823
  (19 shorter events, 0.0 us)
Async XLA Ops:
  7.6 12.7 %collective-permute-start.2 = (f32[96,512]{1,0:T(8,128)}, f32[96,512]{1,0:T(8,128)S(1)}, u32[]{:S(2)}, u32[]{:S(2)}) collective-permute-start(f32[96,512]{1,0:T(8,128)} %get-tuple-element.56), channel_id=1, source_target_pairs={{1,0},{0,1},{3,2},{2,3},{5,4},{4,5},{7,6},{6,7},{9,8},{8,9},{11,10... | collective-permute-start | bytes 589832 | tf_op jit(solution)/shard_map/ppermute | solution.py:23
  10.6 9.7 %collective-permute-start = (f32[48,512]{1,0:T(8,128)}, f32[48,512]{1,0:T(8,128)S(1)}, u32[]{:S(2)}, u32[]{:S(2)}) collective-permute-start(f32[48,512]{1,0:T(8,128)} %get-tuple-element.54), channel_id=1, source_target_pairs={{30,0},{0,2},{2,4},{4,6},{6,8},{8,10},{10,12},{12,14},{14,16},{16,... | collective-permute-start | bytes 294920 | tf_op jit(solution)/shard_map/ppermute | solution.py:23
  10.6 9.7 %collective-permute-start.1 = (f32[48,512]{1,0:T(8,128)}, f32[48,512]{1,0:T(8,128)S(1)}, u32[]{:S(2)}, u32[]{:S(2)}) collective-permute-start(f32[48,512]{1,0:T(8,128)} %get-tuple-element.55), channel_id=1, source_target_pairs={{2,0},{4,2},{6,4},{8,6},{10,8},{12,10},{14,12},{16,14},{18,16},{20... | collective-permute-start | bytes 294920 | tf_op jit(solution)/shard_map/ppermute | solution.py:23
  15.1 1.2 %copy-start.11 = (f32[2008,128]{1,0:T(8,128)S(1)}, f32[2008,128]{1,0:T(8,128)}, u32[]{:S(2)}) copy-start(f32[2008,128]{1,0:T(8,128)} %get-tuple-element.51.refs_0_) | copy-start | bytes 3084292
  20.4 10.4 %copy-start = (f32[6,128,128]{2,1,0:T(8,128)S(1)}, f32[6,128,128]{2,1,0:T(8,128)}, u32[]{:S(2)}) copy-start(f32[6,128,128]{2,1,0:T(8,128)} %node_one.1) | copy-start | bytes 1179652
  20.4 10.4 %copy-start.1 = (f32[5,128,128]{2,1,0:T(8,128)S(1)}, f32[5,128,128]{2,1,0:T(8,128)}, u32[]{:S(2)}) copy-start(f32[5,128,128]{2,1,0:T(8,128)} %node_two.1) | copy-start | bytes 983044
  20.4 10.4 %copy-start.3 = (f32[2,64,64]{2,1,0:T(8,128)S(1)}, f32[2,64,64]{2,1,0:T(8,128)}, u32[]{:S(2)}) copy-start(f32[2,64,64]{2,1,0:T(8,128)} %radial_mid.1) | copy-start | bytes 98308
  20.4 10.3 %copy-start.4 = (f32[256,64]{0,1:T(8,128)S(1)}, f32[256,64]{0,1:T(8,128)}, u32[]{:S(2)}) copy-start(f32[256,64]{0,1:T(8,128)} %param.41) | copy-start | bytes 196612
  20.4 10.3 %copy-start.5 = (s32[20,128]{1,0:T(8,128)S(1)}, s32[20,128]{1,0:T(8,128)}, u32[]{:S(2)}) copy-start(s32[20,128]{1,0:T(8,128)} %get-tuple-element.74.kinds) | copy-start | bytes 30724
  20.4 10.3 %copy-start.6 = (f32[8,128]{1,0:T(8,128)S(1)}, f32[8,128]{1,0:T(8,128)}, u32[]{:S(2)}) copy-start(f32[8,128]{1,0:T(8,128)} %embedding.1) | copy-start | bytes 12292
  20.4 10.3 %copy-start.7 = (f32[64,8]{0,1:T(8,128)S(1)}, f32[64,8]{0,1:T(8,128)}, u32[]{:S(2)}) copy-start(f32[64,8]{0,1:T(8,128)} %param.39) | copy-start | bytes 6148
  20.4 10.3 %copy-start.10 = (f32[128]{0:T(128)S(1)}, f32[128]{0:T(128)}, u32[]{:S(2)}) copy-start(f32[128]{0:T(128)} %param.47) | copy-start | bytes 1540
  26.1 10.2 %collective-permute-start.5 = (f32[112,512]{1,0:T(8,128)S(1)}, f32[112,512]{1,0:T(8,128)S(1)}, u32[]{:S(2)}, u32[]{:S(2)}) collective-permute-start(f32[112,512]{1,0:T(8,128)S(1)} %get-tuple-element.80), channel_id=1, source_target_pairs={{1,0},{0,1},{3,2},{2,3},{5,4},{4,5},{7,6},{6,7},{9,8},{8,9},{11,10... | collective-permute-start | bytes 688136 | tf_op jit(solution)/shard_map/ppermute | solution.py:23
  26.3 10.0 %collective-permute-start.3 = (f32[56,512]{1,0:T(8,128)S(1)}, f32[56,512]{1,0:T(8,128)S(1)}, u32[]{:S(2)}, u32[]{:S(2)}) collective-permute-start(f32[56,512]{1,0:T(8,128)S(1)} %get-tuple-element.78), channel_id=1, source_target_pairs={{30,0},{0,2},{2,4},{4,6},{6,8},{8,10},{10,12},{12,14},{14,16},{16,... | collective-permute-start | bytes 344072 | tf_op jit(solution)/shard_map/ppermute | solution.py:23
  26.3 10.0 %collective-permute-start.4 = (f32[56,512]{1,0:T(8,128)S(1)}, f32[56,512]{1,0:T(8,128)S(1)}, u32[]{:S(2)}, u32[]{:S(2)}) collective-permute-start(f32[56,512]{1,0:T(8,128)S(1)} %get-tuple-element.79), channel_id=1, source_target_pairs={{2,0},{4,2},{6,4},{8,6},{10,8},{12,10},{14,12},{16,14},{18,16},{20... | collective-permute-start | bytes 344072 | tf_op jit(solution)/shard_map/ppermute | solution.py:23
  30.8 5.5 %copy-start.2 = (f32[5,128,128]{2,1,0:T(8,128)S(1)}, f32[5,128,128]{2,1,0:T(8,128)}, u32[]{:S(2)}) copy-start(f32[5,128,128]{2,1,0:T(8,128)} %get-tuple-element.68.refs_2_) | copy-start | bytes 983044
  36.3 16.4 %copy-start.8 = (f32[3,3]{1,0:T(4,128)S(1)}, f32[3,3]{1,0:T(4,128)}, u32[]{:S(2)}) copy-start(f32[3,3]{1,0:T(4,128)} %refs_3_.1) | copy-start | bytes 112
  36.3 16.3 %copy-start.9 = (f32[3,3]{1,0:T(4,128)S(1)}, f32[3,3]{1,0:T(4,128)}, u32[]{:S(2)}) copy-start(f32[3,3]{1,0:T(4,128)} %refs_4_.1) | copy-start | bytes 112

commit v4 on v3

--- a/solution.py
+++ b/solution.py
@@ -129,24 +129,37 @@
     return jnp.concatenate([waves[start : start + count, first + j, :] for j in range(GROUP)], axis=1)
 
 
-def hidden_values(value, inner, mid_a, mid_b):
-    x = dot(inner, value_stack_small(value))
-    for mid in (mid_a, mid_b, None):
-        h = x * sigmoid(x)
-        if mid is not None:
-            x = dot(mid, value_stack(h))
-    return h
-
-
-def hidden_pairs(value, slope, inner, mid_a, mid_b):
-    x, dx = dot(inner, value_stack_small(value)), dot(inner, value_stack_small(slope))
-    for mid in (mid_a, mid_b, None):
+def hidden_values(values, inner, mid_a, mid_b):
+    xs = [dot(inner, value_stack_small(value)) for value in values]
+    for mid in (mid_a, mid_b):
+        xs = [dot(mid, value_stack(x * sigmoid(x))) for x in xs]
+    return [x * sigmoid(x) for x in xs]
+
+
+def hidden_pairs(values, slopes, inner, mid_a, mid_b, between=()):
+    between = list(between)
+
+    def activated(x, dx):
         gate = sigmoid(x)
         h = x * gate
-        dh = (gate + h * (1.0 - gate)) * dx
-        if mid is not None:
-            x, dx = dot(mid, value_stack(h)), dot(mid, value_stack(dh))
-    return h, dh
+        return h, (gate + h * (1.0 - gate)) * dx
+
+    pairs = [
+        (dot(inner, value_stack_small(value)), dot(inner, value_stack_small(slope)))
+        for value, slope in zip(values, slopes)
+    ]
+    for mid in (mid_a, mid_b):
+        after = []
+        for i, (x, dx) in enumerate(pairs):
+            h, dh = activated(x, dx)
+            after.append((dot(mid, value_stack(h)), dot(mid, value_stack(dh))))
+            if between and i % 2:
+                between.pop(0)()
+        pairs = after
+    pairs = [activated(x, dx) for x, dx in pairs]
+    for work in between:
+        work()
+    return pairs
 
 
 def species_matrix(first_mixing, embedding):
@@ -249,11 +262,12 @@
     lifted = species_matrix(node_one[0], embedding[...])
     sums[...] = jnp.zeros_like(sums)
 
+    values = [basis_group(waves, i * GROUP, 0, basis_count) for i in range(slots // GROUP)]
+    hidden = hidden_values(values, inner, mid_a, mid_b)
+
     def group(step, carry):
         first = step * GROUP
-        value = basis_group(waves, first, 0, basis_count)
-        h = hidden_values(value, inner, mid_a, mid_b)
-        weights = dot(outer, value_stack(h))
+        weights = dot(outer, value_stack(hidden[step]))
         picked = picked_group(lifted, geo, kinds, first, species_count)
         totals = [0.0] * 4
         for j in range(GROUP):
@@ -352,7 +366,7 @@
 def radial_kernel(
     packed,
     weights_all, slopes, onehot, outer, fold_high, fold_low, back_high, back_low,
-    geo, table, scalars, extras, facts, heads, waves, *, slab_rows, sub_rows, moves, basis_count,
+    geo, picked_own, scalars, extras, facts, heads, waves, *, slab_rows, sub_rows, moves, basis_count,
 ):
     slots, atoms = geo.shape[1:]
     width = scalars.shape[0]
@@ -376,7 +390,7 @@
     start += heads.shape[0]
     for i in range(2 * basis_count):
         waves[i] = packed[start + i * packed_step(slots) : start + i * packed_step(slots) + slots]
-    table[:, :atoms], table[:, atoms:] = parts(packed[width : 5 * width])
+    table = jnp.concatenate(parts(packed[width : 5 * width]), axis=1)
     for a in range(6):
         start = 5 * width + a * packed_step(slots)
         geo[a] = packed[start : start + slots]
@@ -397,11 +411,15 @@
     inner = weight_stack_t(radial_in)
     mid_a, mid_b = weight_stack(radial_mid[0]), weight_stack(radial_mid[1])
 
+    values, slopes_in = (
+        [basis_group(waves, i * GROUP, start, basis_count) for i in range(slots // GROUP)] for start in (0, basis_count)
+    )
+    hidden = hidden_pairs(values, slopes_in, inner, mid_a, mid_b)
+
     def group(step, carry):
         first = step * GROUP
         at = span_of(step * GROUP * atoms, GROUP * atoms)
-        value, slope = (basis_group(waves, first, i * basis_count, basis_count) for i in range(2))
-        h, dh = hidden_pairs(value, slope, inner, mid_a, mid_b)
+        h, dh = hidden[step]
         slopes[:, at] = value_stack(dh)
         blocks = []
         for j in range(GROUP):
@@ -411,7 +429,9 @@
             blocks.append(jnp.where(iota((rows, atoms), 0) == row, weight, 0.0).astype(bf16))
         block = jnp.concatenate(blocks, axis=1)
         own, ghosts = block[:atoms], block[atoms:]
-        onehot[:, at] = jnp.concatenate([own, own, ghosts, ghosts], axis=0)
+        both = jnp.concatenate([own, own], axis=0)
+        onehot[:, at] = jnp.concatenate([both, ghosts, ghosts], axis=0)
+        picked_own[:, at] = dot(table, both)
         weights_all[:, at] = dot(outer[...], value_stack(h))
         return carry
 
@@ -419,7 +439,7 @@
 
 
 def second_kernel(
-    geo, own_table, from_minus, from_plus, from_sub, scalars, extras,
+    geo, picked_own, from_minus, from_plus, from_sub, scalars, extras,
     weights_all, onehot, fold_high, fold_low, back_high, back_low, heads,
     energy, scalar_pull, picked_all, sums, own_pull, back_minus, back_plus, back_sub,
     table, pulled,
@@ -429,8 +449,7 @@
     depth = 4 * width
     ghosts = jnp.concatenate([from_minus[...], from_plus[...], from_sub[...]], axis=0)
     high = ghosts.astype(bf16).astype(f32)
-    table[:, : 2 * atoms] = own_table[...]
-    table[:, 2 * atoms :] = jnp.transpose(jnp.concatenate([high, ghosts - high], axis=0)).astype(bf16)
+    table[...] = jnp.transpose(jnp.concatenate([high, ghosts - high], axis=0)).astype(bf16)
     ghost_rows = ghosts.shape[0]
     sums[...] = jnp.zeros_like(sums)
 
@@ -440,7 +459,7 @@
     def forward(step, carry):
         first = step * GROUP
         at = span_of(step * GROUP * atoms, GROUP * atoms)
-        picked = dot(table[...], onehot[:, at])
+        picked = picked_own[:, at] + dot(table[...], onehot[2 * atoms :, at])
         picked_all[:, at] = picked
         totals = [0.0] * 4
         for j in range(GROUP):
@@ -538,8 +557,7 @@
     def group(step, carry):
         first = step * GROUP
         at = span_of(step * GROUP * atoms, GROUP * atoms)
-        value, slope = (basis_group(waves, first, i * basis_count, basis_count) for i in range(2))
-        h, dh = hidden_pairs(value, slope, inner, mid_a, mid_b)
+        h, dh = hidden[step]
         picked = picked_group(lifted, geo, kinds, first, species_count)
         weights_slope = dot(outer, value_stack(dh))
         scalar_slope[:, at] = weights_slope[:width] * picked
@@ -570,9 +588,12 @@
                 geo_pull[a + 1, pl.ds(first + j, 1), :] = jnp.sum(turn, axis=0, keepdims=True)
         return carry
 
-    for step in range(slots // GROUP):
-        group(step, 0)
-        edge_group(step, 0)
+    values, slopes_in = (
+        [basis_group(waves, i * GROUP, start, basis_count) for i in range(slots // GROUP)] for start in (0, basis_count)
+    )
+    works = [lambda i=i: edge_group(i, 0) for i in range(slots // GROUP)]
+    hidden = hidden_pairs(values, slopes_in, inner, mid_a, mid_b, works)
+    over_groups(slots // GROUP, group, 0)
 
 
 def third_kernel(
@@ -904,7 +925,7 @@
 
     (
         weights_all, slopes, onehot, outer, fold_high, fold_low, back_high, back_low,
-        geo, own_table, scalars, extras, facts, heads, waves,
+        geo, picked_own, scalars, extras, facts, heads, waves,
     ) = call(
         radial,
         (
@@ -917,7 +938,7 @@
             shape(3 * width, readout_hidden.shape[0], dtype=bf16),
             shape(3 * width, readout_hidden.shape[0], dtype=bf16),
             shape(6, slots, atoms),
-            shape(depth, 2 * atoms, dtype=bf16),
+            shape(depth, edges),
             shape(width, atoms),
             shape(4, 8, 2 * atoms),
             shape(FACTS, atoms),
@@ -925,7 +946,7 @@
             shape(2 * radial_two_in.shape[0], slots, atoms),
         ),
         flops=12 * edges * 10000,
-        vmem=12,
+        vmem=16,
         name="radial_two",
     )(
         packed,
@@ -943,12 +964,15 @@
             shape(ghost_slab + 8, depth),
             shape(2 * (ghost_sub + 8), depth),
         ),
-        scratch=(pltpu.VMEM((depth, 2 * extended), bf16), pltpu.VMEM((extended, depth), f32)),
+        scratch=(
+            pltpu.VMEM((depth, 2 * (extended - atoms)), bf16),
+            pltpu.VMEM((extended, depth), f32),
+        ),
         flops=4 * edges * depth * extended * 2,
-        vmem=28,
+        vmem=20,
         name="layer_two",
     )(
-        geo, own_table, from_minus, from_plus, from_sub, scalars, extras,
+        geo, picked_own, from_minus, from_plus, from_sub, scalars, extras,
         weights_all, onehot, fold_high, fold_low, back_high, back_low, heads,
     )
     ret_minus, ret_plus, ret_sub = trade(back_minus, back_plus, back_sub, -1)

time: 54.5 us -> 51.4 us (0.943)
  Pallas kernels: 26.6 us -> 22.5 us
  blocking collectives: 13.6 us -> 14.6 us
    pallas_call x6, Pallas kernels: 26.6 us -> 22.5 us  [run(): pl.pallas_call(kernel, out_shape=tuple(outs), in_specs=[HB if far_inputs...]
    all_to_all x1, blocking collectives: 13.6 us -> 14.6 us  [body(): everyone = lax.all_to_all(everyone, ('slab', 'sub'), 0, 0, tiled=True)]
  transfers between devices with their start and end apart: 6 -> 6, of which waited for: 0 -> 0; matrix products, arithmetic and copies ran while one was open for 0% -> 0% of each run, Pallas kernels for 18% -> 15%
where the time goes in v4:
time: 51.4 us; the launch traced here: 51.2 us
  Pallas kernels  22.5 us (44%)
  blocking collectives  14.6 us (28%)
  starting transfers between devices  12 us (23%)
  local copies, waits for them, and re-layouts  1.28 us (2%)
  between operations  0.86 us (2%)
    pallas_call x6, Pallas kernels, run(): pl.pallas_call(kernel, out_shape=tuple(outs), in_specs=[HB if far_inputs...  22.5 us
    all_to_all x1, blocking collectives, body(): everyone = lax.all_to_all(everyone, ('slab', 'sub'), 0, 0, tiled=True)  14.6 us
    ppermute x6, starting transfers between devices, shifted(): lax.ppermute(block, axis, [((i - distance) % count, i) for i in range(cou...  12 us
    unnamed x24, local copies, waits for them, and re-layouts  1.28 us
  transfers between devices with their start and end apart: 6, of which 0 were waited for; matrix products, arithmetic and copies ran while one was open for 0% of the time, Pallas kernels for 15%

profile of v4, /device:TPU:0, one launch (start us, length us, event | category | flops | bytes accessed | tf_op | source)
XLA Modules:
  0.0 51.2 jit_solution(15181777077506146603)
XLA Ops:
  0.6 5.0 %layer_one.1 = (s32[20,128]{1,0:T(8,128)}, f32[5,128,128]{2,1,0:T(8,128)}, f32[2008,128]{1,0:T(8,128)}, f32[48,512]{1,0:T(8,128)}, f32[48,512]{1,0:T(8,128)}, /*index=5*/f32[96,512]{1,0:T(8,128)}) custom-call(f32[3,20,128]{2,1,0:T(8,128)} %refs_0_.1, s32[20,128]{1,0:T(8,128)} %refs_1_.1, s32[20,128]{1,0:T(8,128)} %refs_2_.1, s32[1,128]{1,0:T(1,128)} %bitcast.20, ...), custom_call_target="tpu_custom_call" | custom-call | flops 399360000 | bytes 2815680 | tf_op jit(solution)/shard_map/layer_one/pallas_call | solution.py:844
  5.6 3.0 %collective-permute-start.2 = (f32[96,512]{1,0:T(8,128)}, f32[96,512]{1,0:T(8,128)S(1)}, u32[]{:S(2)}, u32[]{:S(2)}) collective-permute-start(f32[96,512]{1,0:T(8,128)} %get-tuple-element.56), channel_id=1, source_target_pairs={{1,0},{0,1},{3,2},{2,3},{5,4},{4,5},{7,6},{6,7},{9,8},{8,9},{11,10... | collective-permute-start | bytes 589832 | tf_op jit(solution)/shard_map/ppermute | solution.py:23
  8.6 0.0 collective-permute-start
  8.6 4.4 %collective-permute-start.1 = (f32[48,512]{1,0:T(8,128)}, f32[48,512]{1,0:T(8,128)S(1)}, u32[]{:S(2)}, u32[]{:S(2)}) collective-permute-start(f32[48,512]{1,0:T(8,128)} %get-tuple-element.55), channel_id=1, source_target_pairs={{2,0},{4,2},{6,4},{8,6},{10,8},{12,10},{14,12},{16,14},{18,16},{20... | collective-permute-start | bytes 294920 | tf_op jit(solution)/shard_map/ppermute | solution.py:23
  13.1 1.2 %copy-done.11 = f32[2008,128]{1,0:T(8,128)S(1)} copy-done((f32[2008,128]{1,0:T(8,128)S(1)}, f32[2008,128]{1,0:T(8,128)}, u32[]{:S(2)}) %copy-start.11) | copy-done | bytes 1028120
  14.3 3.3 %radial_two.1 = (f32[512,2560]{1,0:T(8,128)S(1)}, bf16[192,2560]{1,0:T(8,128)(2,1)S(1)}, bf16[640,2560]{1,0:T(8,128)(2,1)S(1)}, bf16[512,192]{1,0:T(8,128)(2,1)S...) custom-call(f32[2008,128]{1,0:T(8,128)S(1)} %copy-done.11), custom_call_target="tpu_custom_call" | custom-call | flops 307200000 | bytes 16363520 | tf_op jit(solution)/shard_map/radial_two/pallas_call | solution.py:844
  17.6 0.0 collective-permute-done.from_minus
  17.6 0.0 copy-start
  17.7 0.0 copy-start.1
  17.7 0.0 copy-start.3
  17.7 0.0 copy-start.4
  17.7 0.0 copy-start.6
  17.7 0.0 copy-start.7
  17.7 0.0 copy-start.10
  17.7 5.3 %layer_two.1 = (f32[1,128]{1,0:T(1,128)}, f32[128,128]{1,0:T(8,128)S(1)}, f32[512,2560]{1,0:T(8,128)S(1)}, f32[4,128,128]{2,1,0:T(8,128)S(1)}, f32[128,512]{1,0:...) custom-call(f32[6,20,128]{2,1,0:T(8,128)S(1)} %get-tuple-element.52.geo.refs_1_, ...), custom_call_target="tpu_custom_call" | custom-call | flops 3355443200 | bytes 20668928 | tf_op jit(solution)/shard_map/layer_two/pallas_call | solution.py:844
  23.0 0.1 collective-permute-start.5
  23.2 0.0 collective-permute-start.3
  23.2 4.4 %collective-permute-start.4 = (f32[56,512]{1,0:T(8,128)S(1)}, f32[56,512]{1,0:T(8,128)S(1)}, u32[]{:S(2)}, u32[]{:S(2)}) collective-permute-start(f32[56,512]{1,0:T(8,128)S(1)} %get-tuple-element.79), channel_id=1, source_target_pairs={{2,0},{4,2},{6,4},{8,6},{10,8},{12,10},{14,12},{16,14},{18,16},{20... | collective-permute-start | bytes 344072 | tf_op jit(solution)/shard_map/ppermute | solution.py:23
  27.7 4.5 %radial_one.1 = (f32[4,20,128]{2,1,0:T(8,128)S(1)}, f32[128,2560]{1,0:T(8,128)S(1)}, f32[128,2560]{1,0:T(8,128)S(1)}, f32[128,2560]{1,0:T(8,128)S(1)}, bf16[896,...) custom-call(bf16[192,2560]{1,0:T(8,128)(2,1)S(1)} %get-tuple-element.69.slopes, ...), custom_call_target="tpu_custom_call" | custom-call | flops 368640000 | bytes 17551872 | tf_op jit(solution)/shard_map/radial_one/pallas_call | solution.py:844
  32.2 0.0 copy-start.8
  32.2 0.0 copy-start.9
  32.2 2.8 %layer_one_back.1 = (f32[32,16,128]{2,1,0:T(8,128)S(1)}, f32[8,128]{1,0:T(8,128)S(1)}) custom-call(f32[16,128]{1,0:T(8,128)S(1)} %get-tuple-element.67.refs_0_.refs_1_, f32[6,20,128]{2,1,0:T(8,128)S(1)} %get-tuple-element.52.geo.refs_1_, f32[5,128,128]{2,1,0:T(8,128)S(1)} %copy-done.2, f32[4,20,128]{2,1,0:T(8,128)S(1)} %get-tuple-element.76.refs_3_, ...), custom_call_target="tpu_custom_call" | custom-call | flops 15360000 | bytes 9158656 | tf_op jit(solution)/shard_map/layer_one_back/pallas_call | solution.py:844
  35.0 14.6 %all_to_all.5.refs_0_ = f32[32,16,128]{2,1,0:T(8,128)S(1)} all-to-all(f32[32,16,128]{2,1,0:T(8,128)S(1)} %get-tuple-element.87), channel_id=1, replica_groups=mesh['slab'=16,'sub'=2] {'slab','sub'}, dimensions={0} | all-to-all | bytes 524288 | tf_op jit(solution)/shard_map/all_to_all | solution.py:1017
  49.6 1.6 %box.1 = (f32[3,128]{1,0:T(4,128)}, f32[3,128]{1,0:T(4,128)}, f32[3,128]{1,0:T(4,128)}, f32[6,16]{1,0:T(8,128)}, f32[3,3]{1,0:T(4,128)}, /*index=5*/f32[3,3]{1,0:T(4,128)}) custom-call(f32[32,16,128]{2,1,0:T(8,128)S(1)} %all_to_all.5.refs_0_, f32[16,128]{1,0:T(8,128)S(1)} %get-tuple-element.67.refs_0_.refs_1_, f32[8,128]{1,0:T(8,128)S(1)} %get-tuple-element.88.refs_2_, ...), custom_call_target="tpu_custom_call" | custom-call | flops 1000000 | bytes 279568 | tf_op jit(solution)/shard_map/box/pallas_call | solution.py:844
  (19 shorter events, 0.0 us)
Async XLA Ops:
  5.6 12.0 %collective-permute-start.2 = (f32[96,512]{1,0:T(8,128)}, f32[96,512]{1,0:T(8,128)S(1)}, u32[]{:S(2)}, u32[]{:S(2)}) collective-permute-start(f32[96,512]{1,0:T(8,128)} %get-tuple-element.56), channel_id=1, source_target_pairs={{1,0},{0,1},{3,2},{2,3},{5,4},{4,5},{7,6},{6,7},{9,8},{8,9},{11,10... | collective-permute-start | bytes 589832 | tf_op jit(solution)/shard_map/ppermute | solution.py:23
  8.6 9.0 %collective-permute-start = (f32[48,512]{1,0:T(8,128)}, f32[48,512]{1,0:T(8,128)S(1)}, u32[]{:S(2)}, u32[]{:S(2)}) collective-permute-start(f32[48,512]{1,0:T(8,128)} %get-tuple-element.54), channel_id=1, source_target_pairs={{30,0},{0,2},{2,4},{4,6},{6,8},{8,10},{10,12},{12,14},{14,16},{16,... | collective-permute-start | bytes 294920 | tf_op jit(solution)/shard_map/ppermute | solution.py:23
  8.6 9.0 %collective-permute-start.1 = (f32[48,512]{1,0:T(8,128)}, f32[48,512]{1,0:T(8,128)S(1)}, u32[]{:S(2)}, u32[]{:S(2)}) collective-permute-start(f32[48,512]{1,0:T(8,128)} %get-tuple-element.55), channel_id=1, source_target_pairs={{2,0},{4,2},{6,4},{8,6},{10,8},{12,10},{14,12},{16,14},{18,16},{20... | collective-permute-start | bytes 294920 | tf_op jit(solution)/shard_map/ppermute | solution.py:23
  13.1 1.2 %copy-start.11 = (f32[2008,128]{1,0:T(8,128)S(1)}, f32[2008,128]{1,0:T(8,128)}, u32[]{:S(2)}) copy-start(f32[2008,128]{1,0:T(8,128)} %get-tuple-element.51.refs_0_) | copy-start | bytes 3084292
  17.6 10.0 %copy-start = (f32[6,128,128]{2,1,0:T(8,128)S(1)}, f32[6,128,128]{2,1,0:T(8,128)}, u32[]{:S(2)}) copy-start(f32[6,128,128]{2,1,0:T(8,128)} %node_one.1) | copy-start | bytes 1179652
  17.7 9.9 %copy-start.1 = (f32[5,128,128]{2,1,0:T(8,128)S(1)}, f32[5,128,128]{2,1,0:T(8,128)}, u32[]{:S(2)}) copy-start(f32[5,128,128]{2,1,0:T(8,128)} %node_two.1) | copy-start | bytes 983044
  17.7 9.9 %copy-start.3 = (f32[2,64,64]{2,1,0:T(8,128)S(1)}, f32[2,64,64]{2,1,0:T(8,128)}, u32[]{:S(2)}) copy-start(f32[2,64,64]{2,1,0:T(8,128)} %radial_mid.1) | copy-start | bytes 98308
  17.7 9.9 %copy-start.4 = (f32[256,64]{0,1:T(8,128)S(1)}, f32[256,64]{0,1:T(8,128)}, u32[]{:S(2)}) copy-start(f32[256,64]{0,1:T(8,128)} %param.41) | copy-start | bytes 196612
  17.7 9.9 %copy-start.5 = (s32[20,128]{1,0:T(8,128)S(1)}, s32[20,128]{1,0:T(8,128)}, u32[]{:S(2)}) copy-start(s32[20,128]{1,0:T(8,128)} %get-tuple-element.74.kinds) | copy-start | bytes 30724
  17.7 9.9 %copy-start.6 = (f32[8,128]{1,0:T(8,128)S(1)}, f32[8,128]{1,0:T(8,128)}, u32[]{:S(2)}) copy-start(f32[8,128]{1,0:T(8,128)} %embedding.1) | copy-start | bytes 12292
  17.7 9.9 %copy-start.7 = (f32[64,8]{0,1:T(8,128)S(1)}, f32[64,8]{0,1:T(8,128)}, u32[]{:S(2)}) copy-start(f32[64,8]{0,1:T(8,128)} %param.39) | copy-start | bytes 6148
  17.7 9.9 %copy-start.10 = (f32[128]{0:T(128)S(1)}, f32[128]{0:T(128)}, u32[]{:S(2)}) copy-start(f32[128]{0:T(128)} %param.47) | copy-start | bytes 1540
  23.0 9.2 %collective-permute-start.5 = (f32[112,512]{1,0:T(8,128)S(1)}, f32[112,512]{1,0:T(8,128)S(1)}, u32[]{:S(2)}, u32[]{:S(2)}) collective-permute-start(f32[112,512]{1,0:T(8,128)S(1)} %get-tuple-element.80), channel_id=1, source_target_pairs={{1,0},{0,1},{3,2},{2,3},{5,4},{4,5},{7,6},{6,7},{9,8},{8,9},{11,10... | collective-permute-start | bytes 688136 | tf_op jit(solution)/shard_map/ppermute | solution.py:23
  23.2 9.0 %collective-permute-start.3 = (f32[56,512]{1,0:T(8,128)S(1)}, f32[56,512]{1,0:T(8,128)S(1)}, u32[]{:S(2)}, u32[]{:S(2)}) collective-permute-start(f32[56,512]{1,0:T(8,128)S(1)} %get-tuple-element.78), channel_id=1, source_target_pairs={{30,0},{0,2},{2,4},{4,6},{6,8},{8,10},{10,12},{12,14},{14,16},{16,... | collective-permute-start | bytes 344072 | tf_op jit(solution)/shard_map/ppermute | solution.py:23
  23.2 9.0 %collective-permute-start.4 = (f32[56,512]{1,0:T(8,128)S(1)}, f32[56,512]{1,0:T(8,128)S(1)}, u32[]{:S(2)}, u32[]{:S(2)}) collective-permute-start(f32[56,512]{1,0:T(8,128)S(1)} %get-tuple-element.79), channel_id=1, source_target_pairs={{2,0},{4,2},{6,4},{8,6},{10,8},{12,10},{14,12},{16,14},{18,16},{20... | collective-permute-start | bytes 344072 | tf_op jit(solution)/shard_map/ppermute | solution.py:23
  27.7 4.5 %copy-start.2 = (f32[5,128,128]{2,1,0:T(8,128)S(1)}, f32[5,128,128]{2,1,0:T(8,128)}, u32[]{:S(2)}) copy-start(f32[5,128,128]{2,1,0:T(8,128)} %get-tuple-element.68.refs_2_) | copy-start | bytes 983044
  32.2 17.4 %copy-start.8 = (f32[3,3]{1,0:T(4,128)S(1)}, f32[3,3]{1,0:T(4,128)}, u32[]{:S(2)}) copy-start(f32[3,3]{1,0:T(4,128)} %refs_3_.1) | copy-start | bytes 112
  32.2 17.4 %copy-start.9 = (f32[3,3]{1,0:T(4,128)S(1)}, f32[3,3]{1,0:T(4,128)}, u32[]{:S(2)}) copy-start(f32[3,3]{1,0:T(4,128)} %refs_4_.1) | copy-start | bytes 112

commit v5 on v4

--- a/solution.py
+++ b/solution.py
@@ -265,10 +265,16 @@
     values = [basis_group(waves, i * GROUP, 0, basis_count) for i in range(slots // GROUP)]
     hidden = hidden_values(values, inner, mid_a, mid_b)
 
+    def multiplied(step):
+        if step == slots // GROUP:
+            return None
+        weights = dot(outer, value_stack(hidden[step]))
+        return weights, picked_group(lifted, geo, kinds, step * GROUP, species_count)
+
     def group(step, carry):
         first = step * GROUP
-        weights = dot(outer, value_stack(hidden[step]))
-        picked = picked_group(lifted, geo, kinds, first, species_count)
+        weights, picked = carry
+        carry = multiplied(step + 1)
         totals = [0.0] * 4
         for j in range(GROUP):
             at = slice(j * atoms, (j + 1) * atoms)
@@ -281,7 +287,7 @@
             sums[a] += totals[a]
         return carry
 
-    over_groups(slots // GROUP, group, 0)
+    over_groups(slots // GROUP, group, multiplied(0))
 
     early_sums = pltpu.make_async_copy(sums.at[:4], far_sums.at[:4], gone.at[2])
     early_sums.start()
@@ -456,11 +462,17 @@
     def units(first, j):
         return [geo[a, pl.ds(first + j, 1), :] for a in range(3)]
 
+    def gathered(step):
+        if step == slots // GROUP:
+            return None
+        return dot(table[...], onehot[2 * atoms :, span_of(step * GROUP * atoms, GROUP * atoms)])
+
     def forward(step, carry):
         first = step * GROUP
         at = span_of(step * GROUP * atoms, GROUP * atoms)
-        picked = picked_own[:, at] + dot(table[...], onehot[2 * atoms :, at])
+        picked = picked_own[:, at] + carry
         picked_all[:, at] = picked
+        carry = gathered(step + 1)
         totals = [0.0] * 4
         for j in range(GROUP):
             span = slice(j * atoms, (j + 1) * atoms)
@@ -477,7 +489,7 @@
             sums[a] += totals[a]
         return carry
 
-    over_groups(slots // GROUP, forward, 0)
+    over_groups(slots // GROUP, forward, gathered(0))
 
     scalar_sum = sums[0]
     vectors = [sums[1], sums[2], sums[3]]
@@ -500,6 +512,10 @@
         sums[a + 1] = vectors[a] * double
     pulled[...] = jnp.zeros_like(pulled)
 
+    def scatter(at, split):
+        chosen = jnp.concatenate([onehot[:atoms, at], onehot[2 * atoms : 2 * atoms + ghost_rows, at]], axis=0)
+        pulled[...] += dot_nt(jnp.concatenate([chosen, chosen], axis=1), split)
+
     def backward(step, carry):
         first = step * GROUP
         at = span_of(step * GROUP * atoms, GROUP * atoms)
@@ -515,12 +531,11 @@
             high, low = parts(jnp.concatenate(given, axis=0))
             highs.append(high)
             lows.append(low)
-        split = jnp.concatenate(highs + lows, axis=1)
-        chosen = jnp.concatenate([onehot[:atoms, at], onehot[2 * atoms : 2 * atoms + ghost_rows, at]], axis=0)
-        pulled[...] += dot_nt(jnp.concatenate([chosen, chosen], axis=1), split)
-        return carry
-
-    over_groups(slots // GROUP, backward, 0)
+        if carry is not None:
+            scatter(*carry)
+        return at, jnp.concatenate(highs + lows, axis=1)
+
+    scatter(*over_groups(slots // GROUP, backward, None))
     own_pull[...] = pulled[:atoms]
     start = atoms
     fill = jnp.zeros((8, depth - extras.shape[2]), f32)

time: 51.4 us -> 51.4 us (level)
  no operation moved by 1% of the time
where the time goes in v5:
time: 51.4 us; the launch traced here: 51.2 us
  Pallas kernels  22.5 us (44%)
  blocking collectives  14.6 us (28%)
  starting transfers between devices  12 us (23%)
  local copies, waits for them, and re-layouts  1.28 us (2%)
  between operations  0.86 us (2%)
    pallas_call x6, Pallas kernels, run(): pl.pallas_call(kernel, out_shape=tuple(outs), in_specs=[HB if far_inputs...  22.5 us
    all_to_all x1, blocking collectives, body(): everyone = lax.all_to_all(everyone, ('slab', 'sub'), 0, 0, tiled=True)  14.6 us
    ppermute x6, starting transfers between devices, shifted(): lax.ppermute(block, axis, [((i - distance) % count, i) for i in range(cou...  12 us
    unnamed x24, local copies, waits for them, and re-layouts  1.28 us
  transfers between devices with their start and end apart: 6, of which 0 were waited for; matrix products, arithmetic and copies ran while one was open for 0% of the time, Pallas kernels for 15%

profile of v5, /device:TPU:0, one launch (start us, length us, event | category | flops | bytes accessed | tf_op | source)
XLA Modules:
  0.0 51.2 jit_solution(14484605873478222125)
XLA Ops:
  0.6 5.0 %layer_one.1 = (s32[20,128]{1,0:T(8,128)}, f32[5,128,128]{2,1,0:T(8,128)}, f32[2008,128]{1,0:T(8,128)}, f32[48,512]{1,0:T(8,128)}, f32[48,512]{1,0:T(8,128)}, /*index=5*/f32[96,512]{1,0:T(8,128)}) custom-call(f32[3,20,128]{2,1,0:T(8,128)} %refs_0_.1, s32[20,128]{1,0:T(8,128)} %refs_1_.1, s32[20,128]{1,0:T(8,128)} %refs_2_.1, s32[1,128]{1,0:T(1,128)} %bitcast.20, ...), custom_call_target="tpu_custom_call" | custom-call | flops 399360000 | bytes 2815680 | tf_op jit(solution)/shard_map/layer_one/pallas_call | solution.py:859
  5.6 3.0 %collective-permute-start.2 = (f32[96,512]{1,0:T(8,128)}, f32[96,512]{1,0:T(8,128)S(1)}, u32[]{:S(2)}, u32[]{:S(2)}) collective-permute-start(f32[96,512]{1,0:T(8,128)} %get-tuple-element.56), channel_id=1, source_target_pairs={{1,0},{0,1},{3,2},{2,3},{5,4},{4,5},{7,6},{6,7},{9,8},{8,9},{11,10... | collective-permute-start | bytes 589832 | tf_op jit(solution)/shard_map/ppermute | solution.py:23
  8.6 0.0 collective-permute-start
  8.6 4.4 %collective-permute-start.1 = (f32[48,512]{1,0:T(8,128)}, f32[48,512]{1,0:T(8,128)S(1)}, u32[]{:S(2)}, u32[]{:S(2)}) collective-permute-start(f32[48,512]{1,0:T(8,128)} %get-tuple-element.55), channel_id=1, source_target_pairs={{2,0},{4,2},{6,4},{8,6},{10,8},{12,10},{14,12},{16,14},{18,16},{20... | collective-permute-start | bytes 294920 | tf_op jit(solution)/shard_map/ppermute | solution.py:23
  13.1 1.2 %copy-done.11 = f32[2008,128]{1,0:T(8,128)S(1)} copy-done((f32[2008,128]{1,0:T(8,128)S(1)}, f32[2008,128]{1,0:T(8,128)}, u32[]{:S(2)}) %copy-start.11) | copy-done | bytes 1028120
  14.3 3.3 %radial_two.1 = (f32[512,2560]{1,0:T(8,128)S(1)}, bf16[192,2560]{1,0:T(8,128)(2,1)S(1)}, bf16[640,2560]{1,0:T(8,128)(2,1)S(1)}, bf16[512,192]{1,0:T(8,128)(2,1)S...) custom-call(f32[2008,128]{1,0:T(8,128)S(1)} %copy-done.11), custom_call_target="tpu_custom_call" | custom-call | flops 307200000 | bytes 16363520 | tf_op jit(solution)/shard_map/radial_two/pallas_call | solution.py:859
  17.6 0.0 collective-permute-done.from_minus
  17.6 0.0 copy-start
  17.7 0.0 copy-start.1
  17.7 0.0 copy-start.3
  17.7 0.0 copy-start.4
  17.7 0.0 copy-start.6
  17.7 0.0 copy-start.7
  17.7 0.0 copy-start.10
  17.7 5.3 %layer_two.1 = (f32[1,128]{1,0:T(1,128)}, f32[128,128]{1,0:T(8,128)S(1)}, f32[512,2560]{1,0:T(8,128)S(1)}, f32[4,128,128]{2,1,0:T(8,128)S(1)}, f32[128,512]{1,0:...) custom-call(f32[6,20,128]{2,1,0:T(8,128)S(1)} %get-tuple-element.52.geo.refs_1_, ...), custom_call_target="tpu_custom_call" | custom-call | flops 3355443200 | bytes 20668928 | tf_op jit(solution)/shard_map/layer_two/pallas_call | solution.py:859
  23.0 0.1 collective-permute-start.5
  23.2 0.0 collective-permute-start.3
  23.2 4.4 %collective-permute-start.4 = (f32[56,512]{1,0:T(8,128)S(1)}, f32[56,512]{1,0:T(8,128)S(1)}, u32[]{:S(2)}, u32[]{:S(2)}) collective-permute-start(f32[56,512]{1,0:T(8,128)S(1)} %get-tuple-element.79), channel_id=1, source_target_pairs={{2,0},{4,2},{6,4},{8,6},{10,8},{12,10},{14,12},{16,14},{18,16},{20... | collective-permute-start | bytes 344072 | tf_op jit(solution)/shard_map/ppermute | solution.py:23
  27.7 4.5 %radial_one.1 = (f32[4,20,128]{2,1,0:T(8,128)S(1)}, f32[128,2560]{1,0:T(8,128)S(1)}, f32[128,2560]{1,0:T(8,128)S(1)}, f32[128,2560]{1,0:T(8,128)S(1)}, bf16[896,...) custom-call(bf16[192,2560]{1,0:T(8,128)(2,1)S(1)} %get-tuple-element.69.slopes, ...), custom_call_target="tpu_custom_call" | custom-call | flops 368640000 | bytes 17551872 | tf_op jit(solution)/shard_map/radial_one/pallas_call | solution.py:859
  32.2 0.0 copy-start.8
  32.2 0.0 copy-start.9
  32.2 2.8 %layer_one_back.1 = (f32[32,16,128]{2,1,0:T(8,128)S(1)}, f32[8,128]{1,0:T(8,128)S(1)}) custom-call(f32[16,128]{1,0:T(8,128)S(1)} %get-tuple-element.67.refs_0_.refs_1_, f32[6,20,128]{2,1,0:T(8,128)S(1)} %get-tuple-element.52.geo.refs_1_, f32[5,128,128]{2,1,0:T(8,128)S(1)} %copy-done.2, f32[4,20,128]{2,1,0:T(8,128)S(1)} %get-tuple-element.76.refs_3_, ...), custom_call_target="tpu_custom_call" | custom-call | flops 15360000 | bytes 9158656 | tf_op jit(solution)/shard_map/layer_one_back/pallas_call | solution.py:859
  35.0 14.6 %all_to_all.5.refs_0_ = f32[32,16,128]{2,1,0:T(8,128)S(1)} all-to-all(f32[32,16,128]{2,1,0:T(8,128)S(1)} %get-tuple-element.87), channel_id=1, replica_groups=mesh['slab'=16,'sub'=2] {'slab','sub'}, dimensions={0} | all-to-all | bytes 524288 | tf_op jit(solution)/shard_map/all_to_all | solution.py:1032
  49.6 1.6 %box.1 = (f32[3,128]{1,0:T(4,128)}, f32[3,128]{1,0:T(4,128)}, f32[3,128]{1,0:T(4,128)}, f32[6,16]{1,0:T(8,128)}, f32[3,3]{1,0:T(4,128)}, /*index=5*/f32[3,3]{1,0:T(4,128)}) custom-call(f32[32,16,128]{2,1,0:T(8,128)S(1)} %all_to_all.5.refs_0_, f32[16,128]{1,0:T(8,128)S(1)} %get-tuple-element.67.refs_0_.refs_1_, f32[8,128]{1,0:T(8,128)S(1)} %get-tuple-element.88.refs_2_, ...), custom_call_target="tpu_custom_call" | custom-call | flops 1000000 | bytes 279568 | tf_op jit(solution)/shard_map/box/pallas_call | solution.py:859
  (19 shorter events, 0.0 us)
Async XLA Ops:
  5.6 12.0 %collective-permute-start.2 = (f32[96,512]{1,0:T(8,128)}, f32[96,512]{1,0:T(8,128)S(1)}, u32[]{:S(2)}, u32[]{:S(2)}) collective-permute-start(f32[96,512]{1,0:T(8,128)} %get-tuple-element.56), channel_id=1, source_target_pairs={{1,0},{0,1},{3,2},{2,3},{5,4},{4,5},{7,6},{6,7},{9,8},{8,9},{11,10... | collective-permute-start | bytes 589832 | tf_op jit(solution)/shard_map/ppermute | solution.py:23
  8.6 9.0 %collective-permute-start = (f32[48,512]{1,0:T(8,128)}, f32[48,512]{1,0:T(8,128)S(1)}, u32[]{:S(2)}, u32[]{:S(2)}) collective-permute-start(f32[48,512]{1,0:T(8,128)} %get-tuple-element.54), channel_id=1, source_target_pairs={{30,0},{0,2},{2,4},{4,6},{6,8},{8,10},{10,12},{12,14},{14,16},{16,... | collective-permute-start | bytes 294920 | tf_op jit(solution)/shard_map/ppermute | solution.py:23
  8.6 9.0 %collective-permute-start.1 = (f32[48,512]{1,0:T(8,128)}, f32[48,512]{1,0:T(8,128)S(1)}, u32[]{:S(2)}, u32[]{:S(2)}) collective-permute-start(f32[48,512]{1,0:T(8,128)} %get-tuple-element.55), channel_id=1, source_target_pairs={{2,0},{4,2},{6,4},{8,6},{10,8},{12,10},{14,12},{16,14},{18,16},{20... | collective-permute-start | bytes 294920 | tf_op jit(solution)/shard_map/ppermute | solution.py:23
  13.1 1.2 %copy-start.11 = (f32[2008,128]{1,0:T(8,128)S(1)}, f32[2008,128]{1,0:T(8,128)}, u32[]{:S(2)}) copy-start(f32[2008,128]{1,0:T(8,128)} %get-tuple-element.51.refs_0_) | copy-start | bytes 3084292
  17.6 10.0 %copy-start = (f32[6,128,128]{2,1,0:T(8,128)S(1)}, f32[6,128,128]{2,1,0:T(8,128)}, u32[]{:S(2)}) copy-start(f32[6,128,128]{2,1,0:T(8,128)} %node_one.1) | copy-start | bytes 1179652
  17.7 10.0 %copy-start.1 = (f32[5,128,128]{2,1,0:T(8,128)S(1)}, f32[5,128,128]{2,1,0:T(8,128)}, u32[]{:S(2)}) copy-start(f32[5,128,128]{2,1,0:T(8,128)} %node_two.1) | copy-start | bytes 983044
  17.7 10.0 %copy-start.3 = (f32[2,64,64]{2,1,0:T(8,128)S(1)}, f32[2,64,64]{2,1,0:T(8,128)}, u32[]{:S(2)}) copy-start(f32[2,64,64]{2,1,0:T(8,128)} %radial_mid.1) | copy-start | bytes 98308
  17.7 9.9 %copy-start.4 = (f32[256,64]{0,1:T(8,128)S(1)}, f32[256,64]{0,1:T(8,128)}, u32[]{:S(2)}) copy-start(f32[256,64]{0,1:T(8,128)} %param.41) | copy-start | bytes 196612
  17.7 9.9 %copy-start.5 = (s32[20,128]{1,0:T(8,128)S(1)}, s32[20,128]{1,0:T(8,128)}, u32[]{:S(2)}) copy-start(s32[20,128]{1,0:T(8,128)} %get-tuple-element.74.kinds) | copy-start | bytes 30724
  17.7 9.9 %copy-start.6 = (f32[8,128]{1,0:T(8,128)S(1)}, f32[8,128]{1,0:T(8,128)}, u32[]{:S(2)}) copy-start(f32[8,128]{1,0:T(8,128)} %embedding.1) | copy-start | bytes 12292
  17.7 9.9 %copy-start.7 = (f32[64,8]{0,1:T(8,128)S(1)}, f32[64,8]{0,1:T(8,128)}, u32[]{:S(2)}) copy-start(f32[64,8]{0,1:T(8,128)} %param.39) | copy-start | bytes 6148
  17.7 9.9 %copy-start.10 = (f32[128]{0:T(128)S(1)}, f32[128]{0:T(128)}, u32[]{:S(2)}) copy-start(f32[128]{0:T(128)} %param.47) | copy-start | bytes 1540
  23.0 9.2 %collective-permute-start.5 = (f32[112,512]{1,0:T(8,128)S(1)}, f32[112,512]{1,0:T(8,128)S(1)}, u32[]{:S(2)}, u32[]{:S(2)}) collective-permute-start(f32[112,512]{1,0:T(8,128)S(1)} %get-tuple-element.80), channel_id=1, source_target_pairs={{1,0},{0,1},{3,2},{2,3},{5,4},{4,5},{7,6},{6,7},{9,8},{8,9},{11,10... | collective-permute-start | bytes 688136 | tf_op jit(solution)/shard_map/ppermute | solution.py:23
  23.2 9.0 %collective-permute-start.3 = (f32[56,512]{1,0:T(8,128)S(1)}, f32[56,512]{1,0:T(8,128)S(1)}, u32[]{:S(2)}, u32[]{:S(2)}) collective-permute-start(f32[56,512]{1,0:T(8,128)S(1)} %get-tuple-element.78), channel_id=1, source_target_pairs={{30,0},{0,2},{2,4},{4,6},{6,8},{8,10},{10,12},{12,14},{14,16},{16,... | collective-permute-start | bytes 344072 | tf_op jit(solution)/shard_map/ppermute | solution.py:23
  23.2 9.0 %collective-permute-start.4 = (f32[56,512]{1,0:T(8,128)S(1)}, f32[56,512]{1,0:T(8,128)S(1)}, u32[]{:S(2)}, u32[]{:S(2)}) collective-permute-start(f32[56,512]{1,0:T(8,128)S(1)} %get-tuple-element.79), channel_id=1, source_target_pairs={{2,0},{4,2},{6,4},{8,6},{10,8},{12,10},{14,12},{16,14},{18,16},{20... | collective-permute-start | bytes 344072 | tf_op jit(solution)/shard_map/ppermute | solution.py:23
  27.7 4.5 %copy-start.2 = (f32[5,128,128]{2,1,0:T(8,128)S(1)}, f32[5,128,128]{2,1,0:T(8,128)}, u32[]{:S(2)}) copy-start(f32[5,128,128]{2,1,0:T(8,128)} %get-tuple-element.68.refs_2_) | copy-start | bytes 983044
  32.2 17.4 %copy-start.8 = (f32[3,3]{1,0:T(4,128)S(1)}, f32[3,3]{1,0:T(4,128)}, u32[]{:S(2)}) copy-start(f32[3,3]{1,0:T(4,128)} %refs_3_.1) | copy-start | bytes 112
  32.2 17.4 %copy-start.9 = (f32[3,3]{1,0:T(4,128)S(1)}, f32[3,3]{1,0:T(4,128)}, u32[]{:S(2)}) copy-start(f32[3,3]{1,0:T(4,128)} %refs_4_.1) | copy-start | bytes 112
